TPU v7x, 32 devices: a whole 2x2x4 slice. The times are simulated.
32 devices in a mesh: fsdp: 8 (over y, x, core), tp: 4 (over z).
Axes of the slice: x: 2, y: 2, z: 4, core: 2. Of those that a mesh axis runs over, the one named last changes fastest.
Arguments:
- tokens: bfloat16 [2, 4, 1536, 1536], P(None, None, ('fsdp', 'tp')), may hold values from -6 to 6
- memory: bfloat16 [2, 4, 64, 1536], replicated, may hold values from -6 to 6
- text_len: int32 [2, 4], replicated, may hold values from 1 to 64, as said below
- cotangent: bfloat16 [2, 4, 1536, 1536], P(None, None, ('fsdp', 'tp')), may hold values from -6 to 6
- gain_one: float32 [1536], replicated, may hold values from 0.5 to 1.5
- bias_one: float32 [1536], replicated, may hold values from -1 to 1
- gain_two: float32 [1536], replicated, may hold values from 0.5 to 1.5
- bias_two: float32 [1536], replicated, may hold values from -1 to 1
- gain_three: float32 [1536], replicated, may hold values from 0.5 to 1.5
- bias_three: float32 [1536], replicated, may hold values from -1 to 1
- w_query: bfloat16 [1536, 1536], P('fsdp', 'tp'), may hold values from -0.15625 to 0.15625
- w_key: bfloat16 [1536, 1536], P('fsdp', 'tp'), may hold values from -0.15625 to 0.15625
- w_value: bfloat16 [1536, 1536], P('fsdp', 'tp'), may hold values from -0.15625 to 0.15625
- w_out: bfloat16 [1536, 1536], P('tp', 'fsdp'), may hold values from -0.4375 to 0.4375
- c_query: bfloat16 [1536, 1536], P('fsdp', 'tp'), may hold values from -0.15625 to 0.15625
- c_key: bfloat16 [1536, 1536], P('fsdp', 'tp'), may hold values from -0.15625 to 0.15625
- c_value: bfloat16 [1536, 1536], P('fsdp', 'tp'), may hold values from -0.15625 to 0.15625
- c_out: bfloat16 [1536, 1536], P('tp', 'fsdp'), may hold values from -0.3125 to 0.3125
- w_up: bfloat16 [1536, 6144], P('fsdp', 'tp'), may hold values from -0.15625 to 0.15625
- w_down: bfloat16 [6144, 1536], P('tp', 'fsdp'), may hold values from -0.109375 to 0.109375
Outputs:
- layer_out: bfloat16 [2, 4, 1536, 1536], P(None, None, ('fsdp', 'tp'))
- grad_tokens: float32 [2, 4, 1536, 1536], P(None, None, ('fsdp', 'tp'))
- grad_memory: float32 [2, 4, 64, 1536], replicated
- grad_gain_one: float32 [1536], replicated
- grad_bias_one: float32 [1536], replicated
- grad_gain_two: float32 [1536], replicated
- grad_bias_two: float32 [1536], replicated
- grad_gain_three: float32 [1536], replicated
- grad_bias_three: float32 [1536], replicated
- grad_w_query: float32 [1536, 1536], P('fsdp', 'tp')
- grad_w_key: float32 [1536, 1536], P('fsdp', 'tp')
- grad_w_value: float32 [1536, 1536], P('fsdp', 'tp')
- grad_w_out: float32 [1536, 1536], P('tp', 'fsdp')
- grad_c_query: float32 [1536, 1536], P('fsdp', 'tp')
- grad_c_key: float32 [1536, 1536], P('fsdp', 'tp')
- grad_c_value: float32 [1536, 1536], P('fsdp', 'tp')
- grad_c_out: float32 [1536, 1536], P('tp', 'fsdp')
- grad_w_up: float32 [1536, 6144], P('fsdp', 'tp')
- grad_w_down: float32 [6144, 1536], P('tp', 'fsdp')
Inputs may be any that keep to these rules, and one draw needn't show every extreme that they name: `text_len`: in every micro-batch some clip has all 64 text tokens.
All inputs are finite; a program needn't handle non-finite values.
Results may differ from a plain program's by a relative error of at most 0.02.
Values may be sent and summed in bfloat16 or wider, within the bound.
A program may use at most 232 MiB of HBM per device.

v0:
```python
import math

import jax
import jax.numpy as jnp
from jax import lax
from jax.sharding import PartitionSpec as P

HD = 64
MICRO = 2


EPSILON = 1e-05
PRECISE = lax.Precision.HIGHEST
MASKED = -1e30


def layer_norm(values, gain_vec, bias_vec):
    center = values - jnp.mean(values, axis=-1, keepdims=True)
    inverse = lax.rsqrt(jnp.mean(center * center, axis=-1, keepdims=True) + EPSILON)
    scaled = center * inverse
    return (scaled * gain_vec + bias_vec, scaled, inverse)


def norm_back(upstream, scaled, inverse, gain_vec):
    weighted = upstream * gain_vec
    result = inverse * (
        weighted
        - jnp.mean(weighted, axis=-1, keepdims=True)
        - scaled * jnp.mean(weighted * scaled, axis=-1, keepdims=True)
    )
    return (result, jnp.sum(upstream * scaled, axis=(0, 1)), jnp.sum(upstream, axis=(0, 1)))


def spread_rows(values):
    return lax.all_gather(values, "tp", axis=1, tiled=True)


def spread_grads(values):
    return lax.all_gather(values, "tp", axis=1, tiled=True)


def fold_rows(values):
    return lax.psum_scatter(values, "tp", scatter_dimension=1, tiled=True)


def fold_grads(values):
    return lax.psum_scatter(values, "tp", scatter_dimension=1, tiled=True)


def project(left_side, right_side):
    return jnp.einsum("cfd,de->cfe", left_side, right_side, preferred_element_type=jnp.float32)


def project_back(left_side, right_side):
    return jnp.einsum("cfe,de->cfd", left_side, right_side, preferred_element_type=jnp.float32)


def weight_grad(left_side, right_side):
    return jnp.einsum("cfd,cfe->de", left_side, right_side, preferred_element_type=jnp.float32)


def masked_scores(queries, key_rows, allowed):
    factor = 1.0 / math.sqrt(queries.shape[-1])
    scores = (
        jnp.einsum("cqhe,ckhe->chqk", queries, key_rows, preferred_element_type=jnp.float32)
        * factor
    )
    return jnp.where(allowed, scores, MASKED)


def attention_forward(queries, key_rows, value_rows, allowed):
    scores = masked_scores(queries, key_rows, allowed)
    highest = jnp.max(scores, axis=-1, keepdims=True)
    log_total = highest + jnp.log(jnp.sum(jnp.exp(scores - highest), axis=-1, keepdims=True))
    weights = jnp.exp(scores - log_total).astype(jnp.bfloat16)
    mixed = jnp.einsum("chqk,ckhe->cqhe", weights, value_rows, preferred_element_type=jnp.float32)
    return (mixed, log_total)


def score_grads(queries, key_rows, value_rows, allowed, log_total, grad_mixed):
    weights = jnp.exp(masked_scores(queries, key_rows, allowed) - log_total)
    grad_weights = jnp.einsum(
        "cqhe,ckhe->chqk", grad_mixed, value_rows, preferred_element_type=jnp.float32
    )
    row_total = jnp.sum(grad_weights * weights, axis=-1, keepdims=True)
    grad_scores = (weights * (grad_weights - row_total)).astype(jnp.bfloat16)
    return (weights, grad_scores, row_total)


def attention_backward(queries, key_rows, value_rows, allowed, log_total, grad_mixed):
    factor = 1.0 / math.sqrt(queries.shape[-1])
    weights, grad_scores, row_total = score_grads(
        queries, key_rows, value_rows, allowed, log_total, grad_mixed
    )
    grad_queries = (
        jnp.einsum("chqk,ckhe->cqhe", grad_scores, key_rows, preferred_element_type=jnp.float32)
        * factor
    )
    grad_keys = (
        jnp.einsum("chqk,cqhe->ckhe", grad_scores, queries, preferred_element_type=jnp.float32)
        * factor
    )
    grad_values = jnp.einsum(
        "chqk,cqhe->ckhe",
        weights.astype(jnp.bfloat16),
        grad_mixed,
        preferred_element_type=jnp.float32,
    )
    return (grad_queries, grad_keys, grad_values, row_total)


def body(
    tokens,
    memory,
    text_len,
    cotangent,
    gain_one,
    bias_one,
    gain_two,
    bias_two,
    gain_three,
    bias_three,
    w_query,
    w_key,
    w_value,
    w_out,
    c_query,
    c_key,
    c_value,
    c_out,
    w_up,
    w_down,
):
    clips = tokens.shape[1]
    shard_frames = tokens.shape[2] * lax.axis_size("tp")
    text_slots = memory.shape[2]
    local_width = w_query.shape[1]
    local_heads = local_width // HD
    query_pos = lax.axis_index("fsdp") * shard_frames + jnp.arange(shard_frames)
    key_pos = jnp.arange(shard_frames * lax.axis_size("fsdp"))
    causal = (key_pos[None, :] <= query_pos[:, None])[None, None]
    shards = (w_query, w_key, w_value, c_query, c_key, c_value, w_up, w_out, c_out, w_down)
    head_shape = (clips, shard_frames, local_heads, HD)
    text_shape = (clips, text_slots, local_heads, HD)
    outputs = []
    input_grads = []
    text_grads = []
    norm_totals = None
    weight_total = None
    for micro in range(MICRO):
        gathered = (
            lax.all_gather(shards[0], "fsdp", axis=0, tiled=True),
            lax.all_gather(shards[1], "fsdp", axis=0, tiled=True),
            lax.all_gather(shards[2], "fsdp", axis=0, tiled=True),
            lax.all_gather(shards[3], "fsdp", axis=0, tiled=True),
            lax.all_gather(shards[4], "fsdp", axis=0, tiled=True),
            lax.all_gather(shards[5], "fsdp", axis=0, tiled=True),
            lax.all_gather(shards[6], "fsdp", axis=0, tiled=True),
            lax.all_gather(shards[7], "fsdp", axis=1, tiled=True),
            lax.all_gather(shards[8], "fsdp", axis=1, tiled=True),
            lax.all_gather(shards[9], "fsdp", axis=1, tiled=True),
        )
        (
            query_full,
            key_full,
            value_full,
            cross_query,
            cross_key,
            cross_value,
            up_full,
            out_full,
            cross_out,
            down_full,
        ) = gathered
        frames = tokens[micro].astype(jnp.float32)
        text_rows = memory[micro]
        counts = text_len[micro]
        normed_one, scaled_one, inverse_one = layer_norm(frames, gain_one, bias_one)
        rows_one = spread_rows(normed_one.astype(jnp.bfloat16))
        queries = project(rows_one, query_full).astype(jnp.bfloat16).reshape(head_shape)
        key_local = project(rows_one, key_full).astype(jnp.bfloat16)
        value_local = project(rows_one, value_full).astype(jnp.bfloat16)
        key_all, value_all = (
            lax.all_gather(key_local, "fsdp", axis=1, tiled=True),
            lax.all_gather(value_local, "fsdp", axis=1, tiled=True),
        )
        key_all = key_all.reshape(clips, -1, local_heads, HD)
        value_all = value_all.reshape(clips, -1, local_heads, HD)
        mixed_one, total_one = attention_forward(queries, key_all, value_all, causal)
        mixed_one = mixed_one.astype(jnp.bfloat16).reshape(clips, shard_frames, local_width)
        after_self = frames + fold_rows(project(mixed_one, out_full))
        normed_two, scaled_two, inverse_two = layer_norm(after_self, gain_two, bias_two)
        rows_two = spread_rows(normed_two.astype(jnp.bfloat16))
        cross_q = project(rows_two, cross_query).astype(jnp.bfloat16).reshape(head_shape)
        cross_k = project(text_rows, cross_key).astype(jnp.bfloat16).reshape(text_shape)
        cross_v = project(text_rows, cross_value).astype(jnp.bfloat16).reshape(text_shape)
        visible = (jnp.arange(text_slots)[None, :] < counts[:, None])[:, None, None, :]
        mixed_two, total_two = attention_forward(cross_q, cross_k, cross_v, visible)
        mixed_two = mixed_two.astype(jnp.bfloat16).reshape(clips, shard_frames, local_width)
        after_cross = after_self + fold_rows(project(mixed_two, cross_out))
        normed_three, scaled_three, inverse_three = layer_norm(after_cross, gain_three, bias_three)
        rows_three = spread_rows(normed_three.astype(jnp.bfloat16))
        hidden = project(rows_three, up_full)
        active = jax.nn.gelu(hidden).astype(jnp.bfloat16)
        result = after_cross + fold_rows(project(active, down_full))
        outputs.append(result.astype(jnp.bfloat16))
        gathered = (
            lax.all_gather(shards[0], "fsdp", axis=0, tiled=True),
            lax.all_gather(shards[1], "fsdp", axis=0, tiled=True),
            lax.all_gather(shards[2], "fsdp", axis=0, tiled=True),
            lax.all_gather(shards[3], "fsdp", axis=0, tiled=True),
            lax.all_gather(shards[4], "fsdp", axis=0, tiled=True),
            lax.all_gather(shards[5], "fsdp", axis=0, tiled=True),
            lax.all_gather(shards[6], "fsdp", axis=0, tiled=True),
            lax.all_gather(shards[7], "fsdp", axis=1, tiled=True),
            lax.all_gather(shards[8], "fsdp", axis=1, tiled=True),
            lax.all_gather(shards[9], "fsdp", axis=1, tiled=True),
        )
        (
            query_full,
            key_full,
            value_full,
            cross_query,
            cross_key,
            cross_value,
            up_full,
            out_full,
            cross_out,
            down_full,
        ) = gathered
        upstream = cotangent[micro].astype(jnp.float32)
        grad_rows = spread_grads(upstream.astype(jnp.bfloat16))
        grad_down = weight_grad(active, grad_rows)
        grad_active = project_back(grad_rows, down_full)
        _, gelu_pull = jax.vjp(jax.nn.gelu, hidden)
        grad_hidden = gelu_pull(grad_active)[0].astype(jnp.bfloat16)
        grad_up = weight_grad(rows_three, grad_hidden)
        grad_three = fold_grads(project_back(grad_hidden, up_full))
        back_three, gain_g3, bias_g3 = norm_back(
            grad_three, scaled_three, inverse_three, gain_three
        )
        upstream = upstream + back_three
        grad_rows = spread_grads(upstream.astype(jnp.bfloat16))
        grad_cout = weight_grad(mixed_two, grad_rows)
        grad_mixed = project_back(grad_rows, cross_out).astype(jnp.bfloat16).reshape(head_shape)
        grad_cq, grad_ck, grad_cv, _ = attention_backward(
            cross_q, cross_k, cross_v, visible, total_two, grad_mixed
        )
        grad_cq = grad_cq.astype(jnp.bfloat16).reshape(clips, shard_frames, local_width)
        grad_ck = grad_ck.reshape(clips, text_slots, local_width)
        grad_cv = grad_cv.reshape(clips, text_slots, local_width)
        grad_cquery = weight_grad(rows_two, grad_cq)
        text_wide = text_rows.astype(jnp.float32)
        grad_ckey = jnp.einsum("cmd,cme->de", text_wide, grad_ck, precision=PRECISE)
        grad_cvalue = jnp.einsum("cmd,cme->de", text_wide, grad_cv, precision=PRECISE)
        text_grads.append(
            jnp.einsum("cme,de->cmd", grad_ck, cross_key.astype(jnp.float32), precision=PRECISE)
            + jnp.einsum("cme,de->cmd", grad_cv, cross_value.astype(jnp.float32), precision=PRECISE)
        )
        grad_two = fold_grads(project_back(grad_cq, cross_query))
        back_two, gain_g2, bias_g2 = norm_back(grad_two, scaled_two, inverse_two, gain_two)
        upstream = upstream + back_two
        grad_rows = spread_grads(upstream.astype(jnp.bfloat16))
        grad_out = weight_grad(mixed_one, grad_rows)
        grad_mixed = project_back(grad_rows, out_full).astype(jnp.bfloat16).reshape(head_shape)
        grad_q, grad_kall, grad_vall, _ = attention_backward(
            queries, key_all, value_all, causal, total_one, grad_mixed
        )
        grad_kloc, grad_vloc = (
            lax.psum_scatter(
                grad_kall.reshape(clips, -1, local_width).astype(jnp.bfloat16),
                "fsdp",
                scatter_dimension=1,
                tiled=True,
            ).astype(jnp.float32),
            lax.psum_scatter(
                grad_vall.reshape(clips, -1, local_width).astype(jnp.bfloat16),
                "fsdp",
                scatter_dimension=1,
                tiled=True,
            ).astype(jnp.float32),
        )
        grad_q = grad_q.astype(jnp.bfloat16).reshape(clips, shard_frames, local_width)
        grad_kloc = grad_kloc.astype(jnp.bfloat16)
        grad_vloc = grad_vloc.astype(jnp.bfloat16)
        grad_query = weight_grad(rows_one, grad_q)
        grad_key = weight_grad(rows_one, grad_kloc)
        grad_value = weight_grad(rows_one, grad_vloc)
        grad_one = fold_grads(
            project_back(grad_q, query_full)
            + project_back(grad_kloc, key_full)
            + project_back(grad_vloc, value_full)
        )
        back_one, gain_g1, bias_g1 = norm_back(grad_one, scaled_one, inverse_one, gain_one)
        input_grads.append(upstream + back_one)
        norm_parts = (gain_g1, bias_g1, gain_g2, bias_g2, gain_g3, bias_g3)
        norm_totals = norm_parts if micro == 0 else jax.tree.map(jnp.add, norm_totals, norm_parts)
        micro_grads = (
            grad_query,
            grad_key,
            grad_value,
            grad_cquery,
            grad_ckey,
            grad_cvalue,
            grad_up,
            grad_out,
            grad_cout,
            grad_down,
        )
        weight_total = (
            micro_grads if micro == 0 else jax.tree.map(jnp.add, weight_total, micro_grads)
        )
    weight_total = (
        lax.psum_scatter(
            weight_total[0].astype(jnp.bfloat16), "fsdp", scatter_dimension=0, tiled=True
        ).astype(jnp.float32),
        lax.psum_scatter(
            weight_total[1].astype(jnp.bfloat16), "fsdp", scatter_dimension=0, tiled=True
        ).astype(jnp.float32),
        lax.psum_scatter(
            weight_total[2].astype(jnp.bfloat16), "fsdp", scatter_dimension=0, tiled=True
        ).astype(jnp.float32),
        lax.psum_scatter(
            weight_total[3].astype(jnp.bfloat16), "fsdp", scatter_dimension=0, tiled=True
        ).astype(jnp.float32),
        lax.psum_scatter(
            weight_total[4].astype(jnp.bfloat16), "fsdp", scatter_dimension=0, tiled=True
        ).astype(jnp.float32),
        lax.psum_scatter(
            weight_total[5].astype(jnp.bfloat16), "fsdp", scatter_dimension=0, tiled=True
        ).astype(jnp.float32),
        lax.psum_scatter(
            weight_total[6].astype(jnp.bfloat16), "fsdp", scatter_dimension=0, tiled=True
        ).astype(jnp.float32),
        lax.psum_scatter(
            weight_total[7].astype(jnp.bfloat16), "fsdp", scatter_dimension=1, tiled=True
        ).astype(jnp.float32),
        lax.psum_scatter(
            weight_total[8].astype(jnp.bfloat16), "fsdp", scatter_dimension=1, tiled=True
        ).astype(jnp.float32),
        lax.psum_scatter(
            weight_total[9].astype(jnp.bfloat16), "fsdp", scatter_dimension=1, tiled=True
        ).astype(jnp.float32),
    )
    summed = lax.psum(
        (
            jnp.stack(text_grads),
            norm_totals[0],
            norm_totals[1],
            norm_totals[2],
            norm_totals[3],
            norm_totals[4],
            norm_totals[5],
        ),
        ("fsdp", "tp"),
    )
    (
        fin_query,
        fin_key,
        fin_value,
        fin_cquery,
        fin_ckey,
        fin_cvalue,
        fin_up,
        fin_out,
        fin_cout,
        fin_down,
    ) = weight_total
    return (
        jnp.stack(outputs),
        jnp.stack(input_grads),
        summed[0],
        summed[1],
        summed[2],
        summed[3],
        summed[4],
        summed[5],
        summed[6],
        fin_query,
        fin_key,
        fin_value,
        fin_out,
        fin_cquery,
        fin_ckey,
        fin_cvalue,
        fin_cout,
        fin_up,
        fin_down,
    )


def solution(mesh):
    return jax.shard_map(
        body,
        mesh=mesh,
        in_specs=(
            P(None, None, ("fsdp", "tp"), None),
            P(),
            P(),
            P(None, None, ("fsdp", "tp"), None),
            P(),
            P(),
            P(),
            P(),
            P(),
            P(),
            P("fsdp", "tp"),
            P("fsdp", "tp"),
            P("fsdp", "tp"),
            P("tp", "fsdp"),
            P("fsdp", "tp"),
            P("fsdp", "tp"),
            P("fsdp", "tp"),
            P("tp", "fsdp"),
            P("fsdp", "tp"),
            P("tp", "fsdp"),
        ),
        out_specs=(
            P(None, None, ("fsdp", "tp"), None),
            P(None, None, ("fsdp", "tp"), None),
            P(),
            P(),
            P(),
            P(),
            P(),
            P(),
            P(),
            P("fsdp", "tp"),
            P("fsdp", "tp"),
            P("fsdp", "tp"),
            P("tp", "fsdp"),
            P("fsdp", "tp"),
            P("fsdp", "tp"),
            P("fsdp", "tp"),
            P("tp", "fsdp"),
            P("fsdp", "tp"),
            P("tp", "fsdp"),
        ),
        check_vma=False,
    )
```

profile of v0, /device:TPU:0, one launch (start us, length us, event | category | flops | bytes accessed | tf_op | source)
XLA Modules:
  0.0 3174.8 jit_solution(14693784188646747234)
XLA Ops:
  36.7 52.6 %all-gather.29.cloned.1.call-done = bf16[4,192,1536]{2,1,0:T(8,128)(2,1)} async-done(((bf16[4,48,1536]{2,1,0:T(8,128)(2,1)}), bf16[4,192,1536]{2,1,0:T(8,128)(2,1)}) %all-gather.29.cloned.1.call-update) | async-done | bytes 2359312 | tf_op jit(solution)/shard_map/all_gather | solution.py:35
  255.7 83.3 %reduce-scatter.31.cloned.1.call-done = f32[4,48,1536]{2,1,0:T(8,128)} async-done(((f32[4,192,1536]{2,1,0:T(8,128)}), f32[4,48,1536]{2,1,0:T(8,128)}) %reduce-scatter.31.cloned.1.call-update) | async-done | bytes 1179664 | tf_op jit(solution)/shard_map/reduce_scatter | solution.py:43
  417.3 52.5 %all-gather.45.cloned.1.call-done = bf16[4,192,1536]{2,1,0:T(8,128)(2,1)} async-done(((bf16[4,48,1536]{2,1,0:T(8,128)(2,1)}), bf16[4,192,1536]{2,1,0:T(8,128)(2,1)}) %all-gather.45.cloned.1.call-update) | async-done | bytes 2359312 | tf_op jit(solution)/shard_map/all_gather | solution.py:35
  500.5 84.7 %reduce-scatter.33.cloned.1.call-done = f32[4,48,1536]{2,1,0:T(8,128)} async-done(((f32[4,192,1536]{2,1,0:T(8,128)}), f32[4,48,1536]{2,1,0:T(8,128)}) %reduce-scatter.33.cloned.1.call-update) | async-done | bytes 1179664 | tf_op jit(solution)/shard_map/reduce_scatter | solution.py:43
  626.4 52.5 %all-gather.53.cloned.1.call-done = bf16[4,192,1536]{2,1,0:T(8,128)(2,1)} async-done(((bf16[4,48,1536]{2,1,0:T(8,128)(2,1)}), bf16[4,192,1536]{2,1,0:T(8,128)(2,1)}) %all-gather.53.cloned.1.call-update) | async-done | bytes 2359312 | tf_op jit(solution)/shard_map/all_gather | solution.py:35
  798.8 74.8 %reduce-scatter.43.cloned.1.call-done = f32[4,48,1536]{2,1,0:T(8,128)} async-done(((f32[4,192,1536]{2,1,0:T(8,128)}), f32[4,48,1536]{2,1,0:T(8,128)}) %reduce-scatter.43.cloned.1.call-update) | async-done | bytes 1179664 | tf_op jit(solution)/shard_map/reduce_scatter | solution.py:47
  876.4 85.2 %reduce-scatter.35.cloned.1.call-done = f32[4,48,1536]{2,1,0:T(8,128)} async-done(((f32[4,192,1536]{2,1,0:T(8,128)}), f32[4,48,1536]{2,1,0:T(8,128)}) %reduce-scatter.35.cloned.1.call-update) | async-done | bytes 1179664 | tf_op jit(solution)/shard_map/reduce_scatter | solution.py:43
  966.2 50.3 %all-gather.69.cloned.1.call-done = bf16[4,192,1536]{2,1,0:T(8,128)(2,1)} async-done(((bf16[4,48,1536]{2,1,0:T(8,128)(2,1)}), bf16[4,192,1536]{2,1,0:T(8,128)(2,1)}) %all-gather.69.cloned.1.call-update) | async-done | bytes 2359312 | tf_op jit(solution)/shard_map/all_gather | solution.py:39
  1076.2 78.2 %reduce-scatter.45.cloned.1.call-done = f32[4,48,1536]{2,1,0:T(8,128)} async-done(((f32[4,192,1536]{2,1,0:T(8,128)}), f32[4,48,1536]{2,1,0:T(8,128)}) %reduce-scatter.45.cloned.1.call-update) | async-done | bytes 1179664 | tf_op jit(solution)/shard_map/reduce_scatter | solution.py:47
  1373.8 84.2 %reduce-scatter.37.cloned.1.call-done = f32[4,48,1536]{2,1,0:T(8,128)} async-done(((f32[4,192,1536]{2,1,0:T(8,128)}), f32[4,48,1536]{2,1,0:T(8,128)}) %reduce-scatter.37.cloned.1.call-update) | async-done | bytes 1179664 | tf_op jit(solution)/shard_map/reduce_scatter | solution.py:43
  1468.8 44.0 %all-gather.65.cloned.1.call-done = bf16[4,192,1536]{2,1,0:T(8,128)(2,1)} async-done(((bf16[4,48,1536]{2,1,0:T(8,128)(2,1)}), bf16[4,192,1536]{2,1,0:T(8,128)(2,1)}) %all-gather.65.cloned.1.call-update) | async-done | bytes 2359312 | tf_op jit(solution)/shard_map/all_gather | solution.py:35
  1522.5 84.2 %reduce-scatter.39.cloned.1.call-done = f32[4,48,1536]{2,1,0:T(8,128)} async-done(((f32[4,192,1536]{2,1,0:T(8,128)}), f32[4,48,1536]{2,1,0:T(8,128)}) %reduce-scatter.39.cloned.1.call-update) | async-done | bytes 1179664 | tf_op jit(solution)/shard_map/reduce_scatter | solution.py:43
  1611.2 49.9 %all-gather.67.cloned.1.call-done = bf16[4,192,1536]{2,1,0:T(8,128)(2,1)} async-done(((bf16[4,48,1536]{2,1,0:T(8,128)(2,1)}), bf16[4,192,1536]{2,1,0:T(8,128)(2,1)}) %all-gather.67.cloned.1.call-update) | async-done | bytes 2359312 | tf_op jit(solution)/shard_map/all_gather | solution.py:35
  1730.5 84.2 %reduce-scatter.53.cloned.1.call-done = f32[4,48,1536]{2,1,0:T(8,128)} async-done(((f32[4,192,1536]{2,1,0:T(8,128)}), f32[4,48,1536]{2,1,0:T(8,128)}) %reduce-scatter.53.cloned.1.call-update) | async-done | bytes 1179664 | tf_op jit(solution)/shard_map/reduce_scatter | solution.py:47
  1818.6 51.1 %all-gather.73.cloned.1.call-done = bf16[4,192,1536]{2,1,0:T(8,128)(2,1)} async-done(((bf16[4,48,1536]{2,1,0:T(8,128)(2,1)}), bf16[4,192,1536]{2,1,0:T(8,128)(2,1)}) %all-gather.73.cloned.1.call-update) | async-done | bytes 2359312 | tf_op jit(solution)/shard_map/all_gather | solution.py:39
  1894.7 73.9 %reduce-scatter.55.cloned.1.call-done = f32[4,48,1536]{2,1,0:T(8,128)} async-done(((f32[4,192,1536]{2,1,0:T(8,128)}), f32[4,48,1536]{2,1,0:T(8,128)}) %reduce-scatter.55.cloned.1.call-update) | async-done | bytes 1179664 | tf_op jit(solution)/shard_map/reduce_scatter | solution.py:47
  1971.0 85.7 %reduce-scatter.41.cloned.1.call-done = f32[4,48,1536]{2,1,0:T(8,128)} async-done(((f32[4,192,1536]{2,1,0:T(8,128)}), f32[4,48,1536]{2,1,0:T(8,128)}) %reduce-scatter.41.cloned.1.call-update) | async-done | bytes 1179664 | tf_op jit(solution)/shard_map/reduce_scatter | solution.py:43
  2061.3 51.1 %all-gather.75.cloned.1.call-done = bf16[4,192,1536]{2,1,0:T(8,128)(2,1)} async-done(((bf16[4,48,1536]{2,1,0:T(8,128)(2,1)}), bf16[4,192,1536]{2,1,0:T(8,128)(2,1)}) %all-gather.75.cloned.1.call-update) | async-done | bytes 2359312 | tf_op jit(solution)/shard_map/all_gather | solution.py:39
  2356.0 51.1 %reduce-scatter.49.cloned.1.call-done = bf16[4,192,384]{2,1,0:T(8,128)(2,1)} async-done(((bf16[4,1536,384]{2,1,0:T(8,128)(2,1)}), bf16[4,192,384]{2,1,0:T(8,128)(2,1)}) %reduce-scatter.49.cloned.1.call-update) | async-done | bytes 589840 | tf_op jit(solution)/shard_map/reduce_scatter | solution.py:276
  2466.7 55.6 %reduce-scatter.77.cloned.1.call-done = bf16[1536,192]{0,1:T(8,128)(2,1)} async-done(((bf16[1536,1536]{0,1:T(8,128)(2,1)}), bf16[1536,192]{0,1:T(8,128)(2,1)}) %reduce-scatter.77.cloned.1.call-update) | async-done | bytes 589840 | tf_op jit(solution)/shard_map/reduce_scatter | solution.py:341
  2845.3 85.8 %reduce-scatter.51.cloned.1.call-done = f32[4,48,1536]{2,1,0:T(8,128)} async-done(((f32[4,192,1536]{2,1,0:T(8,128)}), f32[4,48,1536]{2,1,0:T(8,128)}) %reduce-scatter.51.cloned.1.call-update) | async-done | bytes 1179664 | tf_op jit(solution)/shard_map/reduce_scatter | solution.py:47
  2931.1 88.1 %reduce-scatter.61.cloned.1.call-done = f32[4,48,1536]{2,1,0:T(8,128)} async-done(((f32[4,192,1536]{2,1,0:T(8,128)}), f32[4,48,1536]{2,1,0:T(8,128)}) %reduce-scatter.61.cloned.1.call-update) | async-done | bytes 1179664 | tf_op jit(solution)/shard_map/reduce_scatter | solution.py:47
  3024.9 42.8 %all-reduce = (f32[1536]{0:T(1024)}, f32[1536]{0:T(1024)}, f32[1536]{0:T(1024)}, f32[1536]{0:T(1024)}, f32[1536]{0:T(1024)}, /*index=5*/f32[1536]{0:T(1024)}) all-reduce(f32[1536]{0:T(1024)} %add.363, f32[1536]{0:T(1024)} %add.364, f32[1536]{0:T(1024)} %add.365, f32[1536]{0:T(1024)} %add.366, ...), channel_id=1, replica_groups=mesh['fsdp'=8,'tp'=4] {'fsdp','tp'}, use_global_device_ids=true, to_apply=%region_55.56 | all-reduce | flops 9216 | bytes 73728 | tf_op jit(solution)/shard_map/psum | solution.py:345
  3073.1 90.6 %all-reduce.3.cloned.1.call-done = f32[2,4,64,1536]{3,2,1,0:T(8,128)} async-done(((f32[2,4,64,1536]{3,2,1,0:T(8,128)}), f32[2,4,64,1536]{3,2,1,0:T(8,128)}) %all-reduce.3.cloned.1.call-update) | async-done | bytes 3145744 | tf_op jit(solution)/shard_map/psum | solution.py:345
  (564 shorter events, 1521.4 us)
Async XLA Ops:
  119.1 219.8 %reduce-scatter.31.cloned.1.call-start = ((), (), s32[]{:S(2)}) async-start(), calls=%async_computation.33 | async-start | bytes 5898240 | tf_op jit(solution)/shard_map/reduce_scatter | solution.py:43
  255.6 214.1 %all-gather.45.cloned.1.call-start = ((), (), s32[]{:S(2)}) async-start(), calls=%async_computation.35 | async-start | bytes 2949120 | tf_op jit(solution)/shard_map/all_gather | solution.py:35
  342.6 242.6 %reduce-scatter.33.cloned.1.call-start = ((), (), s32[]{:S(2)}) async-start(), calls=%async_computation.39 | async-start | bytes 5898240 | tf_op jit(solution)/shard_map/reduce_scatter | solution.py:43
  591.8 281.8 %reduce-scatter.43.cloned.1.call-start = ((), (), s32[]{:S(2)}) async-start(), calls=%async_computation.52 | async-start | bytes 5898240 | tf_op jit(solution)/shard_map/reduce_scatter | solution.py:47
  798.8 217.7 %all-gather.69.cloned.1.call-start = ((), (), s32[]{:S(2)}) async-start(), calls=%async_computation.53 | async-start | bytes 2949120 | tf_op jit(solution)/shard_map/all_gather | solution.py:39
  966.1 188.3 %reduce-scatter.45.cloned.1.call-start = ((), (), s32[]{:S(2)}) async-start(), calls=%async_computation.54 | async-start | bytes 5898240 | tf_op jit(solution)/shard_map/reduce_scatter | solution.py:47
  1076.1 213.4 %all-gather.71.cloned.1.call-start = ((), (), s32[]{:S(2)}) async-start(), calls=%async_computation.55 | async-start | bytes 2949120 | tf_op jit(solution)/shard_map/all_gather | solution.py:39
  1160.6 297.4 %reduce-scatter.37.cloned.1.call-start = ((), (), s32[]{:S(2)}) async-start(), calls=%async_computation.47 | async-start | bytes 5898240 | tf_op jit(solution)/shard_map/reduce_scatter | solution.py:43
  1610.7 204.0 %reduce-scatter.53.cloned.1.call-start = ((), (), s32[]{:S(2)}) async-start(), calls=%async_computation.59 | async-start | bytes 5898240 | tf_op jit(solution)/shard_map/reduce_scatter | solution.py:47
  1894.6 217.7 %all-gather.75.cloned.1.call-start = ((), (), s32[]{:S(2)}) async-start(), calls=%async_computation.62 | async-start | bytes 2949120 | tf_op jit(solution)/shard_map/all_gather | solution.py:39
  2061.2 281.0 %reduce-scatter.57.cloned.1.call-start = ((), (), s32[]{:S(2)}) async-start(), calls=%async_computation.63 | async-start | bytes 5308416 | tf_op jit(solution)/shard_map/reduce_scatter | solution.py:270
  2244.1 220.4 %reduce-scatter.75.cloned.1.call-start = ((), (), s32[]{:S(2)}) async-start(), calls=%async_computation.73 | async-start | bytes 5308416 | tf_op jit(solution)/shard_map/reduce_scatter | solution.py:332
  2257.6 264.7 %reduce-scatter.77.cloned.1.call-start = ((), (), s32[]{:S(2)}) async-start(), calls=%async_computation.74 | async-start | bytes 5308416 | tf_op jit(solution)/shard_map/reduce_scatter | solution.py:341
  2274.9 287.3 %reduce-scatter.79.cloned.1.call-start = ((), (), s32[]{:S(2)}) async-start(), calls=%async_computation.77 | async-start | bytes 1327104
  2282.0 320.6 %reduce-scatter.81.cloned.1.call-start = ((), (), s32[]{:S(2)}) async-start(), calls=%async_computation.78 | async-start | bytes 1327104
  2290.1 353.0 %reduce-scatter.71.cloned.1.call-start = ((), (), s32[]{:S(2)}) async-start(), calls=%async_computation.71 | async-start | bytes 1327104 | tf_op jit(solution)/shard_map/reduce_scatter | solution.py:323
  2296.9 386.4 %reduce-scatter.73.cloned.1.call-start = ((), (), s32[]{:S(2)}) async-start(), calls=%async_computation.72 | async-start | bytes 1327104 | tf_op jit(solution)/shard_map/reduce_scatter | solution.py:338
  2316.2 407.0 %reduce-scatter.63.cloned.1.call-start = ((), (), s32[]{:S(2)}) async-start(), calls=%async_computation.67 | async-start | bytes 1327104 | tf_op jit(solution)/shard_map/reduce_scatter | solution.py:314
  2335.0 428.4 %reduce-scatter.69.cloned.1.call-start = ((), (), s32[]{:S(2)}) async-start(), calls=%async_computation.70 | async-start | bytes 1327104 | tf_op jit(solution)/shard_map/reduce_scatter | solution.py:335
  2342.1 461.2 %reduce-scatter.65.cloned.1.call-start = ((), (), s32[]{:S(2)}) async-start(), calls=%async_computation.68 | async-start | bytes 1327104 | tf_op jit(solution)/shard_map/reduce_scatter | solution.py:317
  2351.4 492.3 %reduce-scatter.67.cloned.1.call-start = ((), (), s32[]{:S(2)}) async-start(), calls=%async_computation.69 | async-start | bytes 1327104 | tf_op jit(solution)/shard_map/reduce_scatter | solution.py:320
  2412.2 518.9 %reduce-scatter.51.cloned.1.call-start = ((), (), s32[]{:S(2)}) async-start(), calls=%async_computation.58 | async-start | bytes 5898240 | tf_op jit(solution)/shard_map/reduce_scatter | solution.py:47
  2419.0 600.2 %reduce-scatter.61.cloned.1.call-start = ((), (), s32[]{:S(2)}) async-start(), calls=%async_computation.65 | async-start | bytes 5898240 | tf_op jit(solution)/shard_map/reduce_scatter | solution.py:47
  2427.0 736.8 %all-reduce.3.cloned.1.call-start = ((), (), s32[]{:S(2)}) async-start(), calls=%async_computation.66 | async-start | bytes 6291456 | tf_op jit(solution)/shard_map/psum | solution.py:345
  (147 other events, 12099.1 us)
Sparse Core Ops, SparseCore 0:
  253.7 85.2 reduce-scatter.30
  499.9 85.2 reduce-scatter.32
  788.4 85.2 reduce-scatter.42
  875.8 85.7 reduce-scatter.34
  965.5 50.9 all-gather.68
  1070.3 84.0 reduce-scatter.44
  1373.8 84.0 reduce-scatter.36
  1461.7 50.9 all-gather.64
  1522.6 84.0 reduce-scatter.38
  1610.1 50.9 all-gather.66
  1730.5 84.0 reduce-scatter.52
  1818.7 50.9 all-gather.72
  1884.5 84.0 reduce-scatter.54
  1970.9 85.7 reduce-scatter.40
  2061.3 50.9 all-gather.74
  2181.7 52.7 reduce-scatter.56
  2238.2 53.9 reduce-scatter.46
  2295.5 53.8 reduce-scatter.58
  2353.3 53.8 reduce-scatter.48
  2410.6 53.8 reduce-scatter.74
  2468.4 53.8 reduce-scatter.76
  2845.8 85.2 reduce-scatter.50
  2933.4 85.7 reduce-scatter.60
  3025.1 138.5 all-reduce.2
  (29 shorter events, 1068.9 us)
where the time goes:
time: 3180 us; the launch traced here: 3170 us
  waiting for transfers between devices  2410 us (76%)
  matrix products  458 us (14%)
  other arithmetic  144 us (5%)
  local copies, waits for them, and re-layouts  99 us (3%)
  blocking collectives  42.8 us (1%)
    reduce_scatter x6, waiting for transfers between devices, fold_rows(): return lax.psum_scatter(values, 'tp', scatter_dimension=1, tiled=True)  507 us
    reduce_scatter x6, waiting for transfers between devices, fold_grads(): return lax.psum_scatter(values, 'tp', scatter_dimension=1, tiled=True)  485 us
    all_gather x6, waiting for transfers between devices, spread_rows(): return lax.all_gather(values, 'tp', axis=1, tiled=True)  288 us
    all_gather x6, waiting for transfers between devices, spread_grads(): return lax.all_gather(values, 'tp', axis=1, tiled=True)  267 us
    dot_general x20, matrix products, project(): jnp.einsum('cfd,de->cfe', left_side, right_side, preferred_element_type=j...  94 us
    psum x1, waiting for transfers between devices, body(): lax.psum((jnp.stack(text_grads), norm_totals[0], norm_totals[1], norm_tot...  90.6 us
    dot_general x16, matrix products, weight_grad(): jnp.einsum('cfd,cfe->de', left_side, right_side, preferred_element_type=j...  73.2 us
    all_gather x2, waiting for transfers between devices, body(): lax.all_gather(key_local, 'fsdp', axis=1, tiled=True)  71.8 us
  transfers between devices with their start and end apart: 53, of which 50 were waited for; matrix products, arithmetic and copies ran while one was open for 14% of the time, Pallas kernels for 0%

commit v1 on v0

--- a/solution.py
+++ b/solution.py
@@ -3,6 +3,8 @@
 import jax
 import jax.numpy as jnp
 from jax import lax
+from jax.experimental import pallas as pl
+from jax.experimental.pallas import tpu as pltpu
 from jax.sharding import PartitionSpec as P
 
 HD = 64
@@ -389,52 +391,580 @@
     )
 
 
+def pair_swap(values, axis_name):
+    return lax.ppermute(values, axis_name, [(0, 1), (1, 0)])
+
+
+def ring_shift(values, distance):
+    size = lax.axis_size("z")
+    return lax.ppermute(values, "z", [(i, (i + distance) % size) for i in range(size)])
+
+
+def ring_flip(values, bit):
+    size = lax.axis_size("z")
+    return lax.ppermute(values, "z", [(i, i ^ bit) for i in range(size)])
+
+
+def take(values, index, axis=0):
+    return lax.dynamic_index_in_dim(values, index, axis, keepdims=False)
+
+
+def place(values, piece, index, axis):
+    return lax.dynamic_update_index_in_dim(values, piece, index, axis)
+
+
+def ordered(index, own, other):
+    return jnp.where(index == 0, jnp.stack([own, other]), jnp.stack([other, own]))
+
+
+def to_clip(values):
+    at_y, at_z, size = lax.axis_index("y"), lax.axis_index("z"), lax.axis_size("z")
+    got = pair_swap(take(values, 1 - at_y), "y")
+    rows = ordered(at_y, take(values, at_y), got)
+    out = rows
+    for distance in range(1, size):
+        piece = ring_shift(take(rows, lax.rem(at_z + distance, size), 1), distance)
+        out = place(out, piece, lax.rem(at_z + size - distance, size), 1)
+    return out
+
+
+def from_clip(values):
+    at_y, at_z, size = lax.axis_index("y"), lax.axis_index("z"), lax.axis_size("z")
+    out = values
+    for distance in range(1, size):
+        piece = ring_shift(take(values, lax.rem(at_z + distance, size), 1), distance)
+        out = place(out, piece, lax.rem(at_z + size - distance, size), 1)
+    got = pair_swap(take(out, 1 - at_y), "y")
+    return ordered(at_y, take(out, at_y), got)
+
+
+def group_rows(values):
+    at_x, at_c = lax.axis_index("x"), lax.axis_index("c")
+    across = pair_swap(values, "x")
+    near = ordered(at_c, values, pair_swap(values, "c"))
+    far = ordered(at_c, across, pair_swap(across, "c"))
+    whole = ordered(at_x, near, far)
+    return jnp.transpose(whole, (2, 0, 1, 3, 4)).reshape(-1, values.shape[-1])
+
+
+def group_sum(values):
+    at_x, at_c = lax.axis_index("x"), lax.axis_index("c")
+    parts = values.astype(jnp.bfloat16).reshape(2, 2, 2, -1, values.shape[-1])
+    far_mine = take(take(parts, 1 - at_x, 1), at_c, 1)
+    far_send = take(take(parts, 1 - at_x, 1), 1 - at_c, 1)
+    near_mine = take(take(parts, at_x, 1), at_c, 1)
+    near_send = take(take(parts, at_x, 1), 1 - at_c, 1)
+    far = far_mine.astype(jnp.float32) + pair_swap(far_send, "c").astype(jnp.float32)
+    got = pair_swap(far.astype(jnp.bfloat16), "x")
+    near = near_mine.astype(jnp.float32) + pair_swap(near_send, "c").astype(jnp.float32)
+    return near + got.astype(jnp.float32)
+
+
+def ring_gather(own):
+    at_z, size = lax.axis_index("z"), lax.axis_size("z")
+    out = place(jnp.zeros((size,) + own.shape, own.dtype), own, at_z, 0)
+    piece = own
+    for distance in range(1, size):
+        piece = ring_shift(piece, 1)
+        out = place(out, piece, lax.rem(at_z + size - distance, size), 0)
+    return out
+
+
+def ring_sum(parts):
+    at_z, size = lax.axis_index("z"), lax.axis_size("z")
+    moving = take(parts, lax.rem(at_z + size - 1, size))
+    for step in range(1, size):
+        got = ring_shift(moving, 1)
+        mine = take(parts, lax.rem(at_z + 2 * size - 1 - step, size))
+        total = got.astype(jnp.float32) + mine.astype(jnp.float32)
+        moving = total.astype(jnp.bfloat16)
+    return total
+
+
+def gather_units(shard, count):
+    at_y, at_x, at_c = lax.axis_index("y"), lax.axis_index("x"), lax.axis_index("c")
+    rows = shard.shape[0]
+    width = shard.shape[1] // count // 2
+    split = jnp.transpose(shard.reshape(rows, count, 2, width), (2, 1, 0, 3))
+    mine = ordered(at_x, take(split, at_x), pair_swap(take(split, 1 - at_x), "x"))
+    ring = ring_gather(mine)
+    size = ring.shape[0]
+    across = pair_swap(ring, "y")
+
+    def halves(values):
+        by_core = values.reshape((2, size // 2) + values.shape[1:])
+        return ordered(at_c, take(by_core, at_c), pair_swap(take(by_core, 1 - at_c), "c"))
+
+    whole = ordered(at_y, halves(ring), halves(across))
+    whole = jnp.transpose(whole, (0, 3, 1, 5, 4, 2, 6))
+    return whole.reshape(8 * rows, count, (size // 2) * width)
+
+
+def sum_units(grad):
+    at_y, at_x, at_c = lax.axis_index("y"), lax.axis_index("x"), lax.axis_index("c")
+    size = lax.axis_size("z")
+    dim, count, units = grad.shape
+    rows = dim // 8
+    width = units // (size // 2)
+    parts = grad.astype(jnp.bfloat16).reshape(2, 2, 2, rows, count, size // 2, width)
+    parts = jnp.transpose(parts, (2, 0, 5, 1, 4, 3, 6))
+    mine, away = take(parts, at_c), pair_swap(take(parts, 1 - at_c), "c")
+    whole = ordered(at_c, mine, away)
+    whole = jnp.swapaxes(whole, 0, 1)
+    got = pair_swap(take(whole, 1 - at_y), "y").astype(jnp.float32)
+    total = (take(whole, at_y).astype(jnp.float32) + got).astype(jnp.bfloat16)
+    total = ring_sum(total.reshape((size,) + total.shape[2:])).astype(jnp.bfloat16)
+    mine, away = take(total, at_x), pair_swap(take(total, 1 - at_x), "x")
+    halves = ordered(at_x, mine, away)
+    return jnp.transpose(halves, (2, 1, 0, 3)).reshape(rows, -1).astype(jnp.float32)
+
+
+def gather_whole(shard, count):
+    at_y, at_x, at_c = lax.axis_index("y"), lax.axis_index("x"), lax.axis_index("c")
+    rows = shard.shape[0]
+    width = shard.shape[1] // count
+    ring = ring_gather(jnp.transpose(shard.reshape(rows, count, width), (1, 0, 2)))
+    pair = ordered(at_y, ring, pair_swap(ring, "y"))
+    quad = ordered(at_x, pair, pair_swap(pair, "x"))
+    whole = ordered(at_c, quad, pair_swap(quad, "c"))
+    whole = jnp.transpose(whole, (4, 2, 1, 0, 5, 3, 6))
+    return whole.reshape(count, 8 * rows, -1)
+
+
+def sum_whole(grads):
+    at_y, at_x, at_c = lax.axis_index("y"), lax.axis_index("x"), lax.axis_index("c")
+    size = lax.axis_size("z")
+    count, dim, units = grads.shape
+    rows = dim // 8
+    parts = grads.astype(jnp.bfloat16).reshape(count, 2, 2, 2, rows, size, units // size)
+    parts = jnp.transpose(parts, (3, 2, 1, 5, 0, 4, 6))
+
+    def fold(values, at, name):
+        got = pair_swap(take(values, 1 - at), name).astype(jnp.float32)
+        return (take(values, at).astype(jnp.float32) + got).astype(jnp.bfloat16)
+
+    parts = fold(fold(fold(parts, at_c, "c"), at_x, "x"), at_y, "y")
+    total = ring_sum(parts)
+    return jnp.transpose(total, (1, 0, 2)).reshape(rows, -1)
+
+
+def everywhere(values):
+    for name in ("c", "x", "y"):
+        values = values + pair_swap(values, name)
+    bit = 1
+    while bit < lax.axis_size("z"):
+        values = values + ring_flip(values, bit)
+        bit *= 2
+    return values
+
+
+def dot_nt(left, right):
+    return lax.dot_general(left, right, (((1,), (1,)), ((), ())), preferred_element_type=jnp.float32)
+
+
+def dot_nn(left, right):
+    return lax.dot_general(left, right, (((1,), (0,)), ((), ())), preferred_element_type=jnp.float32)
+
+
+def dot_tn(left, right):
+    return lax.dot_general(left, right, (((0,), (0,)), ((), ())), preferred_element_type=jnp.float32)
+
+
+BLOCK = 256
+
+
+def diagonal_mask(size):
+    row = lax.broadcasted_iota(jnp.int32, (size, size), 0)
+    column = lax.broadcasted_iota(jnp.int32, (size, size), 1)
+    return column <= row
+
+
+def self_forward_kernel(q_ref, k_ref, v_ref, o_ref, l_ref):
+    frames = q_ref.shape[0]
+    mask = diagonal_mask(BLOCK)
+    for head in range(2):
+        lanes = slice(head * HD, (head + 1) * HD)
+        for at in range(0, frames, BLOCK):
+            rows = slice(at, at + BLOCK)
+            q = q_ref[rows, lanes] * jnp.bfloat16(1.0 / math.sqrt(HD))
+            near = jnp.where(mask, dot_nt(q, k_ref[rows, lanes]), MASKED)
+            top = jnp.max(near, axis=-1, keepdims=True)
+            if at:
+                past = dot_nt(q, k_ref[0:at, lanes])
+                top = jnp.maximum(top, jnp.max(past, axis=-1, keepdims=True))
+            near = jnp.exp(near - top)
+            total = jnp.sum(near, axis=-1, keepdims=True)
+            out = dot_nn(near.astype(jnp.bfloat16), v_ref[rows, lanes])
+            if at:
+                past = jnp.exp(past - top)
+                total = total + jnp.sum(past, axis=-1, keepdims=True)
+                out = out + dot_nn(past.astype(jnp.bfloat16), v_ref[0:at, lanes])
+            o_ref[rows, lanes] = (out / total).astype(jnp.bfloat16)
+            l_ref[rows, lanes] = jnp.broadcast_to(top + jnp.log(total), (BLOCK, HD))
+
+
+def self_backward_kernel(
+    q_ref, k_ref, v_ref, o_ref, l_ref, g_ref, dq_ref, dk_ref, dv_ref, dk_sum, dv_sum
+):
+    frames = q_ref.shape[0]
+    mask = diagonal_mask(BLOCK)
+    factor = 1.0 / math.sqrt(HD)
+    dk_sum[...] = jnp.zeros_like(dk_sum)
+    dv_sum[...] = jnp.zeros_like(dv_sum)
+    for head in range(2):
+        lanes = slice(head * HD, (head + 1) * HD)
+        for at in range(0, frames, BLOCK):
+            rows = slice(at, at + BLOCK)
+            q = q_ref[rows, lanes] * jnp.bfloat16(factor)
+            grad = g_ref[rows, lanes]
+            q_turned = q.astype(jnp.float32).T.astype(jnp.bfloat16)
+            grad_turned = grad.astype(jnp.float32).T.astype(jnp.bfloat16)
+            log_total = l_ref[rows, lanes][:, 0:1]
+            row_total = jnp.sum(
+                grad.astype(jnp.float32) * o_ref[rows, lanes].astype(jnp.float32),
+                axis=-1,
+                keepdims=True,
+            )
+            dq = None
+            for columns in (rows, slice(0, at)):
+                if columns.stop == 0:
+                    continue
+                keys = k_ref[columns, lanes]
+                weights = jnp.exp(dot_nt(q, keys) - log_total)
+                if columns is rows:
+                    weights = jnp.where(mask, weights, 0.0)
+                back = dot_nt(grad, v_ref[columns, lanes])
+                scores = (weights * (back - row_total)).astype(jnp.bfloat16)
+                part = dot_nn(scores, keys)
+                dq = part if dq is None else dq + part
+                dk_sum[lanes, columns] += dot_nn(q_turned, scores)
+                dv_sum[lanes, columns] += dot_nn(grad_turned, weights.astype(jnp.bfloat16))
+            dq_ref[rows, lanes] = (dq * factor).astype(jnp.bfloat16)
+    for at in range(0, frames, BLOCK):
+        rows = slice(at, at + BLOCK)
+        dk_ref[rows, :] = dk_sum[:, rows].T.astype(jnp.bfloat16)
+        dv_ref[rows, :] = dv_sum[:, rows].T.astype(jnp.bfloat16)
+
+
+def pair_spec(rows, offset=0):
+    return pl.BlockSpec((rows, 2 * HD), lambda i: (0, i + offset))
+
+
+def self_forward(qkv):
+    frames, width = qkv.shape[0], qkv.shape[1] // 3
+    pairs = width // (2 * HD)
+    cost = pl.CostEstimate(
+        flops=8 * frames * frames * width, bytes_accessed=14 * frames * width, transcendentals=0
+    )
+    return pl.pallas_call(
+        self_forward_kernel,
+        grid=(pairs,),
+        in_specs=[pair_spec(frames, i * pairs) for i in range(3)],
+        out_specs=[pair_spec(frames)] * 2,
+        out_shape=[
+            jax.ShapeDtypeStruct((frames, width), jnp.bfloat16),
+            jax.ShapeDtypeStruct((frames, width), jnp.float32),
+        ],
+        compiler_params=pltpu.CompilerParams(vmem_limit_bytes=40 * 2**20),
+        cost_estimate=cost,
+    )(qkv, qkv, qkv)
+
+
+def self_backward(qkv, mixed, log_total, grad_mixed):
+    frames, width = mixed.shape
+    pairs = width // (2 * HD)
+    cost = pl.CostEstimate(
+        flops=20 * frames * frames * width, bytes_accessed=20 * frames * width, transcendentals=0
+    )
+    return pl.pallas_call(
+        self_backward_kernel,
+        grid=(pairs,),
+        in_specs=[pair_spec(frames, i * pairs) for i in range(3)] + [pair_spec(frames)] * 3,
+        out_specs=[pair_spec(frames)] * 3,
+        out_shape=[jax.ShapeDtypeStruct((frames, width), jnp.bfloat16)] * 3,
+        scratch_shapes=[pltpu.VMEM((2 * HD, frames), jnp.float32)] * 2,
+        compiler_params=pltpu.CompilerParams(vmem_limit_bytes=40 * 2**20),
+        cost_estimate=cost,
+    )(qkv, qkv, qkv, mixed, log_total, grad_mixed)
+
+
+def block_pair(values):
+    low = lax.broadcasted_iota(jnp.int32, values.shape, 1) < HD
+    zero = jnp.zeros_like(values)
+    return jnp.concatenate([jnp.where(low, values, zero), jnp.where(low, zero, values)], axis=0)
+
+
+def by_half(low, values, reduce, empty):
+    first = reduce(jnp.where(low, values, empty), axis=-1, keepdims=True)
+    second = reduce(jnp.where(low, empty, values), axis=-1, keepdims=True)
+    return jnp.where(low, first, second)
+
+
+def cross_weights(count, queries, keys):
+    slots = keys.shape[0] // 2
+    scores = dot_nt(queries, keys)
+    lane = lax.broadcasted_iota(jnp.int32, scores.shape, 1)
+    low = lane < slots
+    scores = jnp.where(jnp.where(low, lane, lane - slots) < count, scores, MASKED)
+    raised = jnp.exp(scores - by_half(low, scores, jnp.max, MASKED))
+    return raised / by_half(low, raised, jnp.sum, 0.0), low
+
+
+def cross_forward_kernel(count_ref, q_ref, k_ref, v_ref, o_ref):
+    queries = q_ref[...] * jnp.bfloat16(1.0 / math.sqrt(HD))
+    weights, _ = cross_weights(count_ref[0], queries, block_pair(k_ref[...]))
+    o_ref[...] = dot_nn(weights.astype(jnp.bfloat16), block_pair(v_ref[...])).astype(jnp.bfloat16)
+
+
+def cross_backward_kernel(count_ref, q_ref, k_ref, v_ref, g_ref, dq_ref, dk_ref, dv_ref):
+    factor = 1.0 / math.sqrt(HD)
+    queries = q_ref[...] * jnp.bfloat16(factor)
+    keys = block_pair(k_ref[...])
+    weights, low = cross_weights(count_ref[0], queries, keys)
+    grad = g_ref[...]
+    back = dot_nt(grad, block_pair(v_ref[...]))
+    scores = weights * (back - by_half(low, back * weights, jnp.sum, 0.0))
+    scores = scores.astype(jnp.bfloat16)
+    dq_ref[...] = (dot_nn(scores, keys) * factor).astype(jnp.bfloat16)
+    slots = k_ref.shape[0]
+    dims_low = lax.broadcasted_iota(jnp.int32, k_ref.shape, 1) < HD
+    dk = dot_tn(scores, queries)
+    dk_ref[...] = jnp.where(dims_low, dk[:slots], dk[slots:])
+    dv = dot_tn(weights.astype(jnp.bfloat16), grad)
+    dv_ref[...] = jnp.where(dims_low, dv[:slots], dv[slots:])
+
+
+def cross_forward(count, queries, keys_values):
+    rows, width = queries.shape
+    slots = keys_values.shape[0]
+    pairs = width // (2 * HD)
+    return pl.pallas_call(
+        cross_forward_kernel,
+        grid=(pairs,),
+        in_specs=[
+            pl.BlockSpec(memory_space=pltpu.SMEM),
+            pair_spec(rows),
+            pair_spec(slots),
+            pair_spec(slots, pairs),
+        ],
+        out_specs=pair_spec(rows),
+        out_shape=jax.ShapeDtypeStruct((rows, width), jnp.bfloat16),
+        cost_estimate=pl.CostEstimate(
+            flops=8 * rows * slots * width, bytes_accessed=6 * rows * width, transcendentals=0
+        ),
+    )(count, queries, keys_values, keys_values)
+
+
+def cross_backward(count, queries, keys_values, grad_mixed):
+    rows, width = queries.shape
+    slots = keys_values.shape[0]
+    pairs = width // (2 * HD)
+    return pl.pallas_call(
+        cross_backward_kernel,
+        grid=(pairs,),
+        in_specs=[
+            pl.BlockSpec(memory_space=pltpu.SMEM),
+            pair_spec(rows),
+            pair_spec(slots),
+            pair_spec(slots, pairs),
+            pair_spec(rows),
+        ],
+        out_specs=[pair_spec(rows), pair_spec(slots), pair_spec(slots)],
+        out_shape=[
+            jax.ShapeDtypeStruct((rows, width), jnp.bfloat16),
+            jax.ShapeDtypeStruct((slots, width), jnp.float32),
+            jax.ShapeDtypeStruct((slots, width), jnp.float32),
+        ],
+        cost_estimate=pl.CostEstimate(
+            flops=20 * rows * slots * width, bytes_accessed=10 * rows * width, transcendentals=0
+        ),
+    )(count, queries, keys_values, keys_values, grad_mixed)
+
+
+def clip_body(
+    tokens,
+    memory,
+    text_len,
+    cotangent,
+    gain_one,
+    bias_one,
+    gain_two,
+    bias_two,
+    gain_three,
+    bias_three,
+    w_query,
+    w_key,
+    w_value,
+    w_out,
+    c_query,
+    c_key,
+    c_value,
+    c_out,
+    w_up,
+    w_down,
+):
+    at_y, at_x, at_c, at_z = (lax.axis_index(name) for name in ("y", "x", "c", "z"))
+    model = tokens.shape[-1]
+    shard_rows, shard_width = w_query.shape
+    slots = memory.shape[2]
+
+    frames = to_clip(tokens).reshape(2, -1, model).astype(jnp.float32)
+    attend_shard = jnp.concatenate([w_query, w_key, w_value, w_out.T], axis=1)
+    attend_full = gather_units(attend_shard, 4)
+    qkv_full = attend_full[:, :3].reshape(model, -1)
+    out_full = attend_full[:, 3]
+    cross_full = gather_whole(jnp.concatenate([c_query, c_out.T], axis=1), 2)
+    cross_query, cross_out = cross_full[0], cross_full[1]
+    up_full = gather_units(w_up, 1)[:, 0]
+    down_full = gather_units(w_down.T, 1)[:, 0]
+    upstream = to_clip(cotangent).reshape(2, -1, model)
+    grad_rows3 = group_rows(upstream)
+
+    at_f = (at_y * 2 + at_x) * 2 + at_c
+    text_flat = memory.reshape(-1, model)
+    text_mine = lax.dynamic_slice_in_dim(text_flat, at_f * shard_rows, shard_rows, 1)
+    text_shard = jnp.concatenate([c_key, c_value], axis=1)
+    text_part = dot_nn(text_mine, text_shard).astype(jnp.bfloat16)
+    text_part = text_part.reshape(2, -1, slots, 2 * shard_width)
+    got = pair_swap(take(text_part, 1 - at_y), "y").astype(jnp.float32)
+    text_part = (take(text_part, at_y).astype(jnp.float32) + got).astype(jnp.bfloat16)
+    size = text_part.shape[0]
+    text_clip = text_part
+    for distance in range(1, size):
+        piece = ring_shift(take(text_part, lax.rem(at_z + distance, size)), distance)
+        text_clip = place(text_clip, piece, lax.rem(at_z + size - distance, size), 0)
+    text_clip = text_clip.astype(jnp.float32)
+    for name in ("x", "c"):
+        text_clip = text_clip.astype(jnp.bfloat16)
+        text_clip = text_clip.astype(jnp.float32) + pair_swap(text_clip, name).astype(jnp.float32)
+    text_clip = text_clip.astype(jnp.bfloat16).reshape(size, slots, 2, shard_width)
+    keys_values = jnp.transpose(text_clip, (1, 2, 0, 3)).reshape(slots, -1)
+    count = take(take(text_len, at_y), at_z).reshape(1)
+
+    normed_one, scaled_one, inverse_one = layer_norm(frames, gain_one, bias_one)
+    rows_one = group_rows(normed_one.astype(jnp.bfloat16))
+    qkv = dot_nn(rows_one, qkv_full).astype(jnp.bfloat16)
+    mixed_one, log_total = self_forward(qkv)
+    after_self = frames + group_sum(dot_nt(mixed_one, out_full))
+    normed_two, scaled_two, inverse_two = layer_norm(after_self, gain_two, bias_two)
+    rows_two = normed_two.astype(jnp.bfloat16).reshape(-1, model)
+    cross_q = dot_nn(rows_two, cross_query).astype(jnp.bfloat16)
+    mixed_two = cross_forward(count, cross_q, keys_values)
+    after_cross = after_self + dot_nt(mixed_two, cross_out).reshape(after_self.shape)
+    normed_three, scaled_three, inverse_three = layer_norm(after_cross, gain_three, bias_three)
+    rows_three = group_rows(normed_three.astype(jnp.bfloat16))
+    hidden = dot_nn(rows_three, up_full)
+    active = jax.nn.gelu(hidden).astype(jnp.bfloat16)
+
+    grad_active = dot_nn(grad_rows3, down_full)
+    _, gelu_pull = jax.vjp(jax.nn.gelu, hidden)
+    grad_hidden = gelu_pull(grad_active)[0].astype(jnp.bfloat16)
+    grad_three = group_sum(dot_nt(grad_hidden, up_full))
+    back_three, gain_g3, bias_g3 = norm_back(grad_three, scaled_three, inverse_three, gain_three)
+    grad_two_rows = upstream.astype(jnp.float32) + back_three
+    fin_down = sum_units(dot_tn(grad_rows3, active)[:, None])
+    fin_up = sum_units(dot_tn(rows_three, grad_hidden)[:, None])
+
+    result = after_cross + group_sum(dot_nt(active, down_full))
+    result = from_clip(result.astype(jnp.bfloat16).reshape(2, size, -1, model))
+
+    grad_rows2 = grad_two_rows.astype(jnp.bfloat16).reshape(-1, model)
+    grad_mixed2 = dot_nn(grad_rows2, cross_out).astype(jnp.bfloat16)
+    grad_cq, grad_ck, grad_cv = cross_backward(count, cross_q, keys_values, grad_mixed2)
+    grad_two = dot_nt(grad_cq, cross_query).reshape(after_self.shape)
+    back_two, gain_g2, bias_g2 = norm_back(grad_two, scaled_two, inverse_two, gain_two)
+    grad_one_rows = grad_two_rows + back_two
+    fin_cross = sum_whole(jnp.stack([dot_tn(rows_two, grad_cq), dot_tn(grad_rows2, mixed_two)]))
+    fin_cquery, fin_cout = fin_cross[:, :shard_width], fin_cross[:, shard_width:].T
+
+    grad_text = jnp.stack([grad_ck, grad_cv]).reshape(2, slots, size, shard_width)
+    grad_text = jnp.transpose(grad_text, (2, 1, 0, 3)).reshape(size, slots, 2 * shard_width)
+    for name in ("x", "c"):
+        grad_text = grad_text.astype(jnp.bfloat16)
+        grad_text = grad_text.astype(jnp.float32) + pair_swap(grad_text, name).astype(jnp.float32)
+    grad_text = grad_text.astype(jnp.bfloat16)
+    spread = grad_text
+    for distance in range(1, size):
+        piece = ring_shift(take(grad_text, lax.rem(at_z + distance, size)), distance)
+        spread = place(spread, piece, lax.rem(at_z + size - distance, size), 0)
+    spread = ordered(at_y, spread, pair_swap(spread, "y")).reshape(-1, 2 * shard_width)
+    fin_text = dot_tn(text_mine, spread)
+    fin_ckey, fin_cvalue = fin_text[:, :shard_width], fin_text[:, shard_width:]
+    grad_memory = dot_nt(spread, text_shard)
+    bit = 1
+    while bit < size:
+        grad_memory = grad_memory.astype(jnp.bfloat16)
+        grad_memory = grad_memory.astype(jnp.float32) + ring_flip(grad_memory, bit).astype(
+            jnp.float32
+        )
+        bit *= 2
+    grad_memory = grad_memory.astype(jnp.bfloat16)
+    for at, name in ((at_c, "c"), (at_x, "x"), (at_y, "y")):
+        grad_memory = ordered(at, grad_memory, pair_swap(grad_memory, name))
+    grad_memory = jnp.transpose(grad_memory.reshape(8, -1, shard_rows), (1, 0, 2))
+    grad_memory = grad_memory.reshape(memory.shape).astype(jnp.float32)
+
+    grad_rows1 = group_rows(grad_one_rows.astype(jnp.bfloat16))
+    grad_mixed1 = dot_nn(grad_rows1, out_full).astype(jnp.bfloat16)
+    grad_q, grad_k, grad_v = self_backward(qkv, mixed_one, log_total, grad_mixed1)
+    grad_qkv = jnp.concatenate([grad_q, grad_k, grad_v], axis=1)
+    grad_one = group_sum(dot_nt(grad_qkv, qkv_full))
+    back_one, gain_g1, bias_g1 = norm_back(grad_one, scaled_one, inverse_one, gain_one)
+    input_grad = (grad_one_rows + back_one).astype(jnp.bfloat16)
+    input_grad = from_clip(input_grad.reshape(2, size, -1, model)).astype(jnp.float32)
+    grad_attend = jnp.concatenate(
+        [dot_tn(rows_one, grad_qkv), dot_tn(grad_rows1, mixed_one)], axis=1
+    )
+    fin_attend = sum_units(grad_attend.reshape(model, 4, -1))
+    fin_query, fin_key, fin_value, fin_out = (
+        fin_attend[:, i * shard_width : (i + 1) * shard_width] for i in range(4)
+    )
+
+    early = everywhere(jnp.stack([gain_g2, bias_g2, gain_g3, bias_g3]))
+    late = everywhere(jnp.stack([gain_g1, bias_g1]))
+    return (
+        result,
+        input_grad,
+        grad_memory,
+        late[0],
+        late[1],
+        early[0],
+        early[1],
+        early[2],
+        early[3],
+        fin_query,
+        fin_key,
+        fin_value,
+        fin_out.T,
+        fin_cquery,
+        fin_ckey,
+        fin_cvalue,
+        fin_cout,
+        fin_up,
+        fin_down.T,
+    )
+
+
+def clip_groups(mesh):
+    outer, inner = mesh.shape["fsdp"], mesh.shape["tp"]
+    return (2, 2, 2, inner) if outer == 8 and inner == 4 else None
+
+
 def solution(mesh):
+    sizes = clip_groups(mesh)
+    if sizes is None:
+        rows, columns, program, used = "fsdp", "tp", body, mesh
+    else:
+        rows, columns, program = ("y", "x", "c"), "z", clip_body
+        used = jax.sharding.Mesh(mesh.devices.reshape(sizes), ("y", "x", "c", "z"))
+    both = ("fsdp", "tp") if sizes is None else ("y", "x", "c", "z")
+    frames = P(None, None, both, None)
+    tall, wide = P(rows, columns), P(columns, rows)
+    weights = (tall, tall, tall, wide, tall, tall, tall, wide, tall, wide)
     return jax.shard_map(
-        body,
-        mesh=mesh,
-        in_specs=(
-            P(None, None, ("fsdp", "tp"), None),
-            P(),
-            P(),
-            P(None, None, ("fsdp", "tp"), None),
-            P(),
-            P(),
-            P(),
-            P(),
-            P(),
-            P(),
-            P("fsdp", "tp"),
-            P("fsdp", "tp"),
-            P("fsdp", "tp"),
-            P("tp", "fsdp"),
-            P("fsdp", "tp"),
-            P("fsdp", "tp"),
-            P("fsdp", "tp"),
-            P("tp", "fsdp"),
-            P("fsdp", "tp"),
-            P("tp", "fsdp"),
-        ),
-        out_specs=(
-            P(None, None, ("fsdp", "tp"), None),
-            P(None, None, ("fsdp", "tp"), None),
-            P(),
-            P(),
-            P(),
-            P(),
-            P(),
-            P(),
-            P(),
-            P("fsdp", "tp"),
-            P("fsdp", "tp"),
-            P("fsdp", "tp"),
-            P("tp", "fsdp"),
-            P("fsdp", "tp"),
-            P("fsdp", "tp"),
-            P("fsdp", "tp"),
-            P("tp", "fsdp"),
-            P("fsdp", "tp"),
-            P("tp", "fsdp"),
-        ),
+        program,
+        mesh=used,
+        in_specs=(frames, P(), P(), frames) + (P(),) * 6 + weights,
+        out_specs=(frames, frames, P()) + (P(),) * 6 + weights,
         check_vma=False,
     )

time: 3180 us -> 1520 us (0.48)
  waiting for transfers between devices: 2410 us -> 576 us
  matrix products: 458 us -> 143 us
  local copies, waits for them, and re-layouts: 99 us -> 398 us
  starting transfers between devices: 5.43 us -> 100 us
  other arithmetic: 144 us -> 214 us
  Pallas kernels: 0 us -> 69.8 us
  blocking collectives: 42.8 us -> 0 us
    reduce_scatter x24 -> x0, waiting for transfers between devices: 1360 us -> none  [the longest x6 507 us: fold_rows(): return lax.psum_scatter(values, 'tp', scatter_dimension=1, tiled=True)]
    all_gather x26 -> x0, waiting for transfers between devices: 890 us -> none  [the longest x6 288 us: spread_rows(): return lax.all_gather(values, 'tp', axis=1, tiled=True)]
    ppermute x0 -> x118, waiting for transfers between devices: none -> 576 us  [the longest x70 374 us: pair_swap(): return lax.ppermute(values, axis_name, [(0, 1), (1, 0)])]
    dot_general x84 -> x21, matrix products: 458 us -> 143 us  [the longest x7 52.5 us: dot_nn(): lax.dot_general(left, right, (((1,), (0,)), ((), ())), preferred_element_...]
    ppermute x0 -> x118, starting transfers between devices: none -> 100 us  [the longest x42 54.2 us: ring_shift(): lax.ppermute(values, 'z', [(i, (i + distance) % size) for i in range(size)])]
    psum x1 -> x0, waiting for transfers between devices: 90.6 us -> none  [body(): lax.psum((jnp.stack(text_grads), norm_totals[0], norm_totals[1], norm_tot...]
    select_n x0 -> x29, other arithmetic: none -> 73.2 us  [ordered(): jnp.where(index == 0, jnp.stack([own, other]), jnp.stack([other, own]))]
    unnamed x55 -> x0, waiting for transfers between devices: 71.8 us -> none
  transfers between devices with their start and end apart: 53 -> 118, of which waited for: 50 -> 45; matrix products, arithmetic and copies ran while one was open for 14% -> 46% of each run, Pallas kernels for 0% -> 5%
where the time goes in v1:
time: 1520 us; the launch traced here: 1510 us
  waiting for transfers between devices  576 us (38%)
  local copies, waits for them, and re-layouts  398 us (26%)
  other arithmetic  214 us (14%)
  matrix products  143 us (9%)
  starting transfers between devices  100 us (7%)
  Pallas kernels  69.8 us (5%)
    ppermute x70, waiting for transfers between devices, pair_swap(): return lax.ppermute(values, axis_name, [(0, 1), (1, 0)])  374 us
    ppermute x42, waiting for transfers between devices, ring_shift(): lax.ppermute(values, 'z', [(i, (i + distance) % size) for i in range(size)])  180 us
    unnamed x249, local copies, waits for them, and re-layouts  86.2 us
    select_n x29, other arithmetic, ordered(): jnp.where(index == 0, jnp.stack([own, other]), jnp.stack([other, own]))  73.2 us
    dynamic_update_slice x25, local copies, waits for them, and re-layouts, place(): return lax.dynamic_update_index_in_dim(values, piece, index, axis)  66.8 us
    ppermute x42, starting transfers between devices, ring_shift(): lax.ppermute(values, 'z', [(i, (i + distance) % size) for i in range(size)])  54.2 us
    dot_general x7, matrix products, dot_nn(): lax.dot_general(left, right, (((1,), (0,)), ((), ())), preferred_element_...  52.5 us
    dot_general x7, matrix products, dot_nt(): lax.dot_general(left, right, (((1,), (1,)), ((), ())), preferred_element_...  48.9 us
  transfers between devices with their start and end apart: 118, of which 45 were waited for; matrix products, arithmetic and copies ran while one was open for 46% of the time, Pallas kernels for 5%

profile of v1, /device:TPU:0, one launch (start us, length us, event | category | flops | bytes accessed | tf_op | source)
XLA Modules:
  0.0 1505.2 jit_solution(10222729705486740425)
XLA Ops:
  99.9 19.0 %collective-permute-done.25 = bf16[64,768]{1,0:T(8,128)(2,1)S(1)} collective-permute-done((bf16[64,768]{1,0:T(8,128)(2,1)S(1)}, bf16[64,768]{1,0:T(8,128)(2,1)S(1)}, u32[]{:S(2)}, u32[]{:S(2)}) %collective-permute-start.25) | collective-permute-done | bytes 98336 | tf_op jit(solution)/shard_map/ppermute | solution.py:400
  196.4 24.7 %collective-permute-done.55 = bf16[2,48,1536]{2,1,0:T(8,128)(2,1)} collective-permute-done((bf16[2,48,1536]{2,1,0:T(8,128)(2,1)}, bf16[2,48,1536]{2,1,0:T(8,128)(2,1)}, u32[]{:S(2)}, u32[]{:S(2)}) %collective-permute-start.55) | collective-permute-done | bytes 294944 | tf_op jit(solution)/shard_map/ppermute | solution.py:400
  228.6 13.9 collective-permute-done.9
  249.1 14.3 collective-permute-done.10
  302.7 19.8 %collective-permute-done.5 = bf16[2,192,1536]{2,1,0:T(8,128)(2,1)S(1)} collective-permute-done((bf16[2,192,1536]{2,1,0:T(8,128)(2,1)S(1)}, bf16[2,192,1536]{2,1,0:T(8,128)(2,1)S(1)}, u32[]{:S(2)}, u32[]{:S(2)}) %collective-permute-start.5) | collective-permute-done | bytes 1179680 | tf_op jit(solution)/shard_map/ppermute | solution.py:395
  328.7 36.5 %collective-permute-done.12 = bf16[4,2,4,192,192]{4,3,2,1,0:T(8,128)(2,1)S(1)} collective-permute-done((bf16[4,2,4,192,192]{4,3,2,1,0:T(8,128)(2,1)}, bf16[4,2,4,192,192]{4,3,2,1,0:T(8,128)(2,1)S(1)}, u32[]{:S(2)}, u32[]{:S(2)}) %collective-permute-start.12) | collective-permute-done | bytes 2359328 | tf_op jit(solution)/shard_map/ppermute | solution.py:395
  369.4 46.4 %collective-permute-done.37 = bf16[4,2,1,192,768]{4,3,1,0,2:T(8,128)(2,1)S(1)} collective-permute-done((bf16[4,2,1,192,768]{4,3,1,0,2:T(8,128)(2,1)}, bf16[4,2,1,192,768]{4,3,1,0,2:T(8,128)(2,1)S(1)}, u32[]{:S(2)}, u32[]{:S(2)}) %collective-permute-start.37) | collective-permute-done | bytes 2359328 | tf_op jit(solution)/shard_map/ppermute | solution.py:395
  417.5 48.5 %collective-permute-done.44 = bf16[4,2,1,192,768]{4,3,1,0,2:T(8,128)(2,1)S(1)} collective-permute-done((bf16[4,2,1,192,768]{4,3,1,0,2:T(8,128)(2,1)}, bf16[4,2,1,192,768]{4,3,1,0,2:T(8,128)(2,1)S(1)}, u32[]{:S(2)}, u32[]{:S(2)}) %collective-permute-start.44) | collective-permute-done | bytes 2359328 | tf_op jit(solution)/shard_map/ppermute | solution.py:395
  470.2 14.3 copy.203
  517.2 19.0 %shard_map.339 = (bf16[1536,384]{1,0:T(8,128)(2,1)S(1)}, f32[1536,384]{1,0:T(8,128)S(1)}) custom-call(bf16[1536,1152]{1,0:T(8,128)(2,1)S(1)} %convolution_convert_fusion.3.q_ref.k_ref.v_ref, bf16[1536,1152]{1,0:T(8,128)(2,1)S(1)} %convolution_convert_fusion.3.q_ref.k_ref.v_ref, bf16[1536,1152]{1,0:T(8,128)(2,1)S(1)} %convolution_convert_fusion.3.q_ref.k_ref.v_ref), custom_call_target="tpu_custom_call" | custom-call | flops 7247757312 | bytes 8257536 | tf_op jit(solution)/shard_map/pallas_call | solution.py:659
  601.1 14.3 fusion.7
  735.4 17.5 %fusion.6 = (bf16[1536,1536]{1,0:T(8,128)(2,1)S(1)}, f32[1536,1536]{1,0:T(8,128)}) fusion(f32[1536,1536]{1,0:T(8,128)} %fusion.74, bf16[1536,1536]{1,0:T(8,128)(2,1)S(1)} %bitcast.685, bf16[1536,1536]{1,0:T(8,128)(2,1)S(1)} %bitcast.679), kind=kOutput, calls=%fused_computation.12 | convolution fusion | flops 7294943232 | bytes 33030144 | tf_op jit(solution)/shard_map/dot_general | solution.py:566
  860.9 21.6 %collective-permute-done.48 = bf16[2,192,1536]{2,1,0:T(8,128)(2,1)S(1)} collective-permute-done((bf16[2,192,1536]{2,1,0:T(8,128)(2,1)}, bf16[2,192,1536]{2,1,0:T(8,128)(2,1)S(1)}, u32[]{:S(2)}, u32[]{:S(2)}) %collective-permute-start.48) | collective-permute-done | bytes 1179680 | tf_op jit(solution)/shard_map/ppermute | solution.py:395
  965.8 19.8 %collective-permute-done.50 = bf16[2,48,1536]{2,1,0:T(8,128)(2,1)S(1)} collective-permute-done((bf16[2,48,1536]{2,1,0:T(8,128)(2,1)S(1)}, bf16[2,48,1536]{2,1,0:T(8,128)(2,1)S(1)}, u32[]{:S(2)}, u32[]{:S(2)}) %collective-permute-start.50) | collective-permute-done | bytes 294944 | tf_op jit(solution)/shard_map/ppermute | solution.py:400
  1056.1 17.6 %collective-permute-done.113 = bf16[2,2,2,1,192,768]{5,4,2,1,0,3:T(8,128)(2,1)S(1)} collective-permute-done((bf16[2,2,2,1,192,768]{5,4,2,1,0,3:T(8,128)(2,1)S(1)}, bf16[2,2,2,1,192,768]{5,4,2,1,0,3:T(8,128)(2,1)S(1)}, u32[]{:S(2)}, u32[]{:S(2)}) %collective-permute-start.113) | collective-permute-done | bytes 2359328 | tf_op jit(solution)/shard_map/ppermute | solution.py:395
  1076.1 48.2 %collective-permute-done.107 = bf16[2,2,2,1,192,768]{5,4,2,1,0,3:T(8,128)(2,1)S(1)} collective-permute-done((bf16[2,2,2,1,192,768]{5,4,2,1,0,3:T(8,128)(2,1)S(1)}, bf16[2,2,2,1,192,768]{5,4,2,1,0,3:T(8,128)(2,1)S(1)}, u32[]{:S(2)}, u32[]{:S(2)}) %collective-permute-start.107) | collective-permute-done | bytes 2359328 | tf_op jit(solution)/shard_map/ppermute | solution.py:395
  1137.8 27.2 %shard_map.342 = (bf16[1536,384]{1,0:T(8,128)(2,1)S(1)}, bf16[1536,384]{1,0:T(8,128)(2,1)S(1)}, bf16[1536,384]{1,0:T(8,128)(2,1)S(1)}) custom-call(bf16[1536,1152]{1,0:T(8,128)(2,1)S(1)} %copy-done.4, bf16[1536,1152]{1,0:T(8,128)(2,1)S(1)} %copy-done.4, bf16[1536,1152]{1,0:T(8,128)(2,1)S(1)} %copy-done.4, bf16[1536,384]{1,0:T(8,128)(2,1)S(1)} %copy-done.2, ...), custom_call_target="tpu_custom_call" | custom-call | flops 18119393280 | bytes 11796480 | tf_op jit(solution)/shard_map/pallas_call | solution.py:679
  1198.8 16.1 %convert_element_type.702 = bf16[2,2,2,192,4,2,192]{3,2,1,0,6,5,4:T(2,128)(2,1)} reshape(bf16[1536,1536]{0,1:T(8,128)(2,1)} %pad_maximum_fusion.2) | data formatting | bytes 9437184 | tf_op jit(solution)/shard_map/convert_element_type | solution.py:509
  1224.9 14.4 constant_dynamic-slice_fusion.13
  1239.3 19.2 %copy.290 = bf16[2,2,1,192,4,2,192]{6,3,4,1,5,0,2:T(8,128)(2,1)} copy(bf16[2,2,1,192,4,2,192]{3,2,1,0,6,5,4:T(2,128)(2,1)} %get-tuple-element.59) | data formatting | bytes 4718592
  1258.6 19.3 %copy.291 = bf16[2,2,1,192,4,2,192]{6,3,4,1,5,0,2:T(8,128)(2,1)} copy(bf16[2,2,1,192,4,2,192]{3,2,1,0,6,5,4:T(2,128)(2,1)} %get-tuple-element.60) | data formatting | bytes 4718592
  1335.8 50.3 %collective-permute-done.85 = f32[2,1536]{1,0:T(2,128)S(1)} collective-permute-done((f32[2,1536]{1,0:T(2,128)S(1)}, f32[2,1536]{1,0:T(2,128)S(1)}, u32[]{:S(2)}, u32[]{:S(2)}) %collective-permute-start.85) | collective-permute-done | bytes 12320 | tf_op jit(solution)/shard_map/ppermute | solution.py:395
  1404.7 16.2 %collective-permute-done.96 = bf16[2,4,192,192]{3,0,1,2:T(2,128)(2,1)S(1)} collective-permute-done((bf16[2,4,192,192]{3,0,1,2:T(2,128)(2,1)S(1)}, bf16[2,4,192,192]{3,0,1,2:T(2,128)(2,1)S(1)}, u32[]{:S(2)}, u32[]{:S(2)}) %collective-permute-start.96) | collective-permute-done | bytes 589856 | tf_op jit(solution)/shard_map/ppermute | solution.py:400
  1456.0 19.5 %collective-permute-done.71 = bf16[2,48,1536]{2,1,0:T(8,128)(2,1)S(1)} collective-permute-done((bf16[2,48,1536]{2,1,0:T(8,128)(2,1)S(1)}, bf16[2,48,1536]{2,1,0:T(8,128)(2,1)S(1)}, u32[]{:S(2)}, u32[]{:S(2)}) %collective-permute-start.71) | collective-permute-done | bytes 294944 | tf_op jit(solution)/shard_map/ppermute | solution.py:400
  (763 shorter events, 924.2 us)
Async XLA Ops:
  51.6 107.3 %collective-permute-start.33 = (bf16[2,1,192,768]{3,2,1,0:T(8,128)(2,1)}, bf16[2,1,192,768]{3,2,1,0:T(8,128)(2,1)}, u32[]{:S(2)}, u32[]{:S(2)}) collective-permute-start(bf16[2,1,192,768]{3,2,1,0:T(8,128)(2,1)} %maximum_select_fusion.37), channel_id=1, source_target_pairs={{0,1},{1,2},{2,3},{3,0},{4,5},{5,6},{6,7},{7,4},{8,9},{9,10},{10,1... | collective-permute-start | bytes 1769480 | tf_op jit(solution)/shard_map/ppermute | solution.py:400
  55.3 101.5 %collective-permute-start.40 = (bf16[2,1,192,768]{3,2,1,0:T(8,128)(2,1)}, bf16[2,1,192,768]{3,2,1,0:T(8,128)(2,1)}, u32[]{:S(2)}, u32[]{:S(2)}) collective-permute-start(bf16[2,1,192,768]{3,2,1,0:T(8,128)(2,1)} %maximum_select_fusion.39), channel_id=1, source_target_pairs={{0,1},{1,2},{2,3},{3,0},{4,5},{5,6},{6,7},{7,4},{8,9},{9,10},{10,1... | collective-permute-start | bytes 1769480 | tf_op jit(solution)/shard_map/ppermute | solution.py:400
  178.0 86.4 %collective-permute-start.20 = (bf16[4,2,192,384]{3,0,2,1:T(4,128)(2,1)}, bf16[4,2,192,384]{3,0,2,1:T(4,128)(2,1)}, u32[]{:S(2)}, u32[]{:S(2)}) collective-permute-start(bf16[4,2,192,384]{3,0,2,1:T(4,128)(2,1)} %dynamic_update_slice.117), channel_id=1, source_target_pairs={{0,16},{16,0},{1,17},{17,1},{2,18},{18,2},{3,19},{19,3},{4,20},{20... | collective-permute-start | bytes 3538952 | tf_op jit(solution)/shard_map/ppermute | solution.py:395
  299.4 116.5 %collective-permute-start.37 = (bf16[4,2,1,192,768]{4,3,1,0,2:T(8,128)(2,1)}, bf16[4,2,1,192,768]{4,3,1,0,2:T(8,128)(2,1)S(1)}, u32[]{:S(2)}, u32[]{:S(2)}) collective-permute-start(bf16[4,2,1,192,768]{4,3,1,0,2:T(8,128)(2,1)} %bitcast_dynamic-update-slice_fusion.3), channel_id=1, source_target_pairs={{0,16},{16,0},{1,17},{17,1},{2,18},{18,2},{3,19},{19,3},{4,20},{20... | collective-permute-start | bytes 7077896 | tf_op jit(solution)/shard_map/ppermute | solution.py:395
  322.5 143.5 %collective-permute-start.44 = (bf16[4,2,1,192,768]{4,3,1,0,2:T(8,128)(2,1)}, bf16[4,2,1,192,768]{4,3,1,0,2:T(8,128)(2,1)S(1)}, u32[]{:S(2)}, u32[]{:S(2)}) collective-permute-start(bf16[4,2,1,192,768]{4,3,1,0,2:T(8,128)(2,1)} %bitcast_dynamic-update-slice_fusion), channel_id=1, source_target_pairs={{0,16},{16,0},{1,17},{17,1},{2,18},{18,2},{3,19},{19,3},{4,20},{20... | collective-permute-start | bytes 7077896 | tf_op jit(solution)/shard_map/ppermute | solution.py:395
  324.8 218.2 %collective-permute-start.21 = (bf16[2,4,2,192,384]{4,1,3,0,2:T(4,128)(2,1)}, bf16[2,4,2,192,384]{4,1,3,0,2:T(4,128)(2,1)}, u32[]{:S(2)}, u32[]{:S(2)}) collective-permute-start(bf16[2,4,2,192,384]{4,1,3,0,2:T(4,128)(2,1)} %maximum_select_fusion.16), channel_id=1, source_target_pairs={{0,8},{8,0},{1,9},{9,1},{2,10},{10,2},{3,11},{11,3},{4,12},{12,4},... | collective-permute-start | bytes 7077896 | tf_op jit(solution)/shard_map/ppermute | solution.py:395
  365.6 102.0 %collective-permute-start.13 = (bf16[2,2,4,192,192]{4,3,2,1,0:T(8,128)(2,1)S(1)}, bf16[2,2,4,192,192]{4,3,2,1,0:T(8,128)(2,1)S(1)}, u32[]{:S(2)}, u32[]{:S(2)}) collective-permute-start(bf16[2,2,4,192,192]{4,3,2,1,0:T(8,128)(2,1)S(1)} %get-tuple-element.82), channel_id=1, source_target_pairs={{0,4},{4,0},{1,5},{5,1},{2,6},{6,2},{3,7},{7,3},{8,12},{12,8},{9,1... | collective-permute-start | bytes 3538952 | tf_op jit(solution)/shard_map/ppermute | solution.py:395
  417.5 260.7 %collective-permute-start.38 = (bf16[2,2,1,192,768]{4,3,1,0,2:T(8,128)(2,1)}, bf16[2,2,1,192,768]{4,3,1,0,2:T(8,128)(2,1)}, u32[]{:S(2)}, u32[]{:S(2)}) collective-permute-start(bf16[2,2,1,192,768]{4,3,1,0,2:T(8,128)(2,1)} %get-tuple-element.88), channel_id=1, source_target_pairs={{0,4},{4,0},{1,5},{5,1},{2,6},{6,2},{3,7},{7,3},{8,12},{12,8},{9,1... | collective-permute-start | bytes 3538952 | tf_op jit(solution)/shard_map/ppermute | solution.py:395
  467.6 104.7 %collective-permute-start.45 = (bf16[2,2,1,192,768]{4,3,1,0,2:T(8,128)(2,1)}, bf16[2,2,1,192,768]{4,3,1,0,2:T(8,128)(2,1)}, u32[]{:S(2)}, u32[]{:S(2)}) collective-permute-start(bf16[2,2,1,192,768]{4,3,1,0,2:T(8,128)(2,1)} %get-tuple-element.92), channel_id=1, source_target_pairs={{0,4},{4,0},{1,5},{5,1},{2,6},{6,2},{3,7},{7,3},{8,12},{12,8},{9,1... | collective-permute-start | bytes 3538952 | tf_op jit(solution)/shard_map/ppermute | solution.py:395
  847.3 75.4 %collective-permute-start.112 = (bf16[2,2,2,1,192,768]{5,4,2,1,0,3:T(8,128)(2,1)}, bf16[2,2,2,1,192,768]{5,4,2,1,0,3:T(8,128)(2,1)}, u32[]{:S(2)}, u32[]{:S(2)}) collective-permute-start(bf16[2,2,2,1,192,768]{5,4,2,1,0,3:T(8,128)(2,1)} %bitcast.597), channel_id=1, source_target_pairs={{0,4},{4,0},{1,5},{5,1},{2,6},{6,2},{3,7},{7,3},{8,12},{12,8},{9,1... | collective-permute-start | bytes 7077896 | tf_op jit(solution)/shard_map/ppermute | solution.py:395
  847.3 82.5 %collective-permute-start.106 = (bf16[2,2,2,1,192,768]{5,4,2,1,0,3:T(8,128)(2,1)}, bf16[2,2,2,1,192,768]{5,4,2,1,0,3:T(8,128)(2,1)}, u32[]{:S(2)}, u32[]{:S(2)}) collective-permute-start(bf16[2,2,2,1,192,768]{5,4,2,1,0,3:T(8,128)(2,1)} %bitcast.599), channel_id=1, source_target_pairs={{0,4},{4,0},{1,5},{5,1},{2,6},{6,2},{3,7},{7,3},{8,12},{12,8},{9,1... | collective-permute-start | bytes 7077896 | tf_op jit(solution)/shard_map/ppermute | solution.py:395
  914.0 112.0 %collective-permute-start.64 = (bf16[2,192,1536]{2,1,0:T(8,128)(2,1)}, bf16[2,192,1536]{2,1,0:T(8,128)(2,1)}, u32[]{:S(2)}, u32[]{:S(2)}) collective-permute-start(bf16[2,192,1536]{2,1,0:T(8,128)(2,1)} %get-tuple-element.54), channel_id=1, source_target_pairs={{0,8},{8,0},{1,9},{9,1},{2,10},{10,2},{3,11},{11,3},{4,12},{12,4},... | collective-permute-start | bytes 3538952 | tf_op jit(solution)/shard_map/ppermute | solution.py:395
  915.5 113.4 %collective-permute-start.63 = (bf16[2,192,1536]{2,1,0:T(8,128)(2,1)}, bf16[2,192,1536]{2,1,0:T(8,128)(2,1)}, u32[]{:S(2)}, u32[]{:S(2)}) collective-permute-start(bf16[2,192,1536]{2,1,0:T(8,128)(2,1)} %get-tuple-element.54), channel_id=1, source_target_pairs={{0,4},{4,0},{1,5},{5,1},{2,6},{6,2},{3,7},{7,3},{8,12},{12,8},{9,1... | collective-permute-start | bytes 3538952 | tf_op jit(solution)/shard_map/ppermute | solution.py:395
  1000.9 72.9 %collective-permute-start.113 = (bf16[2,2,2,1,192,768]{5,4,2,1,0,3:T(8,128)(2,1)S(1)}, bf16[2,2,2,1,192,768]{5,4,2,1,0,3:T(8,128)(2,1)S(1)}, u32[]{:S(2)}, u32[]{:S(2)}) collective-permute-start(bf16[2,2,2,1,192,768]{5,4,2,1,0,3:T(8,128)(2,1)S(1)} %dynamic-slice_bitcast_fusion.1), channel_id=1, source_target_pairs={{0,16},{16,0},{1,17},{17,1},{2,18},{18,2},{3,19},{19,3},{4,20},{20... | collective-permute-start | bytes 7077896 | tf_op jit(solution)/shard_map/ppermute | solution.py:395
  1010.6 113.8 %collective-permute-start.107 = (bf16[2,2,2,1,192,768]{5,4,2,1,0,3:T(8,128)(2,1)S(1)}, bf16[2,2,2,1,192,768]{5,4,2,1,0,3:T(8,128)(2,1)S(1)}, u32[]{:S(2)}, u32[]{:S(2)}) collective-permute-start(bf16[2,2,2,1,192,768]{5,4,2,1,0,3:T(8,128)(2,1)S(1)} %dynamic-slice_bitcast_fusion.2), channel_id=1, source_target_pairs={{0,16},{16,0},{1,17},{17,1},{2,18},{18,2},{3,19},{19,3},{4,20},{20... | collective-permute-start | bytes 7077896 | tf_op jit(solution)/shard_map/ppermute | solution.py:395
  1026.0 279.3 %collective-permute-start.100 = (bf16[2,2,4,2,192,384]{5,4,2,0,1,3:T(8,128)(2,1)}, bf16[2,2,4,2,192,384]{5,4,2,0,1,3:T(8,128)(2,1)}, u32[]{:S(2)}, u32[]{:S(2)}) collective-permute-start(bf16[2,2,4,2,192,384]{5,4,2,0,1,3:T(8,128)(2,1)} %fusion.12), channel_id=1, source_target_pairs={{0,4},{4,0},{1,5},{5,1},{2,6},{6,2},{3,7},{7,3},{8,12},{12,8},{9,1... | collective-permute-start | bytes 14155784 | tf_op jit(solution)/shard_map/ppermute | solution.py:395
  1028.9 97.9 %collective-permute-start.65 = (bf16[2,192,1536]{2,1,0:T(8,128)(2,1)}, bf16[2,192,1536]{2,1,0:T(8,128)(2,1)S(1)}, u32[]{:S(2)}, u32[]{:S(2)}) collective-permute-start(bf16[2,192,1536]{2,1,0:T(8,128)(2,1)} %collective-permute-done.64), channel_id=1, source_target_pairs={{0,4},{4,0},{1,5},{5,1},{2,6},{6,2},{3,7},{7,3},{8,12},{12,8},{9,1... | collective-permute-start | bytes 3538952 | tf_op jit(solution)/shard_map/ppermute | solution.py:395
  1055.3 222.6 %collective-permute-start.83 = (bf16[2,2,512,192]{2,3,1,0:T(8,128)(2,1)}, bf16[2,2,512,192]{2,3,1,0:T(8,128)(2,1)}, u32[]{:S(2)}, u32[]{:S(2)}) collective-permute-start(bf16[2,2,512,192]{2,3,1,0:T(8,128)(2,1)} %maximum_select_fusion.35), channel_id=1, source_target_pairs={{0,16},{16,0},{1,17},{17,1},{2,18},{18,2},{3,19},{19,3},{4,20},{20... | collective-permute-start | bytes 2359304 | tf_op jit(solution)/shard_map/ppermute | solution.py:395
  1074.5 115.4 %collective-permute-start.114 = (bf16[2,1,192,768]{3,2,1,0:T(8,128)(2,1)S(1)}, bf16[2,1,192,768]{3,2,1,0:T(8,128)(2,1)}, u32[]{:S(2)}, u32[]{:S(2)}) collective-permute-start(bf16[2,1,192,768]{3,2,1,0:T(8,128)(2,1)S(1)} %dynamic-slice_bitcast_fusion.27), channel_id=1, source_target_pairs={{0,1},{1,2},{2,3},{3,0},{4,5},{5,6},{6,7},{7,4},{8,9},{9,10},{10,1... | collective-permute-start | bytes 1769480 | tf_op jit(solution)/shard_map/ppermute | solution.py:400
  1218.0 77.3 %collective-permute-start.67 = (bf16[2,192,1536]{2,1,0:T(8,128)(2,1)S(1)}, bf16[2,192,1536]{2,1,0:T(8,128)(2,1)}, u32[]{:S(2)}, u32[]{:S(2)}) collective-permute-start(bf16[2,192,1536]{2,1,0:T(8,128)(2,1)S(1)} %get-tuple-element.66), channel_id=1, source_target_pairs={{0,4},{4,0},{1,5},{5,1},{2,6},{6,2},{3,7},{7,3},{8,12},{12,8},{9,1... | collective-permute-start | bytes 3538952 | tf_op jit(solution)/shard_map/ppermute | solution.py:395
  1220.2 71.8 %collective-permute-start.116 = (bf16[2,1,192,768]{3,2,1,0:T(8,128)(2,1)}, bf16[2,1,192,768]{3,2,1,0:T(8,128)(2,1)}, u32[]{:S(2)}, u32[]{:S(2)}) collective-permute-start(bf16[2,1,192,768]{3,2,1,0:T(8,128)(2,1)} %fusion.46), channel_id=1, source_target_pairs={{0,1},{1,2},{2,3},{3,0},{4,5},{5,6},{6,7},{7,4},{8,9},{9,10},{10,1... | collective-permute-start | bytes 1769480 | tf_op jit(solution)/shard_map/ppermute | solution.py:400
  1304.7 122.8 %collective-permute-start.111 = (bf16[1,192,768]{2,1,0:T(8,128)(2,1)S(1)}, bf16[1,192,768]{2,1,0:T(8,128)(2,1)S(1)}, u32[]{:S(2)}, u32[]{:S(2)}) collective-permute-start(bf16[1,192,768]{2,1,0:T(8,128)(2,1)S(1)} %get-tuple-element.126), channel_id=1, source_target_pairs={{0,8},{8,0},{1,9},{9,1},{2,10},{10,2},{3,11},{11,3},{4,12},{12,4},... | collective-permute-start | bytes 884744 | tf_op jit(solution)/shard_map/ppermute | solution.py:395
  1310.4 92.6 %collective-permute-start.101 = (bf16[2,4,2,192,384]{4,3,1,0,2:T(8,128)(2,1)S(1)}, bf16[2,4,2,192,384]{4,3,1,0,2:T(8,128)(2,1)S(1)}, u32[]{:S(2)}, u32[]{:S(2)}) collective-permute-start(bf16[2,4,2,192,384]{4,3,1,0,2:T(8,128)(2,1)S(1)} %dynamic-slice_bitcast_fusion.3), channel_id=1, source_target_pairs={{0,8},{8,0},{1,9},{9,1},{2,10},{10,2},{3,11},{11,3},{4,12},{12,4},... | collective-permute-start | bytes 7077896 | tf_op jit(solution)/shard_map/ppermute | solution.py:395
  1316.8 79.5 %collective-permute-start.95 = (bf16[2,2,2,4,192,192]{5,4,3,2,1,0:T(8,128)(2,1)S(1)}, bf16[2,2,2,4,192,192]{5,4,3,2,1,0:T(8,128)(2,1)S(1)}, u32[]{:S(2)}, u32[]{:S(2)}) collective-permute-start(bf16[2,2,2,4,192,192]{5,4,3,2,1,0:T(8,128)(2,1)S(1)} %dynamic-slice_bitcast_fusion), channel_id=1, source_target_pairs={{0,16},{16,0},{1,17},{17,1},{2,18},{18,2},{3,19},{19,3},{4,20},{20... | collective-permute-start | bytes 7077896 | tf_op jit(solution)/shard_map/ppermute | solution.py:395
  (209 other events, 4476.6 us)

commit v2 on v0

--- a/solution.py
+++ b/solution.py
@@ -3,6 +3,8 @@
 import jax
 import jax.numpy as jnp
 from jax import lax
+from jax.experimental import pallas as pl
+from jax.experimental.pallas import tpu as pltpu
 from jax.sharding import PartitionSpec as P
 
 HD = 64
@@ -389,52 +391,1057 @@
     )
 
 
+BLOCK = 256
+SCALE = 1.0 / math.sqrt(HD)
+PIECES = 4
+
+
+def pair_swap(values, axis_name):
+    return lax.ppermute(values, axis_name, [(0, 1), (1, 0)])
+
+
+def ring_shift(values, distance):
+    size = lax.axis_size("z")
+    return lax.ppermute(values, "z", [(i, (i + distance) % size) for i in range(size)])
+
+
+def ring_flip(values, bit):
+    size = lax.axis_size("z")
+    return lax.ppermute(values, "z", [(i, i ^ bit) for i in range(size)])
+
+
+def take(values, index, axis=0):
+    return lax.dynamic_index_in_dim(values, index, axis, keepdims=False)
+
+
+def place(values, piece, index, axis=0):
+    return lax.dynamic_update_index_in_dim(values, piece, index, axis)
+
+
+def ordered(index, own, other):
+    return jnp.where(index == 0, jnp.stack([own, other]), jnp.stack([other, own]))
+
+
+def wide(values):
+    return values.astype(jnp.float32)
+
+
+def narrow(values):
+    return values.astype(jnp.bfloat16)
+
+
+def exchange_clips(values):
+    return lax.all_to_all(values, ("y", "z"), 0, 0, tiled=True)
+
+
+def group_rows(own):
+    across = pair_swap(own, "x")
+    return [own, pair_swap(own, "c"), across, pair_swap(across, "c")]
+
+
+def group_terms(parts):
+    far = wide(parts[2]) + wide(pair_swap(parts[3], "c"))
+    return [parts[0], pair_swap(parts[1], "c"), pair_swap(narrow(far), "x")]
+
+
+def ring_gather(own):
+    at_z, size = lax.axis_index("z"), lax.axis_size("z")
+    out = place(jnp.zeros((size,) + own.shape, own.dtype), own, at_z)
+    piece = own
+    for distance in range(1, size):
+        piece = ring_shift(piece, 1)
+        out = place(out, piece, lax.rem(at_z + size - distance, size))
+    return out
+
+
+def ring_sum(parts):
+    at_z, size = lax.axis_index("z"), lax.axis_size("z")
+    moving = take(parts, lax.rem(at_z + size - 1, size))
+    for step in range(1, size):
+        got = ring_shift(moving, 1)
+        mine = take(parts, lax.rem(at_z + 2 * size - 1 - step, size))
+        total = wide(got) + wide(mine)
+        moving = narrow(total)
+    return total
+
+
+def everywhere(values):
+    for name in ("c", "x", "y"):
+        values = values + pair_swap(values, name)
+    bit = 1
+    while bit < lax.axis_size("z"):
+        values = values + ring_flip(values, bit)
+        bit *= 2
+    return values
+
+
+def gather_attend(shards):
+    at_x, at_c = lax.axis_index("x"), lax.axis_index("c")
+    rows, units = shards[0].shape
+    split = jnp.stack([shard.reshape(rows, 2, units // 2) for shard in shards], axis=1)
+    split = jnp.transpose(split, (2, 0, 1, 3)).reshape(2, rows, -1)
+    mine = jnp.stack([take(split, at_x), pair_swap(take(split, 1 - at_x), "x")])
+    near = ring_gather(mine)
+    across = pair_swap(near, "y")
+    half = near.shape[0] // 2
+
+    def sibling(values):
+        return pair_swap(lax.dynamic_slice_in_dim(values, (1 - at_c) * half, half, 0), "c")
+
+    return [near, across, sibling(near), sibling(across)]
+
+
+def sum_attend(grad):
+    at_x, at_c = lax.axis_index("x"), lax.axis_index("c")
+    away = pair_swap(take(grad, 1 - at_c), "c")
+    whole = ordered(at_c, take(grad, at_c), away)
+    rows, width = whole.shape[-2:]
+    whole = whole.reshape((-1, 2, rows, width))
+    total = lax.psum_scatter(whole, ("z", "y"), scatter_dimension=0, tiled=True).reshape(2, rows, width)
+    halves = ordered(at_x, take(total, at_x), pair_swap(take(total, 1 - at_x), "x"))
+    halves = wide(halves).reshape(2, rows, 4, width // 4)
+    return [
+        jnp.concatenate([halves[0, :, i], halves[1, :, i]], axis=1) for i in range(4)
+    ]
+
+
+def gather_units(shard):
+    at_x, at_c = lax.axis_index("x"), lax.axis_index("c")
+    rows = shard.shape[0]
+    split = jnp.transpose(shard.reshape(rows, 2, 2, -1), (1, 2, 0, 3))
+    mine = take(split, at_x)
+    other = pair_swap(take(split, 1 - at_x), "x")
+    pair = jnp.stack([mine, other], axis=1)
+    pair = jnp.stack([take(pair, at_c), pair_swap(take(pair, 1 - at_c), "c")], axis=1)
+    own = pair.reshape((1, PIECES) + pair.shape[2:])
+    return lax.all_gather(own, ("y", "z"), axis=0, tiled=True)
+
+
+def sum_units(grad):
+    at_x, at_c = lax.axis_index("x"), lax.axis_index("c")
+    grad = grad.reshape((-1,) + grad.shape[2:])
+    total = lax.psum_scatter(grad, ("y", "z"), scatter_dimension=0, tiled=True)[0]
+    away = pair_swap(total[2:], "x")
+    pair = ordered(at_x, total[:2], away)
+    whole = ordered(at_c, pair[:, 0], pair_swap(pair[:, 1], "c"))
+    whole = jnp.transpose(wide(whole), (2, 1, 0, 3))
+    return whole.reshape(whole.shape[0], -1)
+
+
+def gather_whole(shard):
+    near = ring_gather(shard)
+    pieces = [near, pair_swap(near, "y")]
+    pieces = pieces + [pair_swap(piece, "x") for piece in pieces]
+    return pieces + [pair_swap(piece, "c") for piece in pieces]
+
+
+def sum_whole(grad):
+    at_y, at_x, at_c = lax.axis_index("y"), lax.axis_index("x"), lax.axis_index("c")
+    for at, name in ((at_c, "c"), (at_x, "x"), (at_y, "y")):
+        got = pair_swap(take(grad, 1 - at), name)
+        grad = narrow(wide(take(grad, at)) + wide(got))
+    return ring_sum(grad)
+
+
+def dot_nt(left, right):
+    return lax.dot_general(left, right, (((1,), (1,)), ((), ())), preferred_element_type=jnp.float32)
+
+
+def dot_nn(left, right):
+    return lax.dot_general(left, right, (((1,), (0,)), ((), ())), preferred_element_type=jnp.float32)
+
+
+def dot_tn(left, right):
+    return lax.dot_general(left, right, (((0,), (0,)), ((), ())), preferred_element_type=jnp.float32)
+
+
+def whole_spec(array):
+    return pl.BlockSpec(array.shape, lambda *_: (0,) * len(array.shape))
+
+
+ANYWHERE = pl.BlockSpec(memory_space=pl.ANY)
+SCALARS = pl.BlockSpec(memory_space=pltpu.SMEM)
+
+
+def like(shape, dtype=jnp.bfloat16):
+    return jax.ShapeDtypeStruct(shape, dtype)
+
+
+def diagonal_mask(size):
+    row = lax.broadcasted_iota(jnp.int32, (size, size), 0)
+    column = lax.broadcasted_iota(jnp.int32, (size, size), 1)
+    return column <= row
+
+
+def block_of(at_y, at_x, at_c):
+    return (at_y * 2 + at_x) * 2 + at_c
+
+
+def natural_rows(ids, piece, upper, rows):
+    at_x, at_c = ids[1], ids[2]
+    member = (at_x ^ (piece // 2)) * 2 + (at_c ^ (piece % 2))
+    return pl.ds(pl.multiple_of((upper * PIECES + member) * rows, rows), rows)
+
+
+def attend_copies(ids, pieces, weights, sem):
+    at_y, at_x, at_c = ids[0], ids[1], ids[2]
+    rows = pieces[0].shape[-2]
+    half = pieces[2].shape[0]
+    copies = []
+    for index, piece in enumerate(pieces):
+        sibling, other_y = index // 2, index % 2
+        for at in range(half):
+            for other_x in range(2):
+                block = block_of(at_y ^ other_y, at_x ^ other_x, at_c ^ sibling)
+                source = piece.at[at, other_x] if sibling else piece.at[at_c * half + at, other_x]
+                target = weights.at[at, pl.ds(pl.multiple_of(block * rows, rows), rows)]
+                copies.append(pltpu.make_async_copy(source, target, sem.at[len(copies)]))
+    return copies
+
+
+def attend_forward_kernel(ids, *refs):
+    rows_in, pieces = refs[0:4], refs[4:8]
+    parts, qkv, mixed_out, log_out = refs[8:12], refs[12], refs[13], refs[14]
+    weights, mixed, sem = refs[15:18]
+    copies = attend_copies(ids, pieces, weights, sem)
+    for copy in copies:
+        copy.start()
+    for copy in copies:
+        copy.wait()
+    halves, frames, width = qkv.shape
+    third = width // 3
+    rows = rows_in[0].shape[0] // 2
+    for at in range(halves):
+        for piece in range(PIECES):
+            out = narrow(dot_nn(rows_in[piece][...], weights[at, :, :width]))
+            for upper in range(2):
+                qkv[at, natural_rows(ids, piece, upper, rows), :] = out[upper * rows : (upper + 1) * rows]
+    mask = diagonal_mask(BLOCK)
+    log_out[...] = jnp.zeros_like(log_out)
+    lane = lax.broadcasted_iota(jnp.int32, (BLOCK, log_out.shape[1]), 1)
+
+    def half_heads(at, carry):
+        for head in range(third // HD):
+            q_lanes, k_lanes, v_lanes = (
+                slice(i * third + head * HD, i * third + (head + 1) * HD) for i in range(3)
+            )
+            for start in range(0, frames, BLOCK):
+                block = slice(start, start + BLOCK)
+                q = qkv[at, block, q_lanes] * jnp.bfloat16(SCALE)
+                near = jnp.where(mask, dot_nt(q, qkv[at, block, k_lanes]), MASKED)
+                top = jnp.max(near, axis=-1, keepdims=True)
+                if start:
+                    past = dot_nt(q, qkv[at, 0:start, k_lanes])
+                    top = jnp.maximum(top, jnp.max(past, axis=-1, keepdims=True))
+                near = jnp.exp(near - top)
+                total = jnp.sum(near, axis=-1, keepdims=True)
+                out = dot_nn(narrow(near), qkv[at, block, v_lanes])
+                if start:
+                    past = jnp.exp(past - top)
+                    total = total + jnp.sum(past, axis=-1, keepdims=True)
+                    out = out + dot_nn(narrow(past), qkv[at, 0:start, v_lanes])
+                mixed[at, block, head * HD : (head + 1) * HD] = narrow(out / total)
+                log_total = top + jnp.log(total)
+                log_out[block, :] = jnp.where(
+                    lane == at * (third // HD) + head, log_total, log_out[block, :]
+                )
+        return carry
+
+    lax.fori_loop(0, halves, half_heads, 0)
+    for piece in range(PIECES):
+        for upper in range(2):
+            here = natural_rows(ids, piece, upper, rows)
+            there = slice(upper * rows, (upper + 1) * rows)
+            out = None
+            for at in range(halves):
+                own = mixed[at, here, :]
+                mixed_out[at, piece, there, :] = own
+                term = dot_nt(own, weights[at, :, width:])
+                out = term if out is None else out + term
+            parts[piece][there, :] = narrow(out)
+
+
+def attend_backward_kernel(ids, *refs):
+    rows_in, pieces = refs[0:4], refs[4:8]
+    qkv, mixed_in, log_in = refs[8], refs[9], refs[10]
+    parts, grad_out = refs[11:15], refs[15]
+    weights, grads, totals, back, dk_sum, dv_sum, sem = refs[16:23]
+    copies = attend_copies(ids, pieces, weights, sem)
+    for copy in copies:
+        copy.start()
+    for copy in copies:
+        copy.wait()
+    halves, frames, width = qkv.shape
+    third = width // 3
+    heads = third // HD
+    rows = rows_in[0].shape[0] // 2
+    for at in range(halves):
+        for piece in range(PIECES):
+            out = narrow(dot_nn(rows_in[piece][...], weights[at, :, width:]))
+            product = wide(out) * wide(mixed_in[at, piece])
+            lane = lax.broadcasted_iota(jnp.int32, (2 * rows, totals.shape[2]), 1)
+            sums = jnp.zeros((2 * rows, totals.shape[2]), jnp.float32)
+            for head in range(heads):
+                one = jnp.sum(product[:, head * HD : (head + 1) * HD], axis=-1, keepdims=True)
+                sums = jnp.where(lane == head, one, sums)
+            for upper in range(2):
+                here = natural_rows(ids, piece, upper, rows)
+                there = slice(upper * rows, (upper + 1) * rows)
+                grads[at, here, :] = out[there]
+                totals[at, here, :] = sums[there]
+    mask = diagonal_mask(BLOCK)
+
+    def half_heads(at, carry):
+        dk_sum[...] = jnp.zeros_like(dk_sum)
+        dv_sum[...] = jnp.zeros_like(dv_sum)
+        for head in range(heads):
+            q_lanes, k_lanes, v_lanes = (
+                slice(i * third + head * HD, i * third + (head + 1) * HD) for i in range(3)
+            )
+            o_lanes = slice(head * HD, (head + 1) * HD)
+            log_lane = lax.broadcasted_iota(jnp.int32, (BLOCK, log_in.shape[1]), 1)
+            for start in range(0, frames, BLOCK):
+                block = slice(start, start + BLOCK)
+                q = qkv[at, block, q_lanes] * jnp.bfloat16(SCALE)
+                grad = grads[at, block, o_lanes]
+                q_turned = narrow(wide(q).T)
+                grad_turned = narrow(wide(grad).T)
+                log_total = jnp.sum(
+                    jnp.where(log_lane == at * heads + head, log_in[block, :], 0.0),
+                    axis=-1,
+                    keepdims=True,
+                )
+                row_total = totals[at, block, head : head + 1]
+                dq = None
+                for columns in (block, slice(0, start)):
+                    if columns.stop == 0:
+                        continue
+                    keys = qkv[at, columns, k_lanes]
+                    weight = jnp.exp(dot_nt(q, keys) - log_total)
+                    if columns is block:
+                        weight = jnp.where(mask, weight, 0.0)
+                    grad_weight = dot_nt(grad, qkv[at, columns, v_lanes])
+                    scores = narrow(weight * (grad_weight - row_total))
+                    part = dot_nn(scores, keys)
+                    dq = part if dq is None else dq + part
+                    dk_sum[o_lanes, columns] += dot_nn(q_turned, scores)
+                    dv_sum[o_lanes, columns] += dot_nn(grad_turned, narrow(weight))
+                back[at, block, q_lanes] = narrow(dq * SCALE)
+        for start in range(0, frames, BLOCK):
+            block = slice(start, start + BLOCK)
+            back[at, block, third : 2 * third] = narrow(dk_sum[:, block].T)
+            back[at, block, 2 * third :] = narrow(dv_sum[:, block].T)
+        return carry
+
+    lax.fori_loop(0, halves, half_heads, 0)
+    for piece in range(PIECES):
+        for at in range(halves):
+            for upper in range(2):
+                there = slice(upper * rows, (upper + 1) * rows)
+                grad_out[at, piece, there, :] = back[at, natural_rows(ids, piece, upper, rows), :]
+        out = None
+        for at in range(halves):
+            term = dot_nt(grad_out[at, piece], weights[at, :, :width])
+            out = term if out is None else out + term
+        parts[piece][...] = narrow(out)
+
+
+def attend_forward(ids, rows_in, pieces):
+    rows, model = rows_in[0].shape
+    halves, units = pieces[2].shape[0], pieces[0].shape[-1]
+    width = units // 4
+    frames = PIECES * rows
+    outs = [like((rows, model))] * PIECES + [
+        like((halves, frames, 3 * width)),
+        like((halves, PIECES, rows, width)),
+        like((frames, 128), jnp.float32),
+    ]
+    out = pl.pallas_call(
+        attend_forward_kernel,
+        in_specs=[SCALARS] + [pl.BlockSpec(memory_space=pltpu.VMEM)] * PIECES + [ANYWHERE] * 4,
+        out_specs=[pl.BlockSpec(memory_space=pltpu.VMEM)] * len(outs),
+        out_shape=outs,
+        scratch_shapes=[
+            pltpu.VMEM((halves, model, units), jnp.bfloat16),
+            pltpu.VMEM((halves, frames, width), jnp.bfloat16),
+            pltpu.SemaphoreType.DMA((8 * halves,)),
+        ],
+        compiler_params=pltpu.CompilerParams(vmem_limit_bytes=56 * 2**20),
+        cost_estimate=pl.CostEstimate(
+            flops=30 * 10**9, bytes_accessed=24 * 2**20, transcendentals=0
+        ),
+        name="attend_forward",
+    )(ids, *rows_in, *pieces)
+    return out[:4], out[4], out[5], out[6]
+
+
+def attend_backward(ids, rows_in, pieces, qkv, mixed, log_total):
+    rows, model = rows_in[0].shape
+    halves, units = pieces[2].shape[0], pieces[0].shape[-1]
+    frames, width = qkv.shape[1], qkv.shape[2] // 3
+    outs = [like((rows, model))] * PIECES + [like((halves, PIECES, rows, 3 * width))]
+    vmem = pl.BlockSpec(memory_space=pltpu.VMEM)
+    out = pl.pallas_call(
+        attend_backward_kernel,
+        in_specs=[SCALARS] + [vmem] * PIECES + [ANYWHERE] * 4 + [vmem] * 3,
+        out_specs=[vmem] * len(outs),
+        out_shape=outs,
+        scratch_shapes=[
+            pltpu.VMEM((halves, model, units), jnp.bfloat16),
+            pltpu.VMEM((halves, frames, width), jnp.bfloat16),
+            pltpu.VMEM((halves, frames, 128), jnp.float32),
+            pltpu.VMEM((halves, frames, 3 * width), jnp.bfloat16),
+            pltpu.VMEM((width, frames), jnp.float32),
+            pltpu.VMEM((width, frames), jnp.float32),
+            pltpu.SemaphoreType.DMA((8 * halves,)),
+        ],
+        compiler_params=pltpu.CompilerParams(vmem_limit_bytes=58 * 2**20),
+        cost_estimate=pl.CostEstimate(
+            flops=50 * 10**9, bytes_accessed=24 * 2**20, transcendentals=0
+        ),
+        name="attend_backward",
+    )(ids, *rows_in, *pieces, qkv, mixed, log_total)
+    return out[:4], out[4]
+
+
+def attend_grads_kernel(ids, *refs):
+    normed, grads = refs[0:4], refs[4:8]
+    grad_qkv, mixed, out = refs[8:11]
+    halves, _, _, width = grad_qkv.shape
+    rows = out.shape[-2]
+    for at in range(halves):
+        left = right = None
+        for piece in range(PIECES):
+            one = dot_tn(normed[piece][...], grad_qkv[at, piece])
+            two = dot_tn(grads[piece][...], mixed[at, piece])
+            left = one if left is None else left + one
+            right = two if right is None else right + two
+        for core in range(2):
+            block = slice(core * rows, (core + 1) * rows)
+            out[core, at, 0, 0, :, :width] = narrow(left[block])
+            out[core, at, 0, 0, :, width:] = narrow(right[block])
+
+
+def attend_grads(ids, normed, grads, grad_qkv, mixed):
+    rows, model = normed[0].shape
+    halves, units = mixed.shape[0], 4 * mixed.shape[-1]
+    strip = model // 4
+    column = pl.BlockSpec((rows, strip), lambda i, ids: (0, i))
+    return pl.pallas_call(
+        attend_grads_kernel,
+        grid_spec=pltpu.PrefetchScalarGridSpec(
+            num_scalar_prefetch=1,
+            grid=(4,),
+            in_specs=[column] * 8 + [whole_spec(grad_qkv), whole_spec(mixed)],
+            out_specs=pl.BlockSpec(
+                (2, halves, 1, 1, strip // 2, units), lambda i, ids: (0, 0, i // 2, i % 2, 0, 0)
+            ),
+        ),
+        out_shape=like((2, halves, 2, 2, strip // 2, units)),
+        compiler_params=pltpu.CompilerParams(vmem_limit_bytes=40 * 2**20),
+        cost_estimate=pl.CostEstimate(
+            flops=8 * 10**9, bytes_accessed=20 * 2**20, transcendentals=0
+        ),
+        name="attend_grads",
+    )(ids, *normed, *grads, grad_qkv, mixed)
+
+
+def gelu_both(values):
+    factor = math.sqrt(2.0 / math.pi)
+    square = values * values
+    bent = jnp.tanh(factor * values * (1.0 + 0.044715 * square))
+    slope = 0.5 * (1.0 + bent) + 0.5 * values * (1.0 - bent * bent) * factor * (
+        1.0 + 3.0 * 0.044715 * square
+    )
+    return 0.5 * values * (1.0 + bent), slope
+
+
+def feed_kernel(ids, *refs):
+    rows_in, grads_in, up_in, down_in = refs[0:4], refs[4:8], refs[8], refs[9]
+    result_out, back_out, active_out, hidden_out = refs[10:14], refs[14:18], refs[18], refs[19]
+    rows_all, grads_all, up, down, result, back, active, hidden, w_sem, in_sem, out_sem = refs[20:]
+    at_x, at_c = ids[1], ids[2]
+    rows, model = rows_in[0].shape
+    shard_rows, width = up_in.shape[-2:]
+    groups = up_in.shape[0] // 2
+    copies = []
+    for which, (source, target) in enumerate(((up_in, up), (down_in, down))):
+        for other_y in range(2):
+            for at_z in range(groups):
+                for piece in range(PIECES):
+                    block = block_of(other_y, at_x ^ (piece // 2), at_c ^ (piece % 2))
+                    place_rows = pl.ds(pl.multiple_of(block * shard_rows, shard_rows), shard_rows)
+                    lanes = slice((at_z % 2) * width, (at_z % 2 + 1) * width)
+                    copies.append(
+                        pltpu.make_async_copy(
+                            source.at[other_y * groups + at_z, piece],
+                            target.at[at_z // 2, place_rows, lanes],
+                            w_sem.at[len(copies)],
+                        )
+                    )
+    for piece in range(PIECES):
+        copies.append(
+            pltpu.make_async_copy(rows_in[piece], rows_all.at[piece], in_sem.at[2 * piece])
+        )
+        copies.append(
+            pltpu.make_async_copy(grads_in[piece], grads_all.at[piece], in_sem.at[2 * piece + 1])
+        )
+    for copy in copies:
+        copy.start()
+    for copy in copies:
+        copy.wait()
+    blocks = groups // 2
+
+    def outputs(piece, slot):
+        return [
+            pltpu.make_async_copy(source.at[slot], target, out_sem.at[slot, i])
+            for i, (source, target) in enumerate(
+                (
+                    (result, result_out[piece]),
+                    (back, back_out[piece]),
+                    (active, active_out.at[piece]),
+                    (hidden, hidden_out.at[piece]),
+                )
+            )
+        ]
+
+    for piece in range(PIECES):
+        slot = piece % 2
+        if piece >= 2:
+            for copy in outputs(piece - 2, slot):
+                copy.wait()
+
+        def one_block(at, carry):
+            own = rows_all[piece]
+            value, slope = gelu_both(dot_nn(own, up[at]))
+            value = narrow(value)
+            change = narrow(dot_nn(grads_all[piece], down[at]) * slope)
+            lanes = pl.ds(pl.multiple_of(at * 2 * width, 2 * width), 2 * width)
+            active[slot, :, lanes] = value
+            hidden[slot, :, lanes] = change
+            return carry
+
+        lax.fori_loop(0, blocks, one_block, 0)
+
+        def one_result(at, carry):
+            here = pl.ds(pl.multiple_of(at * 2 * width, 2 * width), 2 * width)
+            first = second = None
+            for part in range(blocks):
+                lanes = slice(part * 2 * width, (part + 1) * 2 * width)
+                one = dot_nt(active[slot, :, lanes], down[part, here, :])
+                two = dot_nt(hidden[slot, :, lanes], up[part, here, :])
+                first = one if first is None else first + one
+                second = two if second is None else second + two
+            result[slot, :, here] = narrow(first)
+            back[slot, :, here] = narrow(second)
+            return carry
+
+        lax.fori_loop(0, model // (2 * width), one_result, 0)
+        for copy in outputs(piece, slot):
+            copy.start()
+    for piece in (PIECES - 2, PIECES - 1):
+        for copy in outputs(piece, piece % 2):
+            copy.wait()
+
+
+def feed(ids, rows_in, grads_in, up, down):
+    rows, model = rows_in[0].shape
+    units = up.shape[0] // 2 * up.shape[-1]
+    outs = [like((rows, model))] * 8 + [like((PIECES, rows, units))] * 2
+    blocks = up.shape[0] // 4
+    weight = pltpu.VMEM((blocks, model, 2 * up.shape[-1]), jnp.bfloat16)
+    out = pl.pallas_call(
+        feed_kernel,
+        in_specs=[SCALARS] + [ANYWHERE] * 10,
+        out_specs=[ANYWHERE] * 10,
+        out_shape=outs,
+        scratch_shapes=[
+            pltpu.VMEM((PIECES, rows, model), jnp.bfloat16),
+            pltpu.VMEM((PIECES, rows, model), jnp.bfloat16),
+            weight,
+            weight,
+            pltpu.VMEM((2, rows, model), jnp.bfloat16),
+            pltpu.VMEM((2, rows, model), jnp.bfloat16),
+            pltpu.VMEM((2, rows, units), jnp.bfloat16),
+            pltpu.VMEM((2, rows, units), jnp.bfloat16),
+            pltpu.SemaphoreType.DMA((2 * up.shape[0] * PIECES,)),
+            pltpu.SemaphoreType.DMA((2 * PIECES,)),
+            pltpu.SemaphoreType.DMA((2, 4)),
+        ],
+        compiler_params=pltpu.CompilerParams(vmem_limit_bytes=56 * 2**20),
+        cost_estimate=pl.CostEstimate(
+            flops=8 * PIECES * rows * model * units, bytes_accessed=36 * 2**20, transcendentals=0
+        ),
+        name="feed_forward",
+    )(ids, *rows_in, *grads_in, up, down)
+    return out[0:4], out[4:8], out[8], out[9]
+
+
+def feed_grads_kernel(ids, *refs):
+    left, right, out = refs[0:4], refs[4], refs[5]
+    rows, width = out.shape[-2:]
+    at_c = ids[2]
+    for at_z in range(out.shape[1]):
+        total = None
+        for piece in range(PIECES):
+            one = dot_tn(left[piece][...], right[piece, :, at_z * width : (at_z + 1) * width])
+            total = one if total is None else total + one
+        for core in range(2):
+            out[0, at_z, 0, at_c ^ core] = narrow(total[core * rows : (core + 1) * rows])
+
+
+def feed_grads(ids, left, right):
+    rows, model = left[0].shape
+    units = right.shape[-1]
+    groups = lax.axis_size("z")
+    strip = model // 4
+    shape = (2, groups, 2, 2, strip // 2, units // groups)
+    out = pl.pallas_call(
+        feed_grads_kernel,
+        grid_spec=pltpu.PrefetchScalarGridSpec(
+            num_scalar_prefetch=1,
+            grid=(4,),
+            in_specs=[pl.BlockSpec((rows, strip), lambda i, ids: (0, i))] * 4 + [whole_spec(right)],
+            out_specs=pl.BlockSpec(
+                (1, groups, 1, 2, strip // 2, units // groups),
+                lambda i, ids: (i // 2, 0, (i % 2) ^ ids[1], 0, 0, 0),
+            ),
+        ),
+        out_shape=like(shape),
+        compiler_params=pltpu.CompilerParams(vmem_limit_bytes=40 * 2**20),
+        cost_estimate=pl.CostEstimate(
+            flops=2 * PIECES * rows * model * units, bytes_accessed=16 * 2**20, transcendentals=0
+        ),
+        name="feed_grads",
+    )(ids, *left, right)
+    return out.reshape(2, groups, PIECES, strip // 2, units // groups)
+
+
+def block_pair(values):
+    low = lax.broadcasted_iota(jnp.int32, values.shape, 1) < HD
+    zero = jnp.zeros_like(values)
+    return jnp.concatenate([jnp.where(low, values, zero), jnp.where(low, zero, values)], axis=0)
+
+
+def by_half(low, values, reduce, empty):
+    first = reduce(jnp.where(low, values, empty), axis=-1, keepdims=True)
+    second = reduce(jnp.where(low, empty, values), axis=-1, keepdims=True)
+    return jnp.where(low, first, second)
+
+
+def cross_weights(count, queries, keys):
+    slots = keys.shape[0] // 2
+    scores = dot_nt(queries, keys)
+    lane = lax.broadcasted_iota(jnp.int32, scores.shape, 1)
+    low = lane < slots
+    scores = jnp.where(jnp.where(low, lane, lane - slots) < count, scores, MASKED)
+    raised = jnp.exp(scores - by_half(low, scores, jnp.max, MASKED))
+    return raised / by_half(low, raised, jnp.sum, 0.0), low
+
+
+def cross_copies(ids, pieces, weights, sem):
+    rows = pieces[0].shape[-2]
+    copies = []
+    for index, piece in enumerate(pieces):
+        block = block_of(ids[0] ^ (index % 2), ids[1] ^ (index // 2 % 2), ids[2] ^ (index // 4))
+        target = weights.at[:, pl.ds(pl.multiple_of(block * rows, rows), rows)]
+        copies.append(pltpu.make_async_copy(piece, target, sem.at[index]))
+    return copies
+
+
+def lanes_of(at, size):
+    return pl.ds(pl.multiple_of(at * size, size), size)
+
+
+def cross_forward_kernel(ids, count, *refs):
+    tokens, terms, norms, keys_values, pieces = refs[0], refs[1:4], refs[4], refs[5], refs[6:14]
+    self_out, normed_out, queries, mixed, cross_out, rows_out = refs[14:20]
+    weights, sem = refs[20:22]
+    copies = cross_copies(ids, pieces, weights, sem)
+    for copy in copies:
+        copy.start()
+    after_self = wide(tokens[...])
+    for term in terms:
+        after_self = after_self + wide(term[...])
+    self_out[...] = after_self
+    normed = narrow(layer_norm(after_self, norms[0:1, :], norms[1:2, :])[0])
+    normed_out[...] = normed
+    for copy in copies:
+        copy.wait()
+    width = weights.shape[2] // 2
+    model = tokens.shape[1]
+    for at in range(weights.shape[0]):
+        out = dot_nn(normed_out[...], weights[at, :, :width])
+        queries[:, at * width : (at + 1) * width] = narrow(out)
+
+    def one_pair(at, carry):
+        lanes = lanes_of(at, 2 * HD)
+        query = queries[:, lanes] * jnp.bfloat16(SCALE)
+        keys = block_pair(keys_values[:, lanes])
+        values = block_pair(keys_values[:, lanes_of(at + model // (2 * HD), 2 * HD)])
+        weight, _ = cross_weights(count[0], query, keys)
+        mixed[:, lanes] = narrow(dot_nn(narrow(weight), values))
+        return carry
+
+    lax.fori_loop(0, model // (2 * HD), one_pair, 0)
+    after_cross = self_out[...]
+    for at in range(weights.shape[0]):
+        after_cross = after_cross + dot_nt(
+            mixed[:, at * width : (at + 1) * width], weights[at, :, width:]
+        )
+    cross_out[...] = after_cross
+    rows_out[...] = narrow(layer_norm(after_cross, norms[2:3, :], norms[3:4, :])[0])
+
+
+def cross_forward(ids, count, tokens, terms, norms, keys_values, pieces):
+    rows, model = tokens.shape
+    outs = [
+        like((rows, model), jnp.float32),
+        like((rows, model)),
+        like((rows, model)),
+        like((rows, model)),
+        like((rows, model), jnp.float32),
+        like((rows, model)),
+    ]
+    vmem = pl.BlockSpec(memory_space=pltpu.VMEM)
+    size, shard_rows, width = pieces[0].shape
+    return pl.pallas_call(
+        cross_forward_kernel,
+        in_specs=[SCALARS] * 2 + [vmem] * 6 + [ANYWHERE] * 8,
+        out_specs=[vmem] * len(outs),
+        out_shape=outs,
+        scratch_shapes=[
+            pltpu.VMEM((size, 8 * shard_rows, width), jnp.bfloat16),
+            pltpu.SemaphoreType.DMA((8,)),
+        ],
+        compiler_params=pltpu.CompilerParams(vmem_limit_bytes=48 * 2**20),
+        cost_estimate=pl.CostEstimate(
+            flops=12 * 10**9, bytes_accessed=24 * 2**20, transcendentals=0
+        ),
+        name="cross_forward",
+    )(ids, count, tokens, *terms, norms, keys_values, *pieces)
+
+
+def norm_gradient(upstream, values, gain_vec, bias_vec):
+    _, scaled, inverse = layer_norm(values, gain_vec, bias_vec)
+    weighted = upstream * gain_vec
+    result = inverse * (
+        weighted
+        - jnp.mean(weighted, axis=-1, keepdims=True)
+        - scaled * jnp.mean(weighted * scaled, axis=-1, keepdims=True)
+    )
+    return (
+        result,
+        jnp.sum(upstream * scaled, axis=0, keepdims=True),
+        jnp.sum(upstream, axis=0, keepdims=True),
+    )
+
+
+def cross_backward_kernel(ids, count, *refs):
+    upstream, terms, norms, keys_values = refs[0], refs[1:4], refs[4], refs[5]
+    self_in, cross_in, queries, pieces = refs[6], refs[7], refs[8], refs[9:17]
+    grad_out, first_out, second_out, dq_out, dkv_out, norm_out = refs[17:23]
+    weights, grads, sem = refs[23:26]
+    copies = cross_copies(ids, pieces, weights, sem)
+    for copy in copies:
+        copy.start()
+    grad_three = wide(terms[0][...]) + wide(terms[1][...]) + wide(terms[2][...])
+    back, gain_g, bias_g = norm_gradient(
+        grad_three, cross_in[...], norms[2:3, :], norms[3:4, :]
+    )
+    norm_out[2:3, :] = gain_g
+    norm_out[3:4, :] = bias_g
+    grad_two = wide(upstream[...]) + back
+    grad_out[...] = grad_two
+    second_out[...] = narrow(grad_two)
+    for copy in copies:
+        copy.wait()
+    width = weights.shape[2] // 2
+    model = upstream.shape[1]
+    slots = keys_values.shape[0]
+    for at in range(weights.shape[0]):
+        out = dot_nn(second_out[...], weights[at, :, width:])
+        grads[:, at * width : (at + 1) * width] = narrow(out)
+    dims_low = lax.broadcasted_iota(jnp.int32, (slots, 2 * HD), 1) < HD
+
+    def one_pair(at, carry):
+        lanes = lanes_of(at, 2 * HD)
+        value_lanes = lanes_of(at + model // (2 * HD), 2 * HD)
+        query = queries[:, lanes] * jnp.bfloat16(SCALE)
+        keys = block_pair(keys_values[:, lanes])
+        weight, low = cross_weights(count[0], query, keys)
+        grad = grads[:, lanes]
+        grad_weight = dot_nt(grad, block_pair(keys_values[:, value_lanes]))
+        scores = weight * (grad_weight - by_half(low, grad_weight * weight, jnp.sum, 0.0))
+        scores = narrow(scores)
+        dq_out[:, lanes] = narrow(dot_nn(scores, keys) * SCALE)
+        dk = dot_tn(scores, query)
+        dkv_out[:, lanes] = narrow(jnp.where(dims_low, dk[:slots], dk[slots:]))
+        dv = dot_tn(narrow(weight), grad)
+        dkv_out[:, value_lanes] = narrow(jnp.where(dims_low, dv[:slots], dv[slots:]))
+        return carry
+
+    lax.fori_loop(0, model // (2 * HD), one_pair, 0)
+    grad_two_rows = None
+    for at in range(weights.shape[0]):
+        term = dot_nt(dq_out[:, at * width : (at + 1) * width], weights[at, :, :width])
+        grad_two_rows = term if grad_two_rows is None else grad_two_rows + term
+    back, gain_g, bias_g = norm_gradient(grad_two_rows, self_in[...], norms[0:1, :], norms[1:2, :])
+    norm_out[0:1, :] = gain_g
+    norm_out[1:2, :] = bias_g
+    grad_one = grad_out[...] + back
+    grad_out[...] = grad_one
+    first_out[...] = narrow(grad_one)
+
+
+def cross_backward(
+    ids, count, upstream, terms, norms, keys_values, after_self, after_cross, queries, pieces
+):
+    rows, model = upstream.shape
+    slots = keys_values.shape[0]
+    outs = [
+        like((rows, model), jnp.float32),
+        like((rows, model)),
+        like((rows, model)),
+        like((rows, model)),
+        like((slots, 2 * model)),
+        like((4, model), jnp.float32),
+    ]
+    vmem = pl.BlockSpec(memory_space=pltpu.VMEM)
+    size, shard_rows, width = pieces[0].shape
+    return pl.pallas_call(
+        cross_backward_kernel,
+        in_specs=[SCALARS] * 2 + [vmem] * 9 + [ANYWHERE] * 8,
+        out_specs=[vmem] * len(outs),
+        out_shape=outs,
+        scratch_shapes=[
+            pltpu.VMEM((size, 8 * shard_rows, width), jnp.bfloat16),
+            pltpu.VMEM((rows, model), jnp.bfloat16),
+            pltpu.SemaphoreType.DMA((8,)),
+        ],
+        compiler_params=pltpu.CompilerParams(vmem_limit_bytes=56 * 2**20),
+        cost_estimate=pl.CostEstimate(
+            flops=16 * 10**9, bytes_accessed=28 * 2**20, transcendentals=0
+        ),
+        name="cross_backward",
+    )(
+        ids,
+        count,
+        upstream,
+        *terms,
+        norms,
+        keys_values,
+        after_self,
+        after_cross,
+        queries,
+        *pieces,
+    )
+
+
+def cross_grads_kernel(normed, grad_queries, grads, mixed, out):
+    rows, width = out.shape[-2], out.shape[-1] // 2
+    for at in range(out.shape[3]):
+        lanes = slice(at * width, (at + 1) * width)
+        left = dot_tn(normed[...], grad_queries[:, lanes])
+        right = dot_tn(grads[...], mixed[:, lanes])
+        for core in range(2):
+            block = slice(core * rows, (core + 1) * rows)
+            out[core, 0, 0, at, :, :width] = narrow(left[block])
+            out[core, 0, 0, at, :, width:] = narrow(right[block])
+
+
+def cross_grads(normed, grad_queries, grads, mixed):
+    rows, model = normed.shape
+    size = lax.axis_size("z")
+    strip = model // 4
+    column = pl.BlockSpec((rows, strip), lambda i: (0, i))
+    return pl.pallas_call(
+        cross_grads_kernel,
+        grid=(4,),
+        in_specs=[column, whole_spec(grad_queries), column, whole_spec(mixed)],
+        out_specs=pl.BlockSpec(
+            (2, 1, 1, size, strip // 2, 2 * (model // size)),
+            lambda i: (0, i % 2, i // 2, 0, 0, 0),
+        ),
+        out_shape=like((2, 2, 2, size, strip // 2, 2 * (model // size))),
+        compiler_params=pltpu.CompilerParams(vmem_limit_bytes=40 * 2**20),
+        cost_estimate=pl.CostEstimate(
+            flops=4 * rows * model * model, bytes_accessed=14 * 2**20, transcendentals=0
+        ),
+        name="cross_grads",
+    )(normed, grad_queries, grads, mixed)
+
+
+def clip_body(
+    tokens,
+    memory,
+    text_len,
+    cotangent,
+    gain_one,
+    bias_one,
+    gain_two,
+    bias_two,
+    gain_three,
+    bias_three,
+    w_query,
+    w_key,
+    w_value,
+    w_out,
+    c_query,
+    c_key,
+    c_value,
+    c_out,
+    w_up,
+    w_down,
+):
+    at_y, at_x, at_c, at_z = (lax.axis_index(name) for name in ("y", "x", "c", "z"))
+    ids = jnp.stack([at_y, at_x, at_c, at_z]).astype(jnp.int32)
+    model = tokens.shape[-1]
+    shard_rows, shard_width = w_query.shape
+    slots = memory.shape[2]
+    size = lax.axis_size("z")
+    frame_block = tokens.shape[2]
+
+    attend_pieces = gather_attend([w_query, w_key, w_value, w_out.T])
+    clip_tokens = exchange_clips(tokens.reshape(-1, frame_block, model)).reshape(-1, model)
+    frames = wide(clip_tokens)
+    normed_one, scaled_one, inverse_one = layer_norm(frames[None], gain_one, bias_one)
+    rows_one = group_rows(narrow(normed_one)[0])
+    upstream = exchange_clips(cotangent.reshape(-1, frame_block, model)).reshape(-1, model)
+    cross_pieces = gather_whole(jnp.concatenate([c_query, c_out.T], axis=1))
+    up_full = gather_units(w_up)
+    down_full = gather_units(w_down.T)
+    grad_rows3 = group_rows(upstream)
+
+    at_f = block_of(at_y, at_x, at_c)
+    text_flat = memory.reshape(-1, model)
+    text_mine = lax.dynamic_slice_in_dim(text_flat, at_f * shard_rows, shard_rows, 1)
+    text_shard = jnp.concatenate([c_key, c_value], axis=1)
+    text_part = narrow(dot_nn(text_mine, text_shard)).reshape(2, -1, slots, 2 * shard_width)
+    got = wide(pair_swap(take(text_part, 1 - at_y), "y"))
+    text_part = narrow(wide(take(text_part, at_y)) + got)
+    text_clip = text_part
+    for distance in range(1, size):
+        piece = ring_shift(take(text_part, lax.rem(at_z + distance, size)), distance)
+        text_clip = place(text_clip, piece, lax.rem(at_z + size - distance, size))
+    for name in ("x", "c"):
+        text_clip = narrow(wide(text_clip) + wide(pair_swap(text_clip, name)))
+    text_clip = text_clip.reshape(size, slots, 2, shard_width)
+    keys_values = jnp.transpose(text_clip, (1, 2, 0, 3)).reshape(slots, -1)
+    count = take(take(text_len, at_y), at_z).reshape(1)
+    norms = jnp.stack([gain_two, bias_two, gain_three, bias_three])
+
+    self_parts, qkv, mixed_one, log_total = attend_forward(ids, rows_one, attend_pieces)
+    after_self, rows_two, cross_q, mixed_two, after_cross, own_three = cross_forward(
+        ids, count, clip_tokens, group_terms(self_parts), norms, keys_values, cross_pieces
+    )
+    rows_three = group_rows(own_three)
+
+    feed_parts, back_parts, active, grad_hidden = feed(
+        ids, rows_three, grad_rows3, up_full, down_full
+    )
+    back_terms = group_terms(back_parts)
+    fin_down = sum_units(feed_grads(ids, grad_rows3, active))
+    fin_up = sum_units(feed_grads(ids, rows_three, grad_hidden))
+    feed_terms = group_terms(feed_parts)
+    result = after_cross + wide(feed_terms[0]) + wide(feed_terms[1]) + wide(feed_terms[2])
+    result = exchange_clips(narrow(result).reshape(-1, frame_block, model)).reshape(tokens.shape)
+
+    grad_one_rows, own_one, own_two, grad_cq, grad_text, norm_grads = cross_backward(
+        ids,
+        count,
+        upstream,
+        back_terms,
+        norms,
+        keys_values,
+        after_self,
+        after_cross,
+        cross_q,
+        cross_pieces,
+    )
+    grad_rows1 = group_rows(own_one)
+    fin_cross = sum_whole(cross_grads(rows_two, grad_cq, own_two, mixed_two))
+    fin_cquery, fin_cout = fin_cross[:, :shard_width], fin_cross[:, shard_width:].T
+
+    grad_text = grad_text.reshape(slots, 2, size, shard_width)
+    grad_text = jnp.transpose(grad_text, (2, 0, 1, 3)).reshape(size, slots, 2 * shard_width)
+    for name in ("x", "c"):
+        grad_text = narrow(wide(grad_text) + wide(pair_swap(grad_text, name)))
+    spread = grad_text
+    for distance in range(1, size):
+        piece = ring_shift(take(grad_text, lax.rem(at_z + distance, size)), distance)
+        spread = place(spread, piece, lax.rem(at_z + size - distance, size))
+    spread = ordered(at_y, spread, pair_swap(spread, "y")).reshape(-1, 2 * shard_width)
+    fin_text = dot_tn(text_mine, spread)
+    fin_ckey, fin_cvalue = fin_text[:, :shard_width], fin_text[:, shard_width:]
+    grad_memory = narrow(dot_nt(spread, text_shard))
+    bit = 1
+    while bit < size:
+        grad_memory = narrow(wide(grad_memory) + wide(ring_flip(grad_memory, bit)))
+        bit *= 2
+    for at, name in ((at_c, "c"), (at_x, "x"), (at_y, "y")):
+        grad_memory = ordered(at, grad_memory, pair_swap(grad_memory, name))
+    grad_memory = jnp.transpose(grad_memory.reshape(8, -1, shard_rows), (1, 0, 2))
+    grad_memory = wide(grad_memory.reshape(memory.shape))
+
+    self_back, grad_qkv = attend_backward(
+        ids, grad_rows1, attend_pieces, qkv, mixed_one, log_total
+    )
+    terms = group_terms(self_back)
+    grad_one = wide(terms[0]) + wide(terms[1]) + wide(terms[2])
+    back_one, gain_g1, bias_g1 = norm_back(grad_one[None], scaled_one, inverse_one, gain_one)
+    input_grad = narrow(grad_one_rows + back_one[0])
+    input_grad = exchange_clips(input_grad.reshape(-1, frame_block, model))
+    input_grad = wide(input_grad).reshape(tokens.shape)
+    fin_query, fin_key, fin_value, fin_out = sum_attend(
+        attend_grads(ids, rows_one, grad_rows1, grad_qkv, mixed_one)
+    )
+
+    early = everywhere(norm_grads)
+    late = everywhere(jnp.stack([gain_g1, bias_g1]))
+    return (
+        result,
+        input_grad,
+        grad_memory,
+        late[0],
+        late[1],
+        early[0],
+        early[1],
+        early[2],
+        early[3],
+        fin_query,
+        fin_key,
+        fin_value,
+        fin_out.T,
+        fin_cquery,
+        fin_ckey,
+        fin_cvalue,
+        fin_cout,
+        fin_up,
+        fin_down.T,
+    )
+
+
+def clip_groups(mesh):
+    outer, inner = mesh.shape["fsdp"], mesh.shape["tp"]
+    return (2, 2, 2, inner) if outer == 8 and inner == 4 else None
+
+
 def solution(mesh):
+    sizes = clip_groups(mesh)
+    if sizes is None:
+        rows, columns, program, used = "fsdp", "tp", body, mesh
+    else:
+        rows, columns, program = ("y", "x", "c"), "z", clip_body
+        used = jax.sharding.Mesh(mesh.devices.reshape(sizes), ("y", "x", "c", "z"))
+    both = ("fsdp", "tp") if sizes is None else ("y", "x", "c", "z")
+    frames = P(None, None, both, None)
+    tall, wide = P(rows, columns), P(columns, rows)
+    weights = (tall, tall, tall, wide, tall, tall, tall, wide, tall, wide)
     return jax.shard_map(
-        body,
-        mesh=mesh,
-        in_specs=(
-            P(None, None, ("fsdp", "tp"), None),
-            P(),
-            P(),
-            P(None, None, ("fsdp", "tp"), None),
-            P(),
-            P(),
-            P(),
-            P(),
-            P(),
-            P(),
-            P("fsdp", "tp"),
-            P("fsdp", "tp"),
-            P("fsdp", "tp"),
-            P("tp", "fsdp"),
-            P("fsdp", "tp"),
-            P("fsdp", "tp"),
-            P("fsdp", "tp"),
-            P("tp", "fsdp"),
-            P("fsdp", "tp"),
-            P("tp", "fsdp"),
-        ),
-        out_specs=(
-            P(None, None, ("fsdp", "tp"), None),
-            P(None, None, ("fsdp", "tp"), None),
-            P(),
-            P(),
-            P(),
-            P(),
-            P(),
-            P(),
-            P(),
-            P("fsdp", "tp"),
-            P("fsdp", "tp"),
-            P("fsdp", "tp"),
-            P("tp", "fsdp"),
-            P("fsdp", "tp"),
-            P("fsdp", "tp"),
-            P("fsdp", "tp"),
-            P("tp", "fsdp"),
-            P("fsdp", "tp"),
-            P("tp", "fsdp"),
-        ),
+        program,
+        mesh=used,
+        in_specs=(frames, P(), P(), frames) + (P(),) * 6 + weights,
+        out_specs=(frames, frames, P()) + (P(),) * 6 + weights,
         check_vma=False,
     )

time: 3180 us -> 967 us (0.30)
  waiting for transfers between devices: 2410 us -> 441 us
  matrix products: 458 us -> 2 us
  Pallas kernels: 0 us -> 236 us
  starting transfers between devices: 5.43 us -> 91.3 us
  other arithmetic: 144 us -> 74.9 us
  blocking collectives: 42.8 us -> 0 us
    reduce_scatter x24 -> x3, waiting for transfers between devices: 1360 us -> 0.01 us  [the longest x2 0.01 us: sum_units(): lax.psum_scatter(grad, ('y', 'z'), scatter_dimension=0, tiled=True)[0]]
    all_gather x26 -> x2, waiting for transfers between devices: 890 us -> 0.04 us  [gather_units(): return lax.all_gather(own, ('y', 'z'), axis=0, tiled=True)]
    dot_general x84 -> x3, matrix products: 458 us -> 2 us  [the longest x1 1.09 us: dot_nt(): lax.dot_general(left, right, (((1,), (1,)), ((), ())), preferred_element_...]
    ppermute x0 -> x84, waiting for transfers between devices: none -> 408 us  [the longest x63 256 us: pair_swap(): return lax.ppermute(values, axis_name, [(0, 1), (1, 0)])]
    pallas_call x0 -> x9, Pallas kernels: none -> 236 us  [the longest x1 50.4 us: attend_backward(): pl.pallas_call(attend_backward_kernel, in_specs=[SCALARS] + [vmem] * PIEC...]
    psum x1 -> x0, waiting for transfers between devices: 90.6 us -> none  [body(): lax.psum((jnp.stack(text_grads), norm_totals[0], norm_totals[1], norm_tot...]
    unnamed x55 -> x5, waiting for transfers between devices: 71.8 us -> 0.08 us
    ppermute x0 -> x84, starting transfers between devices: none -> 71.4 us  [the longest x63 45 us: pair_swap(): return lax.ppermute(values, axis_name, [(0, 1), (1, 0)])]
  transfers between devices with their start and end apart: 53 -> 93, of which waited for: 50 -> 35; matrix products, arithmetic and copies ran while one was open for 14% -> 15% of each run, Pallas kernels for 0% -> 19%
where the time goes in v2:
time: 967 us; the launch traced here: 957 us
  waiting for transfers between devices  441 us (46%)
  Pallas kernels  236 us (24%)
  local copies, waits for them, and re-layouts  96.4 us (10%)
  starting transfers between devices  91.3 us (9%)
  other arithmetic  74.9 us (8%)
  between operations  15.7 us (2%)
    ppermute x63, waiting for transfers between devices, pair_swap(): return lax.ppermute(values, axis_name, [(0, 1), (1, 0)])  256 us
    ppermute x15, waiting for transfers between devices, ring_shift(): lax.ppermute(values, 'z', [(i, (i + distance) % size) for i in range(size)])  89 us
    ppermute x6, waiting for transfers between devices, ring_flip(): return lax.ppermute(values, 'z', [(i, i ^ bit) for i in range(size)])  63 us
    pallas_call x1, Pallas kernels, attend_backward(): pl.pallas_call(attend_backward_kernel, in_specs=[SCALARS] + [vmem] * PIEC...  50.4 us
    ppermute x63, starting transfers between devices, pair_swap(): return lax.ppermute(values, axis_name, [(0, 1), (1, 0)])  45 us
    pallas_call x1, Pallas kernels, feed(): pl.pallas_call(feed_kernel, in_specs=[SCALARS] + [ANYWHERE] * 10, out_spe...  43.9 us
    pallas_call x1, Pallas kernels, attend_forward(): pl.pallas_call(attend_forward_kernel, in_specs=[SCALARS] + [pl.BlockSpec(...  39.6 us
    convert_element_type x19, other arithmetic, narrow(): return values.astype(jnp.bfloat16)  33.1 us
  transfers between devices with their start and end apart: 93, of which 35 were waited for; matrix products, arithmetic and copies ran while one was open for 15% of the time, Pallas kernels for 19%

profile of v2, /device:TPU:0, one launch (start us, length us, event | category | flops | bytes accessed | tf_op | source)
XLA Modules:
  0.0 957.1 jit_solution(10208570454697825133)
XLA Ops:
  58.3 41.4 %collective-permute-done.4 = bf16[2,192,768]{2,1,0:T(8,128)(2,1)} collective-permute-done((bf16[2,192,768]{2,1,0:T(8,128)(2,1)}, bf16[2,192,768]{2,1,0:T(8,128)(2,1)}, u32[]{:S(2)}, u32[]{:S(2)}) %collective-permute-start.4) | collective-permute-done | bytes 589856 | tf_op jit(solution)/shard_map/ppermute | solution.py:405
  126.0 17.5 %all-to-all-done = bf16[8,48,1536]{2,1,0:T(8,128)(2,1)S(1)} async-done(((bf16[8,48,1536]{2,1,0:T(8,128)(2,1)}), bf16[8,48,1536]{2,1,0:T(8,128)(2,1)S(1)}, u32[]{:S(2)}, u32[]{:S(2)}) %all-to-all-start) | async-done | bytes 1179680 | tf_op jit(solution)/shard_map/all_to_all | solution.py:434
  157.0 14.5 %collective-permute-done.21 = bf16[192,768]{1,0:T(8,128)(2,1)S(1)} collective-permute-done((bf16[192,768]{1,0:T(8,128)(2,1)}, bf16[192,768]{1,0:T(8,128)(2,1)S(1)}, u32[]{:S(2)}, u32[]{:S(2)}) %collective-permute-start.21) | collective-permute-done | bytes 294944 | tf_op jit(solution)/shard_map/ppermute | solution.py:405
  176.0 43.8 %collective-permute-done.7.refs_5_ = bf16[4,2,192,768]{3,2,1,0:T(8,128)(2,1)} collective-permute-done((bf16[4,2,192,768]{3,2,1,0:T(8,128)(2,1)}, bf16[4,2,192,768]{3,2,1,0:T(8,128)(2,1)}, u32[]{:S(2)}, u32[]{:S(2)}) %collective-permute-start.7) | collective-permute-done | bytes 2359328 | tf_op jit(solution)/shard_map/ppermute | solution.py:400
  227.5 23.6 %collective-permute-done.22.refs_7_.refs_10_ = bf16[4,192,768]{2,1,0:T(8,128)(2,1)} collective-permute-done((bf16[4,192,768]{2,1,0:T(8,128)(2,1)}, bf16[4,192,768]{2,1,0:T(8,128)(2,1)}, u32[]{:S(2)}, u32[]{:S(2)}) %collective-permute-start.22) | collective-permute-done | bytes 1179680 | tf_op jit(solution)/shard_map/ppermute | solution.py:400
  255.5 39.6 %attend_forward.1 = (bf16[384,1536]{1,0:T(8,128)(2,1)}, bf16[384,1536]{1,0:T(8,128)(2,1)}, bf16[384,1536]{1,0:T(8,128)(2,1)}, bf16[384,1536]{1,0:T(8,128)(2,1)},...) custom-call(s32[4]{0:T(128)} %pad_add_fusion.ids, ...), custom_call_target="tpu_custom_call" | custom-call | flops 30000001024 | bytes 25165824 | tf_op jit(solution)/shard_map/attend_forward/pallas_call | solution.py:759
  324.9 14.9 %all-to-all-done.1 = bf16[8,48,1536]{2,1,0:T(8,128)(2,1)} async-done(((bf16[8,48,1536]{2,1,0:T(8,128)(2,1)}), bf16[8,48,1536]{2,1,0:T(8,128)(2,1)}, u32[]{:S(2)}, u32[]{:S(2)}) %all-to-all-start.1) | async-done | bytes 1179680 | tf_op jit(solution)/shard_map/all_to_all | solution.py:434
  348.8 20.6 %cross_forward.1 = (f32[384,1536]{1,0:T(8,128)}, bf16[384,1536]{1,0:T(8,128)(2,1)S(1)}, bf16[384,1536]{1,0:T(8,128)(2,1)S(1)}, bf16[384,1536]{1,0:T(8,128)(2,1)S...) custom-call(s32[4]{0:T(128)S(1)} %copy-done.12, s32[1]{0:T(128)} %bitcast.4.count, bf16[384,1536]{1,0:T(8,128)(2,1)} %bitcast.234, ...), custom_call_target="tpu_custom_call" | custom-call | flops 12000000000 | bytes 25165824 | tf_op jit(solution)/shard_map/cross_forward/pallas_call | solution.py:1108
  375.0 23.9 %collective-permute-done.30.refs_2_ = bf16[384,1536]{1,0:T(8,128)(2,1)} collective-permute-done((bf16[384,1536]{1,0:T(8,128)(2,1)}, bf16[384,1536]{1,0:T(8,128)(2,1)}, u32[]{:S(2)}, u32[]{:S(2)}) %collective-permute-start.30) | collective-permute-done | bytes 1179680 | tf_op jit(solution)/shard_map/ppermute | solution.py:400
  402.0 43.9 %feed_forward.1 = (bf16[384,1536]{1,0:T(8,128)(2,1)}, bf16[384,1536]{1,0:T(8,128)(2,1)}, bf16[384,1536]{1,0:T(8,128)(2,1)}, bf16[384,1536]{1,0:T(8,128)(2,1)}, b...) custom-call(s32[4]{0:T(128)} %pad_add_fusion.ids, ...), custom_call_target="tpu_custom_call" | custom-call | flops 28991029248 | bytes 37748736 | tf_op jit(solution)/shard_map/feed_forward/pallas_call | solution.py:953
  448.3 14.8 %feed_grads.3 = bf16[2,4,2,2,192,384]{5,4,3,2,1,0:T(8,128)(2,1)S(1)} custom-call(s32[4]{0:T(128)S(1)} %copy-done.13, bf16[384,1536]{1,0:T(8,128)(2,1)} %bitcast.33.refs_4_.refs_0_, bf16[384,1536]{1,0:T(8,128)(2,1)} %collective-permute-done.32.refs_5_.refs_1_, bf16[384,1536]{1,0:T(8,128)(2,1)S(1)} %copy-done.18, ...), custom_call_target="tpu_custom_call" | custom-call | flops 7247757312 | bytes 16777216 | tf_op jit(solution)/shard_map/feed_grads/pallas_call | solution.py:999
  471.5 26.6 %collective-permute-done.44.refs_3_ = bf16[384,1536]{1,0:T(8,128)(2,1)S(1)} collective-permute-done((bf16[384,1536]{1,0:T(8,128)(2,1)S(1)}, bf16[384,1536]{1,0:T(8,128)(2,1)S(1)}, u32[]{:S(2)}, u32[]{:S(2)}) %collective-permute-start.44) | collective-permute-done | bytes 1179680 | tf_op jit(solution)/shard_map/ppermute | solution.py:400
  499.1 26.3 %cross_backward.1 = (f32[384,1536]{1,0:T(8,128)}, bf16[384,1536]{1,0:T(8,128)(2,1)}, bf16[384,1536]{1,0:T(8,128)(2,1)}, bf16[384,1536]{1,0:T(8,128)(2,1)}, bf16[64,3072]{1,0:T(8,128)(2,1)}, /*index=5*/f32[4,1536]{1,0:T(4,128)}) custom-call(s32[4]{0:T(128)} %pad_add_fusion.ids, s32[1]{0:T(128)} %bitcast.4.count, bf16[384,1536]{1,0:T(8,128)(2,1)} %bitcast.33.refs_4_.refs_0_, ...), custom_call_target="tpu_custom_call" | custom-call | flops 16000000000 | bytes 29360128 | tf_op jit(solution)/shard_map/cross_backward/pallas_call | solution.py:1212
  529.4 25.3 %collective-permute-done.46.refs_2_.refs_6_ = bf16[384,1536]{1,0:T(8,128)(2,1)} collective-permute-done((bf16[384,1536]{1,0:T(8,128)(2,1)}, bf16[384,1536]{1,0:T(8,128)(2,1)}, u32[]{:S(2)}, u32[]{:S(2)}) %collective-permute-start.46) | collective-permute-done | bytes 1179680 | tf_op jit(solution)/shard_map/ppermute | solution.py:400
  557.1 14.8 %feed_grads.2 = bf16[2,4,2,2,192,384]{5,4,3,2,1,0:T(8,128)(2,1)S(1)} custom-call(s32[4]{0:T(128)S(1)} %copy-done.14, bf16[384,1536]{1,0:T(8,128)(2,1)} %get-tuple-element.58.refs_0_, bf16[384,1536]{1,0:T(8,128)(2,1)} %collective-permute-done.29.refs_1_, bf16[384,1536]{1,0:T(8,128)(2,1)} %collective-permute-done.30.refs_2_, ...), custom_call_target="tpu_custom_call" | custom-call | flops 7247757312 | bytes 16777216 | tf_op jit(solution)/shard_map/feed_grads/pallas_call | solution.py:999
  577.2 50.4 %attend_backward.1 = (bf16[384,1536]{1,0:T(8,128)(2,1)}, bf16[384,1536]{1,0:T(8,128)(2,1)}, bf16[384,1536]{1,0:T(8,128)(2,1)}, bf16[384,1536]{1,0:T(8,128)(2,1)}, bf16[2,4,384,576]{3,2,1,0:T(8,128)(2,1)}) custom-call(s32[4]{0:T(128)} %pad_add_fusion.ids, bf16[384,1536]{1,0:T(8,128)(2,1)} %get-tuple-element.70.refs_0_.refs_4_, ...), custom_call_target="tpu_custom_call" | custom-call | flops 49999998976 | bytes 25165824 | tf_op jit(solution)/shard_map/attend_backward/pallas_call | solution.py:784
  629.0 18.1 %attend_grads.1 = bf16[2,2,2,2,192,768]{5,4,3,2,1,0:T(8,128)(2,1)} custom-call(s32[4]{0:T(128)S(1)} %copy-done.15, bf16[384,1536]{1,0:T(8,128)(2,1)S(1)} %copy-done.9, bf16[384,1536]{1,0:T(8,128)(2,1)} %collective-permute-done.refs_1_, bf16[384,1536]{1,0:T(8,128)(2,1)} %collective-permute-done.1.refs_2_, bf16[384,1536]{1,0:T(8,128)(2,1)} %collective-permute-done.2.refs_3_, ...), custom_call_target="tpu_custom_call" | custom-call | flops 8000000000 | bytes 20971520 | tf_op jit(solution)/shard_map/attend_grads/pallas_call | solution.py:830
  652.4 7.6 cross_grads.1
  697.3 10.9 %collective-permute-done.41 = bf16[384,1536]{1,0:T(8,128)(2,1)} collective-permute-done((bf16[384,1536]{1,0:T(8,128)(2,1)}, bf16[384,1536]{1,0:T(8,128)(2,1)}, u32[]{:S(2)}, u32[]{:S(2)}) %collective-permute-start.41) | collective-permute-done | bytes 1179680 | tf_op jit(solution)/shard_map/ppermute | solution.py:400
  722.0 50.0 %collective-permute-done.71 = f32[4,1536]{1,0:T(4,128)} collective-permute-done((f32[4,1536]{1,0:T(4,128)}, f32[4,1536]{1,0:T(4,128)}, u32[]{:S(2)}, u32[]{:S(2)}) %collective-permute-start.71) | collective-permute-done | bytes 24608 | tf_op jit(solution)/shard_map/ppermute | solution.py:410
  775.0 9.6 %collective-permute-done.58 = bf16[512,192]{0,1:T(8,128)(2,1)S(1)} collective-permute-done((bf16[512,192]{0,1:T(8,128)(2,1)S(1)}, bf16[512,192]{0,1:T(8,128)(2,1)S(1)}, u32[]{:S(2)}, u32[]{:S(2)}) %collective-permute-start.58) | collective-permute-done | bytes 196640 | tf_op jit(solution)/shard_map/ppermute | solution.py:410
  803.9 13.0 %collective-permute-done.50 = bf16[384,1536]{1,0:T(8,128)(2,1)} collective-permute-done((bf16[384,1536]{1,0:T(8,128)(2,1)}, bf16[384,1536]{1,0:T(8,128)(2,1)}, u32[]{:S(2)}, u32[]{:S(2)}) %collective-permute-start.50) | collective-permute-done | bytes 1179680 | tf_op jit(solution)/shard_map/ppermute | solution.py:400
  833.1 42.1 %collective-permute-done.63 = f32[2,1536]{1,0:T(2,128)S(1)} collective-permute-done((f32[2,1536]{1,0:T(2,128)S(1)}, f32[2,1536]{1,0:T(2,128)S(1)}, u32[]{:S(2)}, u32[]{:S(2)}) %collective-permute-start.63) | collective-permute-done | bytes 12320 | tf_op jit(solution)/shard_map/ppermute | solution.py:400
  920.3 7.6 collective-permute-done.78
  (467 shorter events, 340.7 us)
Async XLA Ops:
  7.2 391.7 %all-gather.3.cloned.1.call-start = ((), (), s32[]{:S(2)}) async-start(), calls=%async_computation.7 | async-start | bytes 5308416 | tf_op jit(solution)/shard_map/all_gather | solution.py:517
  42.9 100.6 %all-to-all-start = ((bf16[8,48,1536]{2,1,0:T(8,128)(2,1)}), bf16[8,48,1536]{2,1,0:T(8,128)(2,1)S(1)}, u32[]{:S(2)}, u32[]{:S(2)}) async-start(bf16[8,48,1536]{2,1,0:T(8,128)(2,1)} %bitcast.256), calls=%async_computation | async-start | bytes 2359296 | tf_op jit(solution)/shard_map/all_to_all | solution.py:434
  48.9 350.0 %all-gather.5.cloned.1.call-start = ((), (), s32[]{:S(2)}) async-start(), calls=%async_computation.8 | async-start | bytes 5308416 | tf_op jit(solution)/shard_map/all_gather | solution.py:517
  54.8 54.8 %collective-permute-start.19 = (bf16[192,768]{1,0:T(8,128)(2,1)}, bf16[192,768]{1,0:T(8,128)(2,1)}, u32[]{:S(2)}, u32[]{:S(2)}) collective-permute-start(bf16[192,768]{1,0:T(8,128)(2,1)} %pad_maximum_fusion.3), channel_id=1, source_target_pairs={{0,1},{1,2},{2,3},{3,0},{4,5},{5,6},{6,7},{7,4},{8,9},{9,10},{10,1... | collective-permute-start | bytes 884744 | tf_op jit(solution)/shard_map/ppermute | solution.py:405
  109.6 113.2 %collective-permute-start.38 = (bf16[2,192,384]{2,1,0:T(8,128)(2,1)}, bf16[2,192,384]{2,1,0:T(8,128)(2,1)}, u32[]{:S(2)}, u32[]{:S(2)}) collective-permute-start(bf16[2,192,384]{2,1,0:T(8,128)(2,1)} %bitcast.217), channel_id=1, source_target_pairs={{0,4},{4,0},{1,5},{5,1},{2,6},{6,2},{3,7},{7,3},{8,12},{12,8},{9,1... | collective-permute-start | bytes 884744 | tf_op jit(solution)/shard_map/ppermute | solution.py:400
  145.8 74.0 %collective-permute-start.7 = (bf16[4,2,192,768]{3,2,1,0:T(8,128)(2,1)}, bf16[4,2,192,768]{3,2,1,0:T(8,128)(2,1)}, u32[]{:S(2)}, u32[]{:S(2)}) collective-permute-start(bf16[4,2,192,768]{3,2,1,0:T(8,128)(2,1)} %bitcast_dynamic-update-slice_fusion.refs_4_), channel_id=1, source_target_pairs={{0,16},{16,0},{1,17},{17,1},{2,18},{18,2},{3,19},{19,3},{4,20},{20... | collective-permute-start | bytes 7077896 | tf_op jit(solution)/shard_map/ppermute | solution.py:400
  148.7 74.1 %collective-permute-start.1 = (bf16[384,1536]{1,0:T(8,128)(2,1)S(1)}, bf16[384,1536]{1,0:T(8,128)(2,1)}, u32[]{:S(2)}, u32[]{:S(2)}) collective-permute-start(bf16[384,1536]{1,0:T(8,128)(2,1)S(1)} %add_convert_fusion.6.refs_0_), channel_id=1, source_target_pairs={{0,8},{8,0},{1,9},{9,1},{2,10},{10,2},{3,11},{11,3},{4,12},{12,4},... | collective-permute-start | bytes 3538952 | tf_op jit(solution)/shard_map/ppermute | solution.py:400
  154.7 67.6 %collective-permute-start.14 = (bf16[64,768]{1,0:T(8,128)(2,1)S(1)}, bf16[64,768]{1,0:T(8,128)(2,1)S(1)}, u32[]{:S(2)}, u32[]{:S(2)}) collective-permute-start(bf16[64,768]{1,0:T(8,128)(2,1)S(1)} %dynamic-slice_bitcast_fusion.17), channel_id=1, source_target_pairs={{0,1},{1,2},{2,3},{3,0},{4,5},{5,6},{6,7},{7,4},{8,9},{9,10},{10,1... | collective-permute-start | bytes 294920 | tf_op jit(solution)/shard_map/ppermute | solution.py:405
  172.2 78.9 %collective-permute-start.22 = (bf16[4,192,768]{2,1,0:T(8,128)(2,1)}, bf16[4,192,768]{2,1,0:T(8,128)(2,1)}, u32[]{:S(2)}, u32[]{:S(2)}) collective-permute-start(bf16[4,192,768]{2,1,0:T(8,128)(2,1)} %bitcast_dynamic-update-slice_fusion.4.refs_6_.refs_9_), channel_id=1, source_target_pairs={{0,16},{16,0},{1,17},{17,1},{2,18},{18,2},{3,19},{19,3},{4,20},{20... | collective-permute-start | bytes 3538952 | tf_op jit(solution)/shard_map/ppermute | solution.py:400
  253.5 62.5 %collective-permute-start.23 = (bf16[4,192,768]{2,1,0:T(8,128)(2,1)}, bf16[4,192,768]{2,1,0:T(8,128)(2,1)}, u32[]{:S(2)}, u32[]{:S(2)}) collective-permute-start(bf16[4,192,768]{2,1,0:T(8,128)(2,1)} %bitcast_dynamic-update-slice_fusion.4.refs_6_.refs_9_), channel_id=1, source_target_pairs={{0,8},{8,0},{1,9},{9,1},{2,10},{10,2},{3,11},{11,3},{4,12},{12,4},... | collective-permute-start | bytes 3538952 | tf_op jit(solution)/shard_map/ppermute | solution.py:400
  255.0 61.5 %collective-permute-start.24 = (bf16[4,192,768]{2,1,0:T(8,128)(2,1)}, bf16[4,192,768]{2,1,0:T(8,128)(2,1)}, u32[]{:S(2)}, u32[]{:S(2)}) collective-permute-start(bf16[4,192,768]{2,1,0:T(8,128)(2,1)} %collective-permute-done.22.refs_7_.refs_10_), channel_id=1, source_target_pairs={{0,8},{8,0},{1,9},{9,1},{2,10},{10,2},{3,11},{11,3},{4,12},{12,4},... | collective-permute-start | bytes 3538952 | tf_op jit(solution)/shard_map/ppermute | solution.py:400
  309.4 592.0 %reduce-scatter.8.cloned.1.call-start = ((), (), s32[]{:S(2)}) async-start(), calls=%async_computation.11 | async-start | bytes 5308416 | tf_op jit(solution)/shard_map/reduce_scatter | solution.py:523
  465.3 438.9 %reduce-scatter.6.cloned.1.call-start = ((), (), s32[]{:S(2)}) async-start(), calls=%async_computation.10 | async-start | bytes 5308416 | tf_op jit(solution)/shard_map/reduce_scatter | solution.py:523
  574.0 361.4 %reduce-scatter.4.cloned.1.call-start = ((), (), s32[]{:S(2)}) async-start(), calls=%async_computation.9 | async-start | bytes 5308416 | tf_op jit(solution)/shard_map/reduce_scatter | solution.py:500
  574.8 103.2 %collective-permute-start.40 = (bf16[384,1536]{1,0:T(8,128)(2,1)}, bf16[384,1536]{1,0:T(8,128)(2,1)}, u32[]{:S(2)}, u32[]{:S(2)}) collective-permute-start(bf16[384,1536]{1,0:T(8,128)(2,1)} %get-tuple-element.62), channel_id=1, source_target_pairs={{0,4},{4,0},{1,5},{5,1},{2,6},{6,2},{3,7},{7,3},{8,12},{12,8},{9,1... | collective-permute-start | bytes 3538952 | tf_op jit(solution)/shard_map/ppermute | solution.py:400
  574.9 122.4 %collective-permute-start.39 = (bf16[384,1536]{1,0:T(8,128)(2,1)}, bf16[384,1536]{1,0:T(8,128)(2,1)}, u32[]{:S(2)}, u32[]{:S(2)}) collective-permute-start(bf16[384,1536]{1,0:T(8,128)(2,1)} %get-tuple-element.60), channel_id=1, source_target_pairs={{0,4},{4,0},{1,5},{5,1},{2,6},{6,2},{3,7},{7,3},{8,12},{12,8},{9,1... | collective-permute-start | bytes 3538952 | tf_op jit(solution)/shard_map/ppermute | solution.py:400
  576.1 83.8 %collective-permute-start.67 = (f32[4,1536]{1,0:T(4,128)}, f32[4,1536]{1,0:T(4,128)S(1)}, u32[]{:S(2)}, u32[]{:S(2)}) collective-permute-start(f32[4,1536]{1,0:T(4,128)} %get-tuple-element.79), channel_id=1, source_target_pairs={{0,4},{4,0},{1,5},{5,1},{2,6},{6,2},{3,7},{7,3},{8,12},{12,8},{9,1... | collective-permute-start | bytes 73736 | tf_op jit(solution)/shard_map/ppermute | solution.py:400
  576.6 84.8 %collective-permute-start.53 = (bf16[64,768]{1,0:T(8,128)(2,1)S(1)}, bf16[64,768]{1,0:T(8,128)(2,1)S(1)}, u32[]{:S(2)}, u32[]{:S(2)}) collective-permute-start(bf16[64,768]{1,0:T(8,128)(2,1)S(1)} %dynamic-slice_bitcast_fusion.14), channel_id=1, source_target_pairs={{0,1},{1,2},{2,3},{3,0},{4,5},{5,6},{6,7},{7,4},{8,9},{9,10},{10,1... | collective-permute-start | bytes 294920 | tf_op jit(solution)/shard_map/ppermute | solution.py:405
  665.9 127.3 %collective-permute-start.74 = (bf16[2,2,4,192,768]{4,3,2,1,0:T(8,128)(2,1)}, bf16[2,2,4,192,768]{4,3,2,1,0:T(8,128)(2,1)}, u32[]{:S(2)}, u32[]{:S(2)}) collective-permute-start(bf16[2,2,4,192,768]{4,3,2,1,0:T(8,128)(2,1)} %dynamic-slice_bitcast_fusion), channel_id=1, source_target_pairs={{0,4},{4,0},{1,5},{5,1},{2,6},{6,2},{3,7},{7,3},{8,12},{12,8},{9,1... | collective-permute-start | bytes 14155784 | tf_op jit(solution)/shard_map/ppermute | solution.py:400
  689.5 83.9 %collective-permute-start.57 = (bf16[512,192]{0,1:T(8,128)(2,1)}, bf16[512,192]{0,1:T(8,128)(2,1)}, u32[]{:S(2)}, u32[]{:S(2)}) collective-permute-start(bf16[512,192]{0,1:T(8,128)(2,1)} %convolution_convert_fusion.1), channel_id=1, source_target_pairs={{0,1},{1,0},{2,3},{3,2},{4,5},{5,4},{6,7},{7,6},{8,9},{9,8},{10,11... | collective-permute-start | bytes 589832 | tf_op jit(solution)/shard_map/ppermute | solution.py:410
  697.2 88.0 %collective-permute-start.49 = (bf16[384,1536]{1,0:T(8,128)(2,1)}, bf16[384,1536]{1,0:T(8,128)(2,1)}, u32[]{:S(2)}, u32[]{:S(2)}) collective-permute-start(bf16[384,1536]{1,0:T(8,128)(2,1)} %get-tuple-element.77), channel_id=1, source_target_pairs={{0,4},{4,0},{1,5},{5,1},{2,6},{6,2},{3,7},{7,3},{8,12},{12,8},{9,1... | collective-permute-start | bytes 3538952 | tf_op jit(solution)/shard_map/ppermute | solution.py:400
  712.2 80.9 %all-to-all-start.2 = ((bf16[8,48,1536]{2,1,0:T(8,128)(2,1)}), bf16[8,48,1536]{2,1,0:T(8,128)(2,1)S(1)}, u32[]{:S(2)}, u32[]{:S(2)}) async-start(bf16[8,48,1536]{2,1,0:T(8,128)(2,1)} %bitcast.49), calls=%async_computation.2 | async-start | bytes 2359296 | tf_op jit(solution)/shard_map/all_to_all | solution.py:434
  802.4 74.7 %collective-permute-start.75 = (bf16[2,4,192,768]{3,2,1,0:T(8,128)(2,1)}, bf16[2,4,192,768]{3,2,1,0:T(8,128)(2,1)}, u32[]{:S(2)}, u32[]{:S(2)}) collective-permute-start(bf16[2,4,192,768]{3,2,1,0:T(8,128)(2,1)} %dynamic-slice_bitcast_fusion.1), channel_id=1, source_target_pairs={{0,8},{8,0},{1,9},{9,1},{2,10},{10,2},{3,11},{11,3},{4,12},{12,4},... | collective-permute-start | bytes 7077896 | tf_op jit(solution)/shard_map/ppermute | solution.py:400
  824.5 75.2 %all-to-all-start.3 = ((bf16[8,48,1536]{2,1,0:T(8,128)(2,1)}), bf16[8,48,1536]{2,1,0:T(8,128)(2,1)S(1)}, u32[]{:S(2)}, u32[]{:S(2)}) async-start(bf16[8,48,1536]{2,1,0:T(8,128)(2,1)} %bitcast.242), calls=%async_computation.3 | async-start | bytes 2359296 | tf_op jit(solution)/shard_map/all_to_all | solution.py:434
  (135 other events, 2581.4 us)
Sparse Core Ops, SparseCore 0:
  34.0 174.6 all-gather.2
  227.6 86.8 all-gather.4
  465.4 93.3 reduce-scatter.7
  574.2 96.9 reduce-scatter.5
  697.3 121.4 reduce-scatter.3

commit v3 on v2

--- a/solution.py
+++ b/solution.py
@@ -1,3 +1,4 @@
+import functools
 import math
 
 import jax
@@ -444,27 +445,6 @@
     return [parts[0], pair_swap(parts[1], "c"), pair_swap(narrow(far), "x")]
 
 
-def ring_gather(own):
-    at_z, size = lax.axis_index("z"), lax.axis_size("z")
-    out = place(jnp.zeros((size,) + own.shape, own.dtype), own, at_z)
-    piece = own
-    for distance in range(1, size):
-        piece = ring_shift(piece, 1)
-        out = place(out, piece, lax.rem(at_z + size - distance, size))
-    return out
-
-
-def ring_sum(parts):
-    at_z, size = lax.axis_index("z"), lax.axis_size("z")
-    moving = take(parts, lax.rem(at_z + size - 1, size))
-    for step in range(1, size):
-        got = ring_shift(moving, 1)
-        mine = take(parts, lax.rem(at_z + 2 * size - 1 - step, size))
-        total = wide(got) + wide(mine)
-        moving = narrow(total)
-    return total
-
-
 def everywhere(values):
     for name in ("c", "x", "y"):
         values = values + pair_swap(values, name)
@@ -475,37 +455,24 @@
     return values
 
 
-def gather_attend(shards):
-    at_x, at_c = lax.axis_index("x"), lax.axis_index("c")
+def after(values, *others):
+    return lax.optimization_barrier((values, others))[0]
+
+
+def split_heads(shards):
     rows, units = shards[0].shape
     split = jnp.stack([shard.reshape(rows, 2, units // 2) for shard in shards], axis=1)
-    split = jnp.transpose(split, (2, 0, 1, 3)).reshape(2, rows, -1)
-    mine = jnp.stack([take(split, at_x), pair_swap(take(split, 1 - at_x), "x")])
-    near = ring_gather(mine)
-    across = pair_swap(near, "y")
-    half = near.shape[0] // 2
-
-    def sibling(values):
-        return pair_swap(lax.dynamic_slice_in_dim(values, (1 - at_c) * half, half, 0), "c")
-
-    return [near, across, sibling(near), sibling(across)]
-
-
-def sum_attend(grad):
-    at_x, at_c = lax.axis_index("x"), lax.axis_index("c")
-    away = pair_swap(take(grad, 1 - at_c), "c")
-    whole = ordered(at_c, take(grad, at_c), away)
-    rows, width = whole.shape[-2:]
-    whole = whole.reshape((-1, 2, rows, width))
-    total = lax.psum_scatter(whole, ("z", "y"), scatter_dimension=0, tiled=True).reshape(2, rows, width)
-    halves = ordered(at_x, take(total, at_x), pair_swap(take(total, 1 - at_x), "x"))
-    halves = wide(halves).reshape(2, rows, 4, width // 4)
-    return [
-        jnp.concatenate([halves[0, :, i], halves[1, :, i]], axis=1) for i in range(4)
-    ]
-
-
-def gather_units(shard):
+    return jnp.transpose(split, (2, 0, 1, 3)).reshape(2, rows, -1)
+
+
+def join_heads(own, away):
+    halves = wide(ordered(lax.axis_index("x"), own, away))
+    rows, width = own.shape
+    halves = halves.reshape(2, rows, 4, width // 4)
+    return [jnp.concatenate([halves[0, :, i], halves[1, :, i]], axis=1) for i in range(4)]
+
+
+def gather_units(shard, gate):
     at_x, at_c = lax.axis_index("x"), lax.axis_index("c")
     rows = shard.shape[0]
     split = jnp.transpose(shard.reshape(rows, 2, 2, -1), (1, 2, 0, 3))
@@ -513,7 +480,7 @@
     other = pair_swap(take(split, 1 - at_x), "x")
     pair = jnp.stack([mine, other], axis=1)
     pair = jnp.stack([take(pair, at_c), pair_swap(take(pair, 1 - at_c), "c")], axis=1)
-    own = pair.reshape((1, PIECES) + pair.shape[2:])
+    own = after(pair.reshape((1, PIECES) + pair.shape[2:]), gate)
     return lax.all_gather(own, ("y", "z"), axis=0, tiled=True)
 
 
@@ -528,19 +495,34 @@
     return whole.reshape(whole.shape[0], -1)
 
 
-def gather_whole(shard):
-    near = ring_gather(shard)
-    pieces = [near, pair_swap(near, "y")]
+def gather_whole(shard, gate):
+    pieces = [after(shard, gate)]
+    for _ in range(1, lax.axis_size("z")):
+        pieces.append(ring_shift(pieces[-1], 1))
+    pieces = [jnp.stack(pieces)]
+    pieces = pieces + [pair_swap(pieces[0], "y")]
     pieces = pieces + [pair_swap(piece, "x") for piece in pieces]
     return pieces + [pair_swap(piece, "c") for piece in pieces]
 
 
-def sum_whole(grad):
-    at_y, at_x, at_c = lax.axis_index("y"), lax.axis_index("x"), lax.axis_index("c")
-    for at, name in ((at_c, "c"), (at_x, "x"), (at_y, "y")):
-        got = pair_swap(take(grad, 1 - at), name)
-        grad = narrow(wide(take(grad, at)) + wide(got))
-    return ring_sum(grad)
+def fold_pair(kept, sent, name):
+    return wide(kept) + wide(pair_swap(sent, name))
+
+
+def sum_whole(keep, send):
+    got = pair_swap(send, "c")
+    away = narrow(wide(keep[1]) + wide(got[1]))
+    near = narrow(wide(keep[0]) + wide(got[0]))
+    got = pair_swap(away, "x")
+    away = narrow(wide(near[1]) + wide(got[1]))
+    near = narrow(wide(near[0]) + wide(got[0]))
+    parts = narrow(wide(near) + wide(pair_swap(away, "y")))
+    size = parts.shape[0]
+    moving = parts[1]
+    for step in range(2, size + 1):
+        total = wide(ring_shift(moving, 1)) + wide(parts[step % size])
+        moving = narrow(total)
+    return total
 
 
 def dot_nt(left, right):
@@ -583,31 +565,9 @@
     return pl.ds(pl.multiple_of((upper * PIECES + member) * rows, rows), rows)
 
 
-def attend_copies(ids, pieces, weights, sem):
-    at_y, at_x, at_c = ids[0], ids[1], ids[2]
-    rows = pieces[0].shape[-2]
-    half = pieces[2].shape[0]
-    copies = []
-    for index, piece in enumerate(pieces):
-        sibling, other_y = index // 2, index % 2
-        for at in range(half):
-            for other_x in range(2):
-                block = block_of(at_y ^ other_y, at_x ^ other_x, at_c ^ sibling)
-                source = piece.at[at, other_x] if sibling else piece.at[at_c * half + at, other_x]
-                target = weights.at[at, pl.ds(pl.multiple_of(block * rows, rows), rows)]
-                copies.append(pltpu.make_async_copy(source, target, sem.at[len(copies)]))
-    return copies
-
-
 def attend_forward_kernel(ids, *refs):
-    rows_in, pieces = refs[0:4], refs[4:8]
-    parts, qkv, mixed_out, log_out = refs[8:12], refs[12], refs[13], refs[14]
-    weights, mixed, sem = refs[15:18]
-    copies = attend_copies(ids, pieces, weights, sem)
-    for copy in copies:
-        copy.start()
-    for copy in copies:
-        copy.wait()
+    rows_in, weights = refs[0:4], refs[4]
+    parts, qkv, mixed_out, log_out, mixed = refs[5:9], refs[9], refs[10], refs[11], refs[12]
     halves, frames, width = qkv.shape
     third = width // 3
     rows = rows_in[0].shape[0] // 2
@@ -662,15 +622,10 @@
 
 
 def attend_backward_kernel(ids, *refs):
-    rows_in, pieces = refs[0:4], refs[4:8]
-    qkv, mixed_in, log_in = refs[8], refs[9], refs[10]
-    parts, grad_out = refs[11:15], refs[15]
-    weights, grads, totals, back, dk_sum, dv_sum, sem = refs[16:23]
-    copies = attend_copies(ids, pieces, weights, sem)
-    for copy in copies:
-        copy.start()
-    for copy in copies:
-        copy.wait()
+    rows_in, weights = refs[0:4], refs[4]
+    qkv, mixed_in, log_in = refs[5], refs[6], refs[7]
+    parts, grad_out = refs[8:12], refs[12]
+    grads, totals, back, dk_sum, dv_sum = refs[13:18]
     halves, frames, width = qkv.shape
     third = width // 3
     heads = third // HD
@@ -746,9 +701,9 @@
         parts[piece][...] = narrow(out)
 
 
-def attend_forward(ids, rows_in, pieces):
+def attend_forward(ids, rows_in, weights):
     rows, model = rows_in[0].shape
-    halves, units = pieces[2].shape[0], pieces[0].shape[-1]
+    halves, _, units = weights.shape
     width = units // 4
     frames = PIECES * rows
     outs = [like((rows, model))] * PIECES + [
@@ -758,49 +713,45 @@
     ]
     out = pl.pallas_call(
         attend_forward_kernel,
-        in_specs=[SCALARS] + [pl.BlockSpec(memory_space=pltpu.VMEM)] * PIECES + [ANYWHERE] * 4,
+        in_specs=[SCALARS] + [pl.BlockSpec(memory_space=pltpu.VMEM)] * (PIECES + 1),
         out_specs=[pl.BlockSpec(memory_space=pltpu.VMEM)] * len(outs),
         out_shape=outs,
         scratch_shapes=[
-            pltpu.VMEM((halves, model, units), jnp.bfloat16),
             pltpu.VMEM((halves, frames, width), jnp.bfloat16),
-            pltpu.SemaphoreType.DMA((8 * halves,)),
         ],
         compiler_params=pltpu.CompilerParams(vmem_limit_bytes=56 * 2**20),
         cost_estimate=pl.CostEstimate(
             flops=30 * 10**9, bytes_accessed=24 * 2**20, transcendentals=0
         ),
         name="attend_forward",
-    )(ids, *rows_in, *pieces)
+    )(ids, *rows_in, weights)
     return out[:4], out[4], out[5], out[6]
 
 
-def attend_backward(ids, rows_in, pieces, qkv, mixed, log_total):
+def attend_backward(ids, rows_in, weights, qkv, mixed, log_total):
     rows, model = rows_in[0].shape
-    halves, units = pieces[2].shape[0], pieces[0].shape[-1]
+    halves, _, units = weights.shape
     frames, width = qkv.shape[1], qkv.shape[2] // 3
     outs = [like((rows, model))] * PIECES + [like((halves, PIECES, rows, 3 * width))]
     vmem = pl.BlockSpec(memory_space=pltpu.VMEM)
     out = pl.pallas_call(
         attend_backward_kernel,
-        in_specs=[SCALARS] + [vmem] * PIECES + [ANYWHERE] * 4 + [vmem] * 3,
+        in_specs=[SCALARS] + [vmem] * (PIECES + 4),
         out_specs=[vmem] * len(outs),
         out_shape=outs,
         scratch_shapes=[
-            pltpu.VMEM((halves, model, units), jnp.bfloat16),
             pltpu.VMEM((halves, frames, width), jnp.bfloat16),
             pltpu.VMEM((halves, frames, 128), jnp.float32),
             pltpu.VMEM((halves, frames, 3 * width), jnp.bfloat16),
             pltpu.VMEM((width, frames), jnp.float32),
             pltpu.VMEM((width, frames), jnp.float32),
-            pltpu.SemaphoreType.DMA((8 * halves,)),
         ],
         compiler_params=pltpu.CompilerParams(vmem_limit_bytes=58 * 2**20),
         cost_estimate=pl.CostEstimate(
             flops=50 * 10**9, bytes_accessed=24 * 2**20, transcendentals=0
         ),
         name="attend_backward",
-    )(ids, *rows_in, *pieces, qkv, mixed, log_total)
+    )(ids, *rows_in, weights, qkv, mixed, log_total)
     return out[:4], out[4]
 
 
@@ -809,6 +760,7 @@
     grad_qkv, mixed, out = refs[8:11]
     halves, _, _, width = grad_qkv.shape
     rows = out.shape[-2]
+    at_c = ids[2]
     for at in range(halves):
         left = right = None
         for piece in range(PIECES):
@@ -818,29 +770,29 @@
             right = two if right is None else right + two
         for core in range(2):
             block = slice(core * rows, (core + 1) * rows)
-            out[core, at, 0, 0, :, :width] = narrow(left[block])
-            out[core, at, 0, 0, :, width:] = narrow(right[block])
-
-
-def attend_grads(ids, normed, grads, grad_qkv, mixed):
+            out[at_c ^ core, at, 0, :, :width] = narrow(left[block])
+            out[at_c ^ core, at, 0, :, width:] = narrow(right[block])
+
+
+def attend_grads(ids, normed, grads, grad_qkv, mixed, other_y):
     rows, model = normed[0].shape
     halves, units = mixed.shape[0], 4 * mixed.shape[-1]
     strip = model // 4
-    column = pl.BlockSpec((rows, strip), lambda i, ids: (0, i))
+    column = pl.BlockSpec((rows, strip), lambda i, ids: (0, (ids[0] ^ other_y) * 2 + i))
     return pl.pallas_call(
         attend_grads_kernel,
         grid_spec=pltpu.PrefetchScalarGridSpec(
             num_scalar_prefetch=1,
-            grid=(4,),
+            grid=(2,),
             in_specs=[column] * 8 + [whole_spec(grad_qkv), whole_spec(mixed)],
             out_specs=pl.BlockSpec(
-                (2, halves, 1, 1, strip // 2, units), lambda i, ids: (0, 0, i // 2, i % 2, 0, 0)
+                (2, halves, 1, strip // 2, units), lambda i, ids: (0, 0, i ^ ids[1], 0, 0)
             ),
         ),
-        out_shape=like((2, halves, 2, 2, strip // 2, units)),
+        out_shape=like((2, halves, 2, strip // 2, units)),
         compiler_params=pltpu.CompilerParams(vmem_limit_bytes=40 * 2**20),
         cost_estimate=pl.CostEstimate(
-            flops=8 * 10**9, bytes_accessed=20 * 2**20, transcendentals=0
+            flops=6 * 10**9, bytes_accessed=12 * 2**20, transcendentals=0
         ),
         name="attend_grads",
     )(ids, *normed, *grads, grad_qkv, mixed)
@@ -1044,8 +996,10 @@
     copies = []
     for index, piece in enumerate(pieces):
         block = block_of(ids[0] ^ (index % 2), ids[1] ^ (index // 2 % 2), ids[2] ^ (index // 4))
-        target = weights.at[:, pl.ds(pl.multiple_of(block * rows, rows), rows)]
-        copies.append(pltpu.make_async_copy(piece, target, sem.at[index]))
+        for distance in range(piece.shape[0]):
+            at_z = (ids[3] + piece.shape[0] - distance) % piece.shape[0]
+            target = weights.at[at_z, pl.ds(pl.multiple_of(block * rows, rows), rows)]
+            copies.append(pltpu.make_async_copy(piece.at[distance], target, sem.at[len(copies)]))
     return copies
 
 
@@ -1112,7 +1066,7 @@
         out_shape=outs,
         scratch_shapes=[
             pltpu.VMEM((size, 8 * shard_rows, width), jnp.bfloat16),
-            pltpu.SemaphoreType.DMA((8,)),
+            pltpu.SemaphoreType.DMA((8 * size,)),
         ],
         compiler_params=pltpu.CompilerParams(vmem_limit_bytes=48 * 2**20),
         cost_estimate=pl.CostEstimate(
@@ -1217,7 +1171,7 @@
         scratch_shapes=[
             pltpu.VMEM((size, 8 * shard_rows, width), jnp.bfloat16),
             pltpu.VMEM((rows, model), jnp.bfloat16),
-            pltpu.SemaphoreType.DMA((8,)),
+            pltpu.SemaphoreType.DMA((8 * size,)),
         ],
         compiler_params=pltpu.CompilerParams(vmem_limit_bytes=56 * 2**20),
         cost_estimate=pl.CostEstimate(
@@ -1238,38 +1192,558 @@
     )
 
 
-def cross_grads_kernel(normed, grad_queries, grads, mixed, out):
-    rows, width = out.shape[-2], out.shape[-1] // 2
-    for at in range(out.shape[3]):
+def cross_grads_kernel(ids, normed, grad_queries, grads, mixed, keep, send):
+    size, rows, width = keep.shape[2], keep.shape[3], keep.shape[4] // 2
+    first = ids[2] == 0
+    for at in range(size):
         lanes = slice(at * width, (at + 1) * width)
-        left = dot_tn(normed[...], grad_queries[:, lanes])
-        right = dot_tn(grads[...], mixed[:, lanes])
-        for core in range(2):
-            block = slice(core * rows, (core + 1) * rows)
-            out[core, 0, 0, at, :, :width] = narrow(left[block])
-            out[core, 0, 0, at, :, width:] = narrow(right[block])
-
-
-def cross_grads(normed, grad_queries, grads, mixed):
+        distance = (ids[3] + size - at) % size
+        for part, (left, right) in enumerate(((normed, grad_queries), (grads, mixed))):
+            out = narrow(dot_tn(left[...], right[:, lanes]))
+            there = slice(part * width, (part + 1) * width)
+            keep[0, 0, distance, :, there] = jnp.where(first, out[:rows], out[rows:])
+            send[0, 0, distance, :, there] = jnp.where(first, out[rows:], out[:rows])
+
+
+def cross_grads(ids, normed, grad_queries, grads, mixed):
     rows, model = normed.shape
     size = lax.axis_size("z")
     strip = model // 4
-    column = pl.BlockSpec((rows, strip), lambda i: (0, i))
+    column = pl.BlockSpec((rows, strip), lambda i, ids: (0, i))
+    shape = (2, 2, size, strip // 2, 2 * (model // size))
+    out = pl.BlockSpec(
+        (1, 1) + shape[2:], lambda i, ids: ((i % 2) ^ ids[1], (i // 2) ^ ids[0], 0, 0, 0)
+    )
     return pl.pallas_call(
         cross_grads_kernel,
-        grid=(4,),
-        in_specs=[column, whole_spec(grad_queries), column, whole_spec(mixed)],
-        out_specs=pl.BlockSpec(
-            (2, 1, 1, size, strip // 2, 2 * (model // size)),
-            lambda i: (0, i % 2, i // 2, 0, 0, 0),
+        grid_spec=pltpu.PrefetchScalarGridSpec(
+            num_scalar_prefetch=1,
+            grid=(4,),
+            in_specs=[column, whole_spec(grad_queries), column, whole_spec(mixed)],
+            out_specs=[out, out],
         ),
-        out_shape=like((2, 2, 2, size, strip // 2, 2 * (model // size))),
+        out_shape=[like(shape), like(shape)],
         compiler_params=pltpu.CompilerParams(vmem_limit_bytes=40 * 2**20),
         cost_estimate=pl.CostEstimate(
             flops=4 * rows * model * model, bytes_accessed=14 * 2**20, transcendentals=0
         ),
         name="cross_grads",
-    )(normed, grad_queries, grads, mixed)
+    )(ids, normed, grad_queries, grads, mixed)
+
+
+MESH = pl.DeviceIdType.MESH
+
+
+def where_am_i():
+    return tuple(lax.axis_index(name) for name in ("y", "x", "c", "z"))
+
+
+def send_to(source, target, send_sem, recv_sem, device):
+    return pltpu.make_async_remote_copy(
+        src_ref=source,
+        dst_ref=target,
+        send_sem=send_sem,
+        recv_sem=recv_sem,
+        device_id=device,
+        device_id_type=MESH,
+    )
+
+
+def groups_around(size):
+    at_y, at_x, at_c, at_z = where_am_i()
+    return [
+        ((at_y + step // size) % 2, at_x, at_c, (at_z + step % size) % size)
+        for step in range(2 * size)
+    ]
+
+
+def meet(size):
+    at_y, at_x, at_c, at_z = where_am_i()
+    others = groups_around(size)[1:]
+    others += [(at_y, 1 - at_x, at_c, at_z), (at_y, at_x, 1 - at_c, at_z)]
+    barrier = pltpu.get_barrier_semaphore()
+    for other in others:
+        pl.semaphore_signal(barrier, inc=1, device_id=other, device_id_type=MESH)
+    pl.semaphore_wait(barrier, len(others))
+
+
+def exchange_copies(source, target, size, send_sem, recv_sem):
+    at_y, _, _, at_z = where_am_i()
+    here = at_y * size + at_z
+    copies = []
+    for step, group in enumerate(groups_around(size)):
+        there = group[0] * size + group[3]
+        if step == 0:
+            copies.append(pltpu.make_async_copy(source.at[there], target.at[here], recv_sem.at[0]))
+        else:
+            copies.append(
+                send_to(
+                    source.at[there], target.at[here], send_sem.at[step], recv_sem.at[step], group
+                )
+            )
+    return copies
+
+
+def block_rows(at_y, at_x, at_c, rows):
+    return pl.ds(pl.multiple_of(((at_y * 2 + at_x) * 2 + at_c) * rows, rows), rows)
+
+
+def start_kernel(
+    size,
+    tokens,
+    split,
+    norm,
+    clip_out,
+    rows_own,
+    rows_c,
+    rows_x,
+    rows_xc,
+    weights,
+    held,
+    clip,
+    normed,
+    clip_send,
+    clip_recv,
+    x_sem,
+    ring_send,
+    ring_recv,
+    y_send,
+    y_recv,
+    c_send,
+    c_recv,
+    c_local,
+    row_sem,
+    out_sem,
+):
+    at_y, at_x, at_c, at_z = where_am_i()
+    rows = split.shape[1]
+    half = size // 2
+    x_side = (at_y, 1 - at_x, at_c, at_z)
+    y_side = (1 - at_y, at_x, at_c, at_z)
+    c_side = (at_y, at_x, 1 - at_c, at_z)
+    z_next = (at_y, at_x, at_c, (at_z + 1) % size)
+    meet(size)
+    frames = exchange_copies(tokens, clip, size, clip_send, clip_recv)
+    for copy in frames:
+        copy.start()
+    first = pltpu.make_async_copy(split.at[at_x], held.at[0, 0, 0], out_sem.at[0])
+    first.start()
+    over = send_to(split.at[1 - at_x], held.at[0, 0, 1], x_sem.at[0], x_sem.at[1], x_side)
+    over.start()
+
+    def ring(step, side):
+        return send_to(
+            held.at[step, 0, side],
+            held.at[step + 1, 0, side],
+            ring_send.at[step, side],
+            ring_recv.at[step, side],
+            z_next,
+        )
+
+    def across(step, side):
+        return send_to(
+            held.at[step, 0, side],
+            held.at[step, 1, side],
+            y_send.at[step, side],
+            y_recv.at[step, side],
+            y_side,
+        )
+
+    def settle(step, other_y, side):
+        target = weights.at[
+            step % half, block_rows((at_y + other_y) % 2, (at_x + side) % 2, at_c, rows)
+        ]
+        source = held.at[step, other_y, side]
+        slot = (step % half, other_y, side)
+        local = pltpu.make_async_copy(source, target, c_local.at[slot])
+        remote = send_to(source, target, c_send.at[slot], c_recv.at[slot], c_side)
+        return local, remote
+
+    def settle_start(step, other_y, side):
+        local, remote = settle(step, other_y, side)
+
+        @pl.when(at_c == step // half)
+        def _():
+            local.start()
+
+        @pl.when(at_c != step // half)
+        def _():
+            remote.start()
+
+    for side in range(2):
+        if side == 0:
+            first.wait()
+        else:
+            over.wait_recv()
+        ring(0, side).start()
+        across(0, side).start()
+        settle_start(0, 0, side)
+    for step in range(1, size):
+        if step == size - 1:
+            for copy in frames:
+                if copy is frames[0]:
+                    copy.wait()
+                else:
+                    copy.wait_recv()
+            keep = pltpu.make_async_copy(clip, clip_out, out_sem.at[1])
+            keep.start()
+            gain, bias = norm[0:1, :], norm[1:2, :]
+
+            def one_block(at, carry):
+                here = pl.ds(pl.multiple_of(at * clip.shape[1], clip.shape[1]), clip.shape[1])
+                normed[here, :] = narrow(layer_norm(wide(clip[at]), gain, bias)[0])
+                return carry
+
+            lax.fori_loop(0, clip.shape[0], one_block, 0)
+            own = pltpu.make_async_copy(normed, rows_own, out_sem.at[2])
+            to_x = send_to(normed, rows_x, row_sem.at[0], row_sem.at[1], x_side)
+            to_c = send_to(normed, rows_c, row_sem.at[2], row_sem.at[3], c_side)
+            to_x.start()
+            to_c.start()
+            own.start()
+        for side in range(2):
+            ring(step - 1, side).wait_recv()
+            if step < size - 1:
+                ring(step, side).start()
+            across(step, side).start()
+            settle_start(step, 0, side)
+    for step in range(size):
+        for side in range(2):
+            across(step, side).wait_recv()
+            settle_start(step, 1, side)
+    to_x.wait_recv()
+    relay = send_to(rows_x, rows_xc, row_sem.at[4], row_sem.at[5], c_side)
+    relay.start()
+    for step in range(half):
+        for other_y in range(2):
+            for side in range(2):
+                local, remote = settle(step, other_y, side)
+                local.wait()
+                remote.wait()
+    relay.wait()
+    to_c.wait()
+    to_x.wait_send()
+    own.wait()
+    keep.wait()
+    over.wait_send()
+    for copy in frames[1:]:
+        copy.wait_send()
+    for step in range(size):
+        for side in range(2):
+            across(step, side).wait_send()
+            if step < size - 1:
+                ring(step, side).wait_send()
+
+
+def start_up(tokens, split, norm):
+    size = lax.axis_size("z")
+    groups, frames, model = tokens.shape
+    rows, units = split.shape[1:]
+    half = size // 2
+    vmem = pl.BlockSpec(memory_space=pltpu.VMEM)
+    dma = pltpu.SemaphoreType.DMA
+    out = pl.pallas_call(
+        functools.partial(start_kernel, size),
+        in_specs=[vmem] * 3,
+        out_specs=[ANYWHERE] * 6,
+        out_shape=[like(tokens.shape)]
+        + [like((groups * frames, model))] * PIECES
+        + [like((half, 8 * rows, units))],
+        scratch_shapes=[
+            pltpu.VMEM((size, 2, 2, rows, units), jnp.bfloat16),
+            pltpu.VMEM(tokens.shape, jnp.bfloat16),
+            pltpu.VMEM((groups * frames, model), jnp.bfloat16),
+            dma((groups,)),
+            dma((groups,)),
+            dma((2,)),
+            dma((size - 1, 2)),
+            dma((size - 1, 2)),
+            dma((size, 2)),
+            dma((size, 2)),
+            dma((half, 2, 2)),
+            dma((half, 2, 2)),
+            dma((half, 2, 2)),
+            dma((6,)),
+            dma((3,)),
+        ],
+        compiler_params=pltpu.CompilerParams(
+            collective_id=1, has_side_effects=True, vmem_limit_bytes=32 * 2**20
+        ),
+        cost_estimate=pl.CostEstimate(
+            flops=10**7, bytes_accessed=200 * 2**20, transcendentals=0
+        ),
+        name="start_up",
+    )(tokens, split, norm)
+    return out[0].reshape(-1, model), out[1:5], out[5]
+
+
+def end_kernel(
+    size,
+    far,
+    near,
+    part_own,
+    part_c,
+    part_x,
+    part_xc,
+    upstream,
+    clip,
+    norm,
+    norm_in,
+    grad_out,
+    norm_out,
+    unit_own,
+    unit_x,
+    y_held,
+    folded,
+    both,
+    moved,
+    ring_held,
+    unit_held,
+    core_held,
+    x_moved,
+    x_held,
+    grads,
+    grads_held,
+    sums,
+    sums_held,
+    y_send,
+    y_recv,
+    c_send,
+    c_recv,
+    core_sem,
+    x_sem,
+    ring_send,
+    ring_recv,
+    clip_send,
+    clip_recv,
+    hop_send,
+    hop_recv,
+    unit_sem,
+    out_sem,
+):
+    at_y, at_x, at_c, at_z = where_am_i()
+    x_side = (at_y, 1 - at_x, at_c, at_z)
+    y_side = (1 - at_y, at_x, at_c, at_z)
+    c_side = (at_y, at_x, 1 - at_c, at_z)
+    z_next = (at_y, at_x, at_c, (at_z + 1) % size)
+    half = size // 2
+    meet(size)
+
+    def across(core, at, side):
+        return send_to(
+            far.at[core, at, side],
+            y_held.at[core, at, side],
+            y_send.at[core, at, side],
+            y_recv.at[core, at, side],
+            y_side,
+        )
+
+    places = [(at, side) for at in range(half) for side in range(2)]
+    core_far = send_to(part_xc, core_held.at[1], core_sem.at[0], core_sem.at[1], c_side)
+    core_near = send_to(part_c, core_held.at[0], core_sem.at[2], core_sem.at[3], c_side)
+    core_far.start()
+    for core in (1, 0):
+        for at, side in places:
+            across(core, at, side).start()
+    core_near.start()
+    frames = clip.shape[1]
+
+    def rows_of(at):
+        return pl.ds(pl.multiple_of(at * frames, frames), frames)
+
+    core_far.wait_recv()
+
+    def add_far(at, carry):
+        here = rows_of(at)
+        x_moved[here, :] = narrow(wide(part_x[here, :]) + wide(core_held[1, here, :]))
+        return carry
+
+    lax.fori_loop(0, clip.shape[0], add_far, 0)
+    over = send_to(x_moved, x_held, x_sem.at[0], x_sem.at[1], x_side)
+    over.start()
+
+    def to_core(at, side):
+        return send_to(
+            folded.at[at, side],
+            both.at[1, at, side],
+            c_send.at[at, side],
+            c_recv.at[at, side],
+            c_side,
+        )
+
+    for at, side in places:
+        across(1, at, side).wait_recv()
+        folded[at, side] = narrow(wide(near[1, at, side]) + wide(y_held[1, at, side]))
+        to_core(at, side).start()
+    core_near.wait_recv()
+    over.wait_recv()
+    sums[...] = jnp.zeros_like(sums)
+    sums[2:6, :] = norm_in[...]
+    gain, bias = norm[0:1, :], norm[1:2, :]
+
+    def one_block(at, carry):
+        here = rows_of(at)
+        change = wide(part_own[here, :]) + wide(core_held[0, here, :]) + wide(x_held[here, :])
+        back, gain_g, bias_g = norm_gradient(change, wide(clip[at]), gain, bias)
+        grads[at] = narrow(upstream[here, :] + back)
+        sums[0:1, :] += gain_g
+        sums[1:2, :] += bias_g
+        return carry
+
+    lax.fori_loop(0, clip.shape[0], one_block, 0)
+    exchange = exchange_copies(grads, grads_held, size, clip_send, clip_recv)
+    for copy in exchange:
+        copy.start()
+    hops = [c_side, x_side, y_side]
+    for bit in (1, 2):
+        low = at_z % 2
+        other = (at_z + 1 - 2 * low) if bit == 1 else (at_z + 2) % size
+        hops.append((at_y, at_x, at_c, other))
+
+    def hop(number):
+        source = sums if number == 0 else sums_held.at[1, number - 1]
+        return send_to(
+            source, sums_held.at[0, number], hop_send.at[number], hop_recv.at[number], hops[number]
+        )
+
+    def hop_next(number):
+        hop(number).wait_recv()
+        source = sums[...] if number == 0 else sums_held[1, number - 1]
+        sums_held[1, number] = source + sums_held[0, number]
+        if number + 1 < len(hops):
+            hop(number + 1).start()
+
+    hop(0).start()
+    hop_next(0)
+    for at, side in places:
+        across(0, at, side).wait_recv()
+        both[0, at, side] = narrow(wide(near[0, at, side]) + wide(y_held[0, at, side]))
+    hop_next(1)
+    for at, side in places:
+        to_core(at, side).wait_recv()
+
+    def chunk(step):
+        return ((step // half) + at_c) % 2, step % half
+
+    def ring(step, side):
+        source = both.at[chunk(1) + (side,)] if step == 0 else moved.at[step - 1, side]
+        return send_to(
+            source,
+            ring_held.at[step, side],
+            ring_send.at[step, side],
+            ring_recv.at[step, side],
+            z_next,
+        )
+
+    for side in range(2):
+        ring(0, side).start()
+    hop_next(2)
+    for step in range(1, size):
+        which, at = chunk((step + 1) % size)
+        for side in range(2):
+            ring(step - 1, side).wait_recv()
+            moved[step - 1, side] = narrow(
+                wide(ring_held[step - 1, side]) + wide(both[which, at, side])
+            )
+            if step < size - 1:
+                ring(step, side).start()
+        if step < size - 1:
+            hop_next(2 + step)
+    last = send_to(moved.at[size - 2, 1], unit_held, unit_sem.at[0], unit_sem.at[1], x_side)
+    last.start()
+    for copy in exchange:
+        if copy is exchange[0]:
+            copy.wait()
+        else:
+            copy.wait_recv()
+    outs = [
+        pltpu.make_async_copy(grads_held, grad_out, out_sem.at[0]),
+        pltpu.make_async_copy(moved.at[size - 2, 0], unit_own, out_sem.at[1]),
+        pltpu.make_async_copy(sums_held.at[1, len(hops) - 1], norm_out, out_sem.at[2]),
+    ]
+    for copy in outs:
+        copy.start()
+    last.wait_recv()
+    final = pltpu.make_async_copy(unit_held, unit_x, out_sem.at[3])
+    final.start()
+    for copy in outs:
+        copy.wait()
+    final.wait()
+    last.wait_send()
+    core_far.wait_send()
+    core_near.wait_send()
+    over.wait_send()
+    for at, side in places:
+        across(0, at, side).wait_send()
+        across(1, at, side).wait_send()
+        to_core(at, side).wait_send()
+    for step in range(size - 1):
+        for side in range(2):
+            ring(step, side).wait_send()
+    for copy in exchange[1:]:
+        copy.wait_send()
+    for number in range(len(hops)):
+        hop(number).wait_send()
+
+
+def end(far, near, parts, upstream, clip, norm, norm_in):
+    size = lax.axis_size("z")
+    half = size // 2
+    groups, frames, model = clip.shape
+    rows, units = far.shape[-2:]
+    vmem = pl.BlockSpec(memory_space=pltpu.VMEM)
+    dma = pltpu.SemaphoreType.DMA
+
+    def buffer(*shape, dtype=jnp.bfloat16):
+        return pltpu.VMEM(shape, dtype)
+
+    return pl.pallas_call(
+        functools.partial(end_kernel, size),
+        in_specs=[vmem] * 10,
+        out_specs=[ANYWHERE] * 4,
+        out_shape=[
+            like(clip.shape),
+            like((8, model), jnp.float32),
+            like((rows, units)),
+            like((rows, units)),
+        ],
+        scratch_shapes=[
+            buffer(2, half, 2, rows, units),
+            buffer(half, 2, rows, units),
+            buffer(2, half, 2, rows, units),
+            buffer(size - 1, 2, rows, units),
+            buffer(size - 1, 2, rows, units),
+            buffer(rows, units),
+            buffer(2, groups * frames, model),
+            buffer(groups * frames, model),
+            buffer(groups * frames, model),
+            buffer(groups, frames, model),
+            buffer(groups, frames, model),
+            buffer(8, model, dtype=jnp.float32),
+            buffer(2, 5, 8, model, dtype=jnp.float32),
+            dma((2, half, 2)),
+            dma((2, half, 2)),
+            dma((half, 2)),
+            dma((half, 2)),
+            dma((4,)),
+            dma((2,)),
+            dma((size - 1, 2)),
+            dma((size - 1, 2)),
+            dma((groups,)),
+            dma((groups,)),
+            dma((5,)),
+            dma((5,)),
+            dma((2,)),
+            dma((4,)),
+        ],
+        compiler_params=pltpu.CompilerParams(
+            collective_id=2, has_side_effects=True, vmem_limit_bytes=56 * 2**20
+        ),
+        cost_estimate=pl.CostEstimate(
+            flops=10**7, bytes_accessed=300 * 2**20, transcendentals=0
+        ),
+        name="end",
+    )(far, near, *parts, upstream, clip, norm, norm_in)
 
 
 def clip_body(
@@ -1302,15 +1776,16 @@
     size = lax.axis_size("z")
     frame_block = tokens.shape[2]
 
-    attend_pieces = gather_attend([w_query, w_key, w_value, w_out.T])
-    clip_tokens = exchange_clips(tokens.reshape(-1, frame_block, model)).reshape(-1, model)
-    frames = wide(clip_tokens)
-    normed_one, scaled_one, inverse_one = layer_norm(frames[None], gain_one, bias_one)
-    rows_one = group_rows(narrow(normed_one)[0])
-    upstream = exchange_clips(cotangent.reshape(-1, frame_block, model)).reshape(-1, model)
-    cross_pieces = gather_whole(jnp.concatenate([c_query, c_out.T], axis=1))
-    up_full = gather_units(w_up)
-    down_full = gather_units(w_down.T)
+    split = split_heads([w_query, w_key, w_value, w_out.T])
+    norm_one = jnp.stack([gain_one, bias_one])
+    clip_tokens, rows_one, attend_weights = start_up(
+        tokens.reshape(-1, frame_block, model), split, norm_one
+    )
+    cross_pieces = gather_whole(jnp.concatenate([c_query, c_out.T], axis=1), clip_tokens)
+    upstream = after(cotangent.reshape(-1, frame_block, model), clip_tokens)
+    upstream = exchange_clips(upstream).reshape(-1, model)
+    up_full = gather_units(w_up, clip_tokens)
+    down_full = gather_units(w_down.T, clip_tokens)
     grad_rows3 = group_rows(upstream)
 
     at_f = block_of(at_y, at_x, at_c)
@@ -1331,7 +1806,7 @@
     count = take(take(text_len, at_y), at_z).reshape(1)
     norms = jnp.stack([gain_two, bias_two, gain_three, bias_three])
 
-    self_parts, qkv, mixed_one, log_total = attend_forward(ids, rows_one, attend_pieces)
+    self_parts, qkv, mixed_one, log_total = attend_forward(ids, rows_one, attend_weights)
     after_self, rows_two, cross_q, mixed_two, after_cross, own_three = cross_forward(
         ids, count, clip_tokens, group_terms(self_parts), norms, keys_values, cross_pieces
     )
@@ -1341,11 +1816,14 @@
         ids, rows_three, grad_rows3, up_full, down_full
     )
     back_terms = group_terms(back_parts)
-    fin_down = sum_units(feed_grads(ids, grad_rows3, active))
-    fin_up = sum_units(feed_grads(ids, rows_three, grad_hidden))
+    part_down = feed_grads(ids, grad_rows3, active)
+    part_up = feed_grads(ids, rows_three, grad_hidden)
+    fin_down, fin_up = sum_units(part_down), sum_units(part_up)
     feed_terms = group_terms(feed_parts)
     result = after_cross + wide(feed_terms[0]) + wide(feed_terms[1]) + wide(feed_terms[2])
-    result = exchange_clips(narrow(result).reshape(-1, frame_block, model)).reshape(tokens.shape)
+    result = narrow(result)
+    own_result = result
+    result = exchange_clips(result.reshape(-1, frame_block, model)).reshape(tokens.shape)
 
     grad_one_rows, own_one, own_two, grad_cq, grad_text, norm_grads = cross_backward(
         ids,
@@ -1360,7 +1838,8 @@
         cross_pieces,
     )
     grad_rows1 = group_rows(own_one)
-    fin_cross = sum_whole(cross_grads(rows_two, grad_cq, own_two, mixed_two))
+    cross_keep, cross_send = cross_grads(ids, rows_two, grad_cq, own_two, mixed_two)
+    fin_cross = sum_whole(cross_keep, cross_send)
     fin_cquery, fin_cout = fin_cross[:, :shard_width], fin_cross[:, shard_width:].T
 
     grad_text = grad_text.reshape(slots, 2, size, shard_width)
@@ -1385,30 +1864,37 @@
     grad_memory = wide(grad_memory.reshape(memory.shape))
 
     self_back, grad_qkv = attend_backward(
-        ids, grad_rows1, attend_pieces, qkv, mixed_one, log_total
-    )
-    terms = group_terms(self_back)
-    grad_one = wide(terms[0]) + wide(terms[1]) + wide(terms[2])
-    back_one, gain_g1, bias_g1 = norm_back(grad_one[None], scaled_one, inverse_one, gain_one)
-    input_grad = narrow(grad_one_rows + back_one[0])
-    input_grad = exchange_clips(input_grad.reshape(-1, frame_block, model))
+        after(ids, cross_keep, part_up, part_down, own_result),
+        grad_rows1,
+        attend_weights,
+        qkv,
+        mixed_one,
+        log_total,
+    )
+    far = attend_grads(ids, rows_one, grad_rows1, grad_qkv, mixed_one, 1)
+    near = attend_grads(ids, rows_one, grad_rows1, grad_qkv, mixed_one, 0)
+    input_grad, norm_grads, unit_own, unit_away = end(
+        far,
+        near,
+        self_back,
+        grad_one_rows,
+        clip_tokens.reshape(-1, frame_block, model),
+        norm_one,
+        norm_grads,
+    )
     input_grad = wide(input_grad).reshape(tokens.shape)
-    fin_query, fin_key, fin_value, fin_out = sum_attend(
-        attend_grads(ids, rows_one, grad_rows1, grad_qkv, mixed_one)
-    )
-
-    early = everywhere(norm_grads)
-    late = everywhere(jnp.stack([gain_g1, bias_g1]))
+    fin_query, fin_key, fin_value, fin_out = join_heads(unit_own, unit_away)
+
     return (
         result,
         input_grad,
         grad_memory,
-        late[0],
-        late[1],
-        early[0],
-        early[1],
-        early[2],
-        early[3],
+        norm_grads[0],
+        norm_grads[1],
+        norm_grads[2],
+        norm_grads[3],
+        norm_grads[4],
+        norm_grads[5],
         fin_query,
         fin_key,
         fin_value,

time: 967 us -> 918 us (0.949)
  Pallas kernels: 236 us -> 452 us
  waiting for transfers between devices: 441 us -> 231 us
  starting transfers between devices: 91.3 us -> 64.2 us
  other arithmetic: 74.9 us -> 55.5 us
    pallas_call x2 -> x4, Pallas kernels: 57.9 us -> 273 us  [the longest x1 115 us: end(): pl.pallas_call(functools.partial(end_kernel, size), in_specs=[vmem] * 10,...]
    ppermute x63 -> x45, waiting for transfers between devices: 256 us -> 166 us  [pair_swap(): return lax.ppermute(values, axis_name, [(0, 1), (1, 0)])]
    ppermute x6 -> x2, waiting for transfers between devices: 63 us -> 10.7 us  [ring_flip(): return lax.ppermute(values, 'z', [(i, i ^ bit) for i in range(size)])]
    ppermute x15 -> x12, waiting for transfers between devices: 89 us -> 53.7 us  [ring_shift(): lax.ppermute(values, 'z', [(i, (i + distance) % size) for i in range(size)])]
    all_to_all x4 -> x2, waiting for transfers between devices: 32.4 us -> 0.01 us  [exchange_clips(): return lax.all_to_all(values, ('y', 'z'), 0, 0, tiled=True)]
    unnamed x146 -> x170, local copies, waits for them, and re-layouts: 20.2 us -> 42.5 us
    ppermute x63 -> x45, starting transfers between devices: 45 us -> 23.8 us  [pair_swap(): return lax.ppermute(values, axis_name, [(0, 1), (1, 0)])]
    all_to_all x4 -> x2, starting transfers between devices: 19.6 us -> 7.95 us  [exchange_clips(): return lax.all_to_all(values, ('y', 'z'), 0, 0, tiled=True)]
  transfers between devices with their start and end apart: 93 -> 65, of which waited for: 35 -> 25; matrix products, arithmetic and copies ran while one was open for 15% -> 10% of each run, Pallas kernels for 19% -> 45%
where the time goes in v3:
time: 918 us; the launch traced here: 907 us
  Pallas kernels  452 us (49%)
  waiting for transfers between devices  231 us (25%)
  local copies, waits for them, and re-layouts  88 us (10%)
  starting transfers between devices  64.2 us (7%)
  other arithmetic  55.5 us (6%)
  between operations  15.5 us (2%)
    ppermute x45, waiting for transfers between devices, pair_swap(): return lax.ppermute(values, axis_name, [(0, 1), (1, 0)])  166 us
    pallas_call x1, Pallas kernels, end(): pl.pallas_call(functools.partial(end_kernel, size), in_specs=[vmem] * 10,...  115 us
    pallas_call x1, Pallas kernels, start_up(): pl.pallas_call(functools.partial(start_kernel, size), in_specs=[vmem] * 3...  99.8 us
    ppermute x12, waiting for transfers between devices, ring_shift(): lax.ppermute(values, 'z', [(i, (i + distance) % size) for i in range(size)])  53.7 us
    pallas_call x1, Pallas kernels, attend_backward(): pl.pallas_call(attend_backward_kernel, in_specs=[SCALARS] + [vmem] * (PIE...  49.4 us
    pallas_call x1, Pallas kernels, feed(): pl.pallas_call(feed_kernel, in_specs=[SCALARS] + [ANYWHERE] * 10, out_spe...  44.3 us
    unnamed x170, local copies, waits for them, and re-layouts  42.5 us
    pallas_call x1, Pallas kernels, attend_forward(): pl.pallas_call(attend_forward_kernel, in_specs=[SCALARS] + [pl.BlockSpec(...  38.3 us
  transfers between devices with their start and end apart: 65, of which 25 were waited for; matrix products, arithmetic and copies ran while one was open for 10% of the time, Pallas kernels for 45%

profile of v3, /device:TPU:0, one launch (start us, length us, event | category | flops | bytes accessed | tf_op | source)
XLA Modules:
  0.0 907.5 jit_solution(6525731849474069247)
XLA Ops:
  38.6 99.8 %start_up.1 = (bf16[8,48,1536]{2,1,0:T(8,128)(2,1)S(1)}, bf16[384,1536]{1,0:T(8,128)(2,1)S(1)}, bf16[384,1536]{1,0:T(8,128)(2,1)S(1)}, bf16[384,1536]{1,0:T(8,12...) custom-call(bf16[8,48,1536]{2,1,0:T(8,128)(2,1)S(1)} %bitcast.202, ...), custom_call_target="tpu_custom_call" | custom-call | flops 10000000 | bytes 209715200 | tf_op jit(solution)/shard_map/start_up/pallas_call | solution.py:1445
  152.9 10.8 %collective-permute-done.9 = bf16[192,768]{1,0:T(8,128)(2,1)} collective-permute-done((bf16[192,768]{1,0:T(8,128)(2,1)S(1)}, bf16[192,768]{1,0:T(8,128)(2,1)}, u32[]{:S(2)}, u32[]{:S(2)}) %collective-permute-start.9) | collective-permute-done | bytes 294944 | tf_op jit(solution)/shard_map/ppermute | solution.py:406
  170.5 11.3 %collective-permute-done.10 = bf16[192,768]{1,0:T(8,128)(2,1)S(1)} collective-permute-done((bf16[192,768]{1,0:T(8,128)(2,1)}, bf16[192,768]{1,0:T(8,128)(2,1)S(1)}, u32[]{:S(2)}, u32[]{:S(2)}) %collective-permute-start.10) | collective-permute-done | bytes 294944 | tf_op jit(solution)/shard_map/ppermute | solution.py:406
  197.8 38.3 %attend_forward.1 = (bf16[384,1536]{1,0:T(8,128)(2,1)}, bf16[384,1536]{1,0:T(8,128)(2,1)}, bf16[384,1536]{1,0:T(8,128)(2,1)}, bf16[384,1536]{1,0:T(8,128)(2,1)},...) custom-call(s32[4]{0:T(128)} %pad_add_fusion.ids, ...), custom_call_target="tpu_custom_call" | custom-call | flops 30000001024 | bytes 25165824 | tf_op jit(solution)/shard_map/attend_forward/pallas_call | solution.py:714
  259.2 19.6 %collective-permute-done.13.refs_8_.refs_11_ = bf16[4,192,768]{2,1,0:T(8,128)(2,1)} collective-permute-done((bf16[4,192,768]{2,1,0:T(8,128)(2,1)}, bf16[4,192,768]{2,1,0:T(8,128)(2,1)}, u32[]{:S(2)}, u32[]{:S(2)}) %collective-permute-start.13) | collective-permute-done | bytes 1179680 | tf_op jit(solution)/shard_map/ppermute | solution.py:401
  278.8 25.3 %collective-permute-done.14.refs_9_.refs_12_ = bf16[4,192,768]{2,1,0:T(8,128)(2,1)} collective-permute-done((bf16[4,192,768]{2,1,0:T(8,128)(2,1)}, bf16[4,192,768]{2,1,0:T(8,128)(2,1)}, u32[]{:S(2)}, u32[]{:S(2)}) %collective-permute-start.14) | collective-permute-done | bytes 1179680 | tf_op jit(solution)/shard_map/ppermute | solution.py:401
  313.1 16.2 %collective-permute-done.2.refs_3_ = bf16[384,1536]{1,0:T(8,128)(2,1)} collective-permute-done((bf16[384,1536]{1,0:T(8,128)(2,1)}, bf16[384,1536]{1,0:T(8,128)(2,1)}, u32[]{:S(2)}, u32[]{:S(2)}) %collective-permute-start.2) | collective-permute-done | bytes 1179680 | tf_op jit(solution)/shard_map/ppermute | solution.py:401
  329.4 20.5 %cross_forward.1 = (f32[384,1536]{1,0:T(8,128)}, bf16[384,1536]{1,0:T(8,128)(2,1)S(1)}, bf16[384,1536]{1,0:T(8,128)(2,1)S(1)}, bf16[384,1536]{1,0:T(8,128)(2,1)S...) custom-call(s32[4]{0:T(128)S(1)} %copy-done.14, s32[1]{0:T(128)} %bitcast.4.count, bf16[384,1536]{1,0:T(8,128)(2,1)} %bitcast.201, ...), custom_call_target="tpu_custom_call" | custom-call | flops 12000000000 | bytes 25165824 | tf_op jit(solution)/shard_map/cross_forward/pallas_call | solution.py:1062
  354.3 24.3 %collective-permute-done.20.refs_2_ = bf16[384,1536]{1,0:T(8,128)(2,1)S(1)} collective-permute-done((bf16[384,1536]{1,0:T(8,128)(2,1)S(1)}, bf16[384,1536]{1,0:T(8,128)(2,1)S(1)}, u32[]{:S(2)}, u32[]{:S(2)}) %collective-permute-start.20) | collective-permute-done | bytes 1179680 | tf_op jit(solution)/shard_map/ppermute | solution.py:401
  381.8 44.3 %feed_forward.1 = (bf16[384,1536]{1,0:T(8,128)(2,1)}, bf16[384,1536]{1,0:T(8,128)(2,1)}, bf16[384,1536]{1,0:T(8,128)(2,1)}, bf16[384,1536]{1,0:T(8,128)(2,1)}, b...) custom-call(s32[4]{0:T(128)} %pad_add_fusion.ids, ...), custom_call_target="tpu_custom_call" | custom-call | flops 28991029248 | bytes 37748736 | tf_op jit(solution)/shard_map/feed_forward/pallas_call | solution.py:905
  428.9 14.9 %feed_grads.2 = bf16[2,4,2,2,192,384]{5,4,3,2,1,0:T(8,128)(2,1)S(1)} custom-call(s32[4]{0:T(128)S(1)} %copy-done.15, bf16[384,1536]{1,0:T(8,128)(2,1)S(1)} %copy-done.36, bf16[384,1536]{1,0:T(8,128)(2,1)S(1)} %copy-done.40, bf16[384,1536]{1,0:T(8,128)(2,1)S(1)} %copy-done.38, bf16[384,1536]{1,0:T(8,128)(2,1)} %collective-permute-done.21.refs_3_, ...), custom_call_target="tpu_custom_call" | custom-call | flops 7247757312 | bytes 16777216 | tf_op jit(solution)/shard_map/feed_grads/pallas_call | solution.py:951
  449.7 27.2 %collective-permute-done.34.refs_3_ = bf16[384,1536]{1,0:T(8,128)(2,1)S(1)} collective-permute-done((bf16[384,1536]{1,0:T(8,128)(2,1)S(1)}, bf16[384,1536]{1,0:T(8,128)(2,1)S(1)}, u32[]{:S(2)}, u32[]{:S(2)}) %collective-permute-start.34) | collective-permute-done | bytes 1179680 | tf_op jit(solution)/shard_map/ppermute | solution.py:401
  477.9 26.3 %cross_backward.1 = (f32[384,1536]{1,0:T(8,128)}, bf16[384,1536]{1,0:T(8,128)(2,1)}, bf16[384,1536]{1,0:T(8,128)(2,1)}, bf16[384,1536]{1,0:T(8,128)(2,1)}, bf16[64,3072]{1,0:T(8,128)(2,1)}, /*index=5*/f32[4,1536]{1,0:T(4,128)}) custom-call(s32[4]{0:T(128)} %pad_add_fusion.ids, s32[1]{0:T(128)} %bitcast.4.count, bf16[384,1536]{1,0:T(8,128)(2,1)} %bitcast.206, ...), custom_call_target="tpu_custom_call" | custom-call | flops 16000000000 | bytes 29360128 | tf_op jit(solution)/shard_map/cross_backward/pallas_call | solution.py:1166
  506.8 9.7 %collective-permute-done.38 = bf16[4,64,768]{2,1,0:T(8,128)(2,1)S(1)} collective-permute-done((bf16[4,64,768]{2,1,0:T(8,128)(2,1)S(1)}, bf16[4,64,768]{2,1,0:T(8,128)(2,1)S(1)}, u32[]{:S(2)}, u32[]{:S(2)}) %collective-permute-start.38) | collective-permute-done | bytes 393248 | tf_op jit(solution)/shard_map/ppermute | solution.py:401
  521.2 8.6 cross_grads.1
  536.9 8.1 collective-permute-done.41
  547.5 8.6 collective-permute-done.43
  582.7 14.0 %feed_grads.3 = bf16[2,4,2,2,192,384]{5,4,3,2,1,0:T(8,128)(2,1)S(1)} custom-call(s32[4]{0:T(128)S(1)} %copy-done.16, bf16[384,1536]{1,0:T(8,128)(2,1)S(1)} %bitcast.207, bf16[384,1536]{1,0:T(8,128)(2,1)S(1)} %copy-done.30, bf16[384,1536]{1,0:T(8,128)(2,1)S(1)} %copy-done.28, bf16[384,1536]{1,0:T(8,128)(2,1)S(1)} %copy-done.32, ...), custom_call_target="tpu_custom_call" | custom-call | flops 7247757312 | bytes 16777216 | tf_op jit(solution)/shard_map/feed_grads/pallas_call | solution.py:951
  599.5 10.7 %collective-permute-done.45 = bf16[512,192]{0,1:T(8,128)(2,1)} collective-permute-done((bf16[512,192]{0,1:T(8,128)(2,1)}, bf16[512,192]{0,1:T(8,128)(2,1)}, u32[]{:S(2)}, u32[]{:S(2)}) %collective-permute-start.45) | collective-permute-done | bytes 196640 | tf_op jit(solution)/shard_map/ppermute | solution.py:411
  613.9 10.2 %collective-permute-done.47 = bf16[2,512,192]{1,2,0:T(8,128)(2,1)S(1)} collective-permute-done((bf16[2,512,192]{1,2,0:T(8,128)(2,1)S(1)}, bf16[2,512,192]{1,2,0:T(8,128)(2,1)S(1)}, u32[]{:S(2)}, u32[]{:S(2)}) %collective-permute-start.47) | collective-permute-done | bytes 393248 | tf_op jit(solution)/shard_map/ppermute | solution.py:401
  634.2 49.4 %attend_backward.1 = (bf16[384,1536]{1,0:T(8,128)(2,1)}, bf16[384,1536]{1,0:T(8,128)(2,1)}, bf16[384,1536]{1,0:T(8,128)(2,1)}, bf16[384,1536]{1,0:T(8,128)(2,1)}, bf16[2,4,384,576]{3,2,1,0:T(8,128)(2,1)}) custom-call(s32[4]{0:T(128)} %pad_add_fusion.ids, bf16[384,1536]{1,0:T(8,128)(2,1)} %get-tuple-element.96.refs_0_.refs_4_, bf16[384,1536]{1,0:T(8,128)(2,1)} %copy-done.33, ...), custom_call_target="tpu_custom_call" | custom-call | flops 49999998976 | bytes 25165824 | tf_op jit(solution)/shard_map/attend_backward/pallas_call | solution.py:737
  686.2 10.2 %attend_grads.3.near = bf16[2,2,2,192,768]{4,3,2,1,0:T(8,128)(2,1)S(1)} custom-call(s32[4]{0:T(128)S(1)} %copy-done.17, bf16[384,1536]{1,0:T(8,128)(2,1)S(1)} %copy-done.20, bf16[384,1536]{1,0:T(8,128)(2,1)S(1)} %copy-done.22, bf16[384,1536]{1,0:T(8,128)(2,1)S(1)} %copy-done.24, bf16[384,1536]{1,0:T(8,128)(2,1)S(1)} %copy-done.26, ...), custom_call_target="tpu_custom_call" | custom-call | flops 6000000000 | bytes 12582912 | tf_op jit(solution)/shard_map/attend_grads/pallas_call | solution.py:782
  697.8 10.3 %attend_grads.2.far = bf16[2,2,2,192,768]{4,3,2,1,0:T(8,128)(2,1)S(1)} custom-call(s32[4]{0:T(128)S(1)} %copy-done.17, bf16[384,1536]{1,0:T(8,128)(2,1)S(1)} %copy-done.20, bf16[384,1536]{1,0:T(8,128)(2,1)S(1)} %copy-done.22, bf16[384,1536]{1,0:T(8,128)(2,1)S(1)} %copy-done.24, bf16[384,1536]{1,0:T(8,128)(2,1)S(1)} %copy-done.26, ...), custom_call_target="tpu_custom_call" | custom-call | flops 6000000000 | bytes 12582912 | tf_op jit(solution)/shard_map/attend_grads/pallas_call | solution.py:782
  709.5 115.2 %end.1 = (bf16[8,48,1536]{2,1,0:T(8,128)(2,1)}, f32[8,1536]{1,0:T(8,128)}, bf16[192,768]{1,0:T(8,128)(2,1)}, bf16[192,768]{1,0:T(8,128)(2,1)}) custom-call(bf16[2,2,2,192,768]{4,3,2,1,0:T(8,128)(2,1)} %copy-done.6, bf16[2,2,2,192,768]{4,3,2,1,0:T(8,128)(2,1)} %copy-done.5, bf16[384,1536]{1,0:T(8,128)(2,1)} %get-tuple-element.107.part_own, ...), custom_call_target="tpu_custom_call" | custom-call | flops 10000000 | bytes 314572800 | tf_op jit(solution)/shard_map/end/pallas_call | solution.py:1700
  (397 shorter events, 258.3 us)
Async XLA Ops:
  7.2 374.5 %all-gather.3.cloned.1.call-start = ((), (), s32[]{:S(2)}) async-start(), calls=%async_computation.4 | async-start | bytes 5308416 | tf_op jit(solution)/shard_map/all_gather | solution.py:484
  33.5 110.3 %collective-permute-start.26 = (bf16[2,192,384]{2,1,0:T(8,128)(2,1)}, bf16[2,192,384]{2,1,0:T(8,128)(2,1)}, u32[]{:S(2)}, u32[]{:S(2)}) collective-permute-start(bf16[2,192,384]{2,1,0:T(8,128)(2,1)} %bitcast.195), channel_id=1, source_target_pairs={{0,4},{4,0},{1,5},{5,1},{2,6},{6,2},{3,7},{7,3},{8,12},{12,8},{9,1... | collective-permute-start | bytes 884744 | tf_op jit(solution)/shard_map/ppermute | solution.py:401
  146.0 235.8 %all-gather.5.cloned.1.call-start = ((), (), s32[]{:S(2)}) async-start(), calls=%async_computation.5 | async-start | bytes 5308416 | tf_op jit(solution)/shard_map/all_gather | solution.py:484
  152.8 35.3 %collective-permute-start.28 = (bf16[2,192,384]{2,1,0:T(8,128)(2,1)S(1)}, bf16[2,192,384]{2,1,0:T(8,128)(2,1)S(1)}, u32[]{:S(2)}, u32[]{:S(2)}) collective-permute-start(bf16[2,192,384]{2,1,0:T(8,128)(2,1)S(1)} %bitcast.238), channel_id=1, source_target_pairs={{0,4},{4,0},{1,5},{5,1},{2,6},{6,2},{3,7},{7,3},{8,12},{12,8},{9,1... | collective-permute-start | bytes 884744 | tf_op jit(solution)/shard_map/ppermute | solution.py:401
  185.3 50.9 %collective-permute-start.5 = (bf16[64,768]{1,0:T(8,128)(2,1)S(1)}, bf16[64,768]{1,0:T(8,128)(2,1)S(1)}, u32[]{:S(2)}, u32[]{:S(2)}) collective-permute-start(bf16[64,768]{1,0:T(8,128)(2,1)S(1)} %get-tuple-element.159), channel_id=1, source_target_pairs={{0,2},{1,3},{2,0},{3,1},{4,6},{5,7},{6,4},{7,5},{8,10},{9,11},{10,... | collective-permute-start | bytes 294920 | tf_op jit(solution)/shard_map/ppermute | solution.py:406
  196.7 50.5 %collective-permute-start.12 = (bf16[4,192,768]{2,1,0:T(8,128)(2,1)}, bf16[4,192,768]{2,1,0:T(8,128)(2,1)}, u32[]{:S(2)}, u32[]{:S(2)}) collective-permute-start(bf16[4,192,768]{2,1,0:T(8,128)(2,1)} %pad_maximum_fusion.refs_6_.refs_9_), channel_id=1, source_target_pairs={{0,16},{16,0},{1,17},{17,1},{2,18},{18,2},{3,19},{19,3},{4,20},{20... | collective-permute-start | bytes 3538952 | tf_op jit(solution)/shard_map/ppermute | solution.py:401
  242.1 36.7 %collective-permute-start.13 = (bf16[4,192,768]{2,1,0:T(8,128)(2,1)}, bf16[4,192,768]{2,1,0:T(8,128)(2,1)}, u32[]{:S(2)}, u32[]{:S(2)}) collective-permute-start(bf16[4,192,768]{2,1,0:T(8,128)(2,1)} %pad_maximum_fusion.refs_6_.refs_9_), channel_id=1, source_target_pairs={{0,8},{8,0},{1,9},{9,1},{2,10},{10,2},{3,11},{11,3},{4,12},{12,4},... | collective-permute-start | bytes 3538952 | tf_op jit(solution)/shard_map/ppermute | solution.py:401
  247.3 56.8 %collective-permute-start.14 = (bf16[4,192,768]{2,1,0:T(8,128)(2,1)}, bf16[4,192,768]{2,1,0:T(8,128)(2,1)}, u32[]{:S(2)}, u32[]{:S(2)}) collective-permute-start(bf16[4,192,768]{2,1,0:T(8,128)(2,1)} %collective-permute-done.12.refs_7_.refs_10_), channel_id=1, source_target_pairs={{0,8},{8,0},{1,9},{9,1},{2,10},{10,2},{3,11},{11,3},{4,12},{12,4},... | collective-permute-start | bytes 3538952 | tf_op jit(solution)/shard_map/ppermute | solution.py:401
  248.3 64.0 %all-to-all-start = ((bf16[8,48,1536]{2,1,0:T(8,128)(2,1)}), bf16[8,48,1536]{2,1,0:T(8,128)(2,1)S(1)}, u32[]{:S(2)}, u32[]{:S(2)}) async-start(bf16[8,48,1536]{2,1,0:T(8,128)(2,1)} %bitcast.229), calls=%async_computation | async-start | bytes 2359296 | tf_op jit(solution)/shard_map/all_to_all | solution.py:435
  251.9 585.8 %reduce-scatter.3.cloned.1.call-start = ((), (), s32[]{:S(2)}) async-start(), calls=%async_computation.6 | async-start | bytes 5308416 | tf_op jit(solution)/shard_map/reduce_scatter | solution.py:490
  254.2 58.2 %collective-permute-start.15 = (bf16[4,192,768]{2,1,0:T(8,128)(2,1)}, bf16[4,192,768]{2,1,0:T(8,128)(2,1)}, u32[]{:S(2)}, u32[]{:S(2)}) collective-permute-start(bf16[4,192,768]{2,1,0:T(8,128)(2,1)} %pad_maximum_fusion.refs_6_.refs_9_), channel_id=1, source_target_pairs={{0,4},{4,0},{1,5},{5,1},{2,6},{6,2},{3,7},{7,3},{8,12},{12,8},{9,1... | collective-permute-start | bytes 3538952 | tf_op jit(solution)/shard_map/ppermute | solution.py:401
  258.5 70.9 %collective-permute-start.2 = (bf16[384,1536]{1,0:T(8,128)(2,1)}, bf16[384,1536]{1,0:T(8,128)(2,1)}, u32[]{:S(2)}, u32[]{:S(2)}) collective-permute-start(bf16[384,1536]{1,0:T(8,128)(2,1)} %add_convert_fusion.5), channel_id=1, source_target_pairs={{0,8},{8,0},{1,9},{9,1},{2,10},{10,2},{3,11},{11,3},{4,12},{12,4},... | collective-permute-start | bytes 3538952 | tf_op jit(solution)/shard_map/ppermute | solution.py:401
  259.2 70.2 %collective-permute-start.16 = (bf16[4,192,768]{2,1,0:T(8,128)(2,1)}, bf16[4,192,768]{2,1,0:T(8,128)(2,1)}, u32[]{:S(2)}, u32[]{:S(2)}) collective-permute-start(bf16[4,192,768]{2,1,0:T(8,128)(2,1)} %collective-permute-done.12.refs_7_.refs_10_), channel_id=1, source_target_pairs={{0,4},{4,0},{1,5},{5,1},{2,6},{6,2},{3,7},{7,3},{8,12},{12,8},{9,1... | collective-permute-start | bytes 3538952 | tf_op jit(solution)/shard_map/ppermute | solution.py:401
  278.8 50.6 %collective-permute-start.17 = (bf16[4,192,768]{2,1,0:T(8,128)(2,1)}, bf16[4,192,768]{2,1,0:T(8,128)(2,1)}, u32[]{:S(2)}, u32[]{:S(2)}) collective-permute-start(bf16[4,192,768]{2,1,0:T(8,128)(2,1)} %collective-permute-done.13.refs_8_.refs_11_), channel_id=1, source_target_pairs={{0,4},{4,0},{1,5},{5,1},{2,6},{6,2},{3,7},{7,3},{8,12},{12,8},{9,1... | collective-permute-start | bytes 3538952 | tf_op jit(solution)/shard_map/ppermute | solution.py:401
  312.4 41.4 %collective-permute-start.23 = (bf16[384,1536]{1,0:T(8,128)(2,1)S(1)}, bf16[384,1536]{1,0:T(8,128)(2,1)S(1)}, u32[]{:S(2)}, u32[]{:S(2)}) collective-permute-start(bf16[384,1536]{1,0:T(8,128)(2,1)S(1)} %bitcast.203), channel_id=1, source_target_pairs={{0,8},{8,0},{1,9},{9,1},{2,10},{10,2},{3,11},{11,3},{4,12},{12,4},... | collective-permute-start | bytes 3538952 | tf_op jit(solution)/shard_map/ppermute | solution.py:401
  517.2 45.4 %collective-permute-start.29 = (bf16[384,1536]{1,0:T(8,128)(2,1)}, bf16[384,1536]{1,0:T(8,128)(2,1)}, u32[]{:S(2)}, u32[]{:S(2)}) collective-permute-start(bf16[384,1536]{1,0:T(8,128)(2,1)} %get-tuple-element.87), channel_id=1, source_target_pairs={{0,4},{4,0},{1,5},{5,1},{2,6},{6,2},{3,7},{7,3},{8,12},{12,8},{9,1... | collective-permute-start | bytes 3538952 | tf_op jit(solution)/shard_map/ppermute | solution.py:401
  531.9 95.1 %collective-permute-start.49 = (bf16[2,2,4,192,768]{4,3,2,1,0:T(8,128)(2,1)}, bf16[2,2,4,192,768]{4,3,2,1,0:T(8,128)(2,1)}, u32[]{:S(2)}, u32[]{:S(2)}) collective-permute-start(bf16[2,2,4,192,768]{4,3,2,1,0:T(8,128)(2,1)} %get-tuple-element.118), channel_id=1, source_target_pairs={{0,4},{4,0},{1,5},{5,1},{2,6},{6,2},{3,7},{7,3},{8,12},{12,8},{9,1... | collective-permute-start | bytes 14155784 | tf_op jit(solution)/shard_map/ppermute | solution.py:401
  546.6 52.4 %collective-permute-start.36 = (bf16[384,1536]{1,0:T(8,128)(2,1)}, bf16[384,1536]{1,0:T(8,128)(2,1)}, u32[]{:S(2)}, u32[]{:S(2)}) collective-permute-start(bf16[384,1536]{1,0:T(8,128)(2,1)} %get-tuple-element.96.refs_0_.refs_4_), channel_id=1, source_target_pairs={{0,8},{8,0},{1,9},{9,1},{2,10},{10,2},{3,11},{11,3},{4,12},{12,4},... | collective-permute-start | bytes 3538952 | tf_op jit(solution)/shard_map/ppermute | solution.py:401
  567.6 46.3 %all-to-all-start.1 = ((bf16[8,48,1536]{2,1,0:T(8,128)(2,1)}), bf16[8,48,1536]{2,1,0:T(8,128)(2,1)}, u32[]{:S(2)}, u32[]{:S(2)}) async-start(bf16[8,48,1536]{2,1,0:T(8,128)(2,1)} %bitcast.211), calls=%async_computation.1 | async-start | bytes 2359296 | tf_op jit(solution)/shard_map/all_to_all | solution.py:435
  572.0 268.5 %reduce-scatter.5.cloned.1.call-start = ((), (), s32[]{:S(2)}) async-start(), calls=%async_computation.7 | async-start | bytes 5308416 | tf_op jit(solution)/shard_map/reduce_scatter | solution.py:490
  573.8 36.4 %collective-permute-start.45 = (bf16[512,192]{0,1:T(8,128)(2,1)}, bf16[512,192]{0,1:T(8,128)(2,1)}, u32[]{:S(2)}, u32[]{:S(2)}) collective-permute-start(bf16[512,192]{0,1:T(8,128)(2,1)} %add_convert_fusion.11), channel_id=1, source_target_pairs={{0,2},{1,3},{2,0},{3,1},{4,6},{5,7},{6,4},{7,5},{8,10},{9,11},{10,... | collective-permute-start | bytes 589832 | tf_op jit(solution)/shard_map/ppermute | solution.py:411
  598.9 34.3 %collective-permute-start.35 = (bf16[384,1536]{1,0:T(8,128)(2,1)}, bf16[384,1536]{1,0:T(8,128)(2,1)S(1)}, u32[]{:S(2)}, u32[]{:S(2)}) collective-permute-start(bf16[384,1536]{1,0:T(8,128)(2,1)} %get-tuple-element.96.refs_0_.refs_4_), channel_id=1, source_target_pairs={{0,4},{4,0},{1,5},{5,1},{2,6},{6,2},{3,7},{7,3},{8,12},{12,8},{9,1... | collective-permute-start | bytes 3538952 | tf_op jit(solution)/shard_map/ppermute | solution.py:401
  625.1 210.9 %collective-permute-start.48 = (bf16[2,2,512,192]{2,3,1,0:T(8,128)(2,1)}, bf16[2,2,512,192]{2,3,1,0:T(8,128)(2,1)}, u32[]{:S(2)}, u32[]{:S(2)}) collective-permute-start(bf16[2,2,512,192]{2,3,1,0:T(8,128)(2,1)} %maximum_select_fusion.3), channel_id=1, source_target_pairs={{0,16},{16,0},{1,17},{17,1},{2,18},{18,2},{3,19},{19,3},{4,20},{20... | collective-permute-start | bytes 2359304 | tf_op jit(solution)/shard_map/ppermute | solution.py:401
  632.9 195.0 %collective-permute-start.50 = (bf16[2,4,192,768]{3,2,1,0:T(8,128)(2,1)}, bf16[2,4,192,768]{3,2,1,0:T(8,128)(2,1)}, u32[]{:S(2)}, u32[]{:S(2)}) collective-permute-start(bf16[2,4,192,768]{3,2,1,0:T(8,128)(2,1)} %get-tuple-element.128), channel_id=1, source_target_pairs={{0,8},{8,0},{1,9},{9,1},{2,10},{10,2},{3,11},{11,3},{4,12},{12,4},... | collective-permute-start | bytes 7077896 | tf_op jit(solution)/shard_map/ppermute | solution.py:401
  (123 other events, 2049.7 us)
Sparse Core Ops, SparseCore 0:
  146.1 127.3 all-gather.2
  275.6 87.2 all-gather.4
  446.2 101.6 reduce-scatter.2
  599.0 98.6 reduce-scatter.4

commit v4 on v3

--- a/solution.py
+++ b/solution.py
@@ -472,22 +472,26 @@
     return [jnp.concatenate([halves[0, :, i], halves[1, :, i]], axis=1) for i in range(4)]
 
 
-def gather_units(shard, gate):
+def gather_units(shards):
     at_x, at_c = lax.axis_index("x"), lax.axis_index("c")
-    rows = shard.shape[0]
-    split = jnp.transpose(shard.reshape(rows, 2, 2, -1), (1, 2, 0, 3))
+    rows, units = shards[0].shape
+    split = jnp.stack([shard.reshape(rows, 2, 2, units // 4) for shard in shards])
+    split = jnp.transpose(split, (2, 3, 0, 1, 4))
     mine = take(split, at_x)
     other = pair_swap(take(split, 1 - at_x), "x")
     pair = jnp.stack([mine, other], axis=1)
     pair = jnp.stack([take(pair, at_c), pair_swap(take(pair, 1 - at_c), "c")], axis=1)
-    own = after(pair.reshape((1, PIECES) + pair.shape[2:]), gate)
+    own = pair.reshape((1, PIECES) + pair.shape[2:])
     return lax.all_gather(own, ("y", "z"), axis=0, tiled=True)
 
 
-def sum_units(grad):
+def scatter_units(grad):
+    grad = grad.reshape((-1,) + grad.shape[2:])
+    return lax.psum_scatter(grad, ("y", "z"), scatter_dimension=0, tiled=True)[0]
+
+
+def join_units(total):
     at_x, at_c = lax.axis_index("x"), lax.axis_index("c")
-    grad = grad.reshape((-1,) + grad.shape[2:])
-    total = lax.psum_scatter(grad, ("y", "z"), scatter_dimension=0, tiled=True)[0]
     away = pair_swap(total[2:], "x")
     pair = ordered(at_x, total[:2], away)
     whole = ordered(at_c, pair[:, 0], pair_swap(pair[:, 1], "c"))
@@ -495,34 +499,17 @@
     return whole.reshape(whole.shape[0], -1)
 
 
-def gather_whole(shard, gate):
-    pieces = [after(shard, gate)]
-    for _ in range(1, lax.axis_size("z")):
-        pieces.append(ring_shift(pieces[-1], 1))
-    pieces = [jnp.stack(pieces)]
-    pieces = pieces + [pair_swap(pieces[0], "y")]
-    pieces = pieces + [pair_swap(piece, "x") for piece in pieces]
-    return pieces + [pair_swap(piece, "c") for piece in pieces]
-
-
-def fold_pair(kept, sent, name):
-    return wide(kept) + wide(pair_swap(sent, name))
-
-
-def sum_whole(keep, send):
+def sum_plane(keep, send, gate):
     got = pair_swap(send, "c")
     away = narrow(wide(keep[1]) + wide(got[1]))
     near = narrow(wide(keep[0]) + wide(got[0]))
-    got = pair_swap(away, "x")
+    return near, pair_swap(after(away, gate), "x")
+
+
+def sum_plane_rest(near, got):
     away = narrow(wide(near[1]) + wide(got[1]))
     near = narrow(wide(near[0]) + wide(got[0]))
-    parts = narrow(wide(near) + wide(pair_swap(away, "y")))
-    size = parts.shape[0]
-    moving = parts[1]
-    for step in range(2, size + 1):
-        total = wide(ring_shift(moving, 1)) + wide(parts[step % size])
-        moving = narrow(total)
-    return total
+    return narrow(wide(near) + wide(pair_swap(away, "y")))
 
 
 def dot_nt(left, right):
@@ -809,15 +796,15 @@
 
 
 def feed_kernel(ids, *refs):
-    rows_in, grads_in, up_in, down_in = refs[0:4], refs[4:8], refs[8], refs[9]
-    result_out, back_out, active_out, hidden_out = refs[10:14], refs[14:18], refs[18], refs[19]
-    rows_all, grads_all, up, down, result, back, active, hidden, w_sem, in_sem, out_sem = refs[20:]
+    rows_in, grads_in, units_in = refs[0:4], refs[4:8], refs[8]
+    result_out, back_out, active_out, hidden_out = refs[9:13], refs[13:17], refs[17], refs[18]
+    rows_all, grads_all, up, down, result, back, active, hidden, w_sem, in_sem, out_sem = refs[19:]
     at_x, at_c = ids[1], ids[2]
     rows, model = rows_in[0].shape
-    shard_rows, width = up_in.shape[-2:]
-    groups = up_in.shape[0] // 2
+    shard_rows, width = units_in.shape[-2:]
+    groups = units_in.shape[0] // 2
     copies = []
-    for which, (source, target) in enumerate(((up_in, up), (down_in, down))):
+    for which, target in enumerate((up, down)):
         for other_y in range(2):
             for at_z in range(groups):
                 for piece in range(PIECES):
@@ -826,7 +813,7 @@
                     lanes = slice((at_z % 2) * width, (at_z % 2 + 1) * width)
                     copies.append(
                         pltpu.make_async_copy(
-                            source.at[other_y * groups + at_z, piece],
+                            units_in.at[other_y * groups + at_z, piece, which],
                             target.at[at_z // 2, place_rows, lanes],
                             w_sem.at[len(copies)],
                         )
@@ -896,15 +883,15 @@
             copy.wait()
 
 
-def feed(ids, rows_in, grads_in, up, down):
+def feed(ids, rows_in, grads_in, both):
     rows, model = rows_in[0].shape
-    units = up.shape[0] // 2 * up.shape[-1]
+    units = both.shape[0] // 2 * both.shape[-1]
     outs = [like((rows, model))] * 8 + [like((PIECES, rows, units))] * 2
-    blocks = up.shape[0] // 4
-    weight = pltpu.VMEM((blocks, model, 2 * up.shape[-1]), jnp.bfloat16)
+    blocks = both.shape[0] // 4
+    weight = pltpu.VMEM((blocks, model, 2 * both.shape[-1]), jnp.bfloat16)
     out = pl.pallas_call(
         feed_kernel,
-        in_specs=[SCALARS] + [ANYWHERE] * 10,
+        in_specs=[SCALARS] + [ANYWHERE] * 9,
         out_specs=[ANYWHERE] * 10,
         out_shape=outs,
         scratch_shapes=[
@@ -916,7 +903,7 @@
             pltpu.VMEM((2, rows, model), jnp.bfloat16),
             pltpu.VMEM((2, rows, units), jnp.bfloat16),
             pltpu.VMEM((2, rows, units), jnp.bfloat16),
-            pltpu.SemaphoreType.DMA((2 * up.shape[0] * PIECES,)),
+            pltpu.SemaphoreType.DMA((2 * both.shape[0] * PIECES,)),
             pltpu.SemaphoreType.DMA((2 * PIECES,)),
             pltpu.SemaphoreType.DMA((2, 4)),
         ],
@@ -925,7 +912,7 @@
             flops=8 * PIECES * rows * model * units, bytes_accessed=36 * 2**20, transcendentals=0
         ),
         name="feed_forward",
-    )(ids, *rows_in, *grads_in, up, down)
+    )(ids, *rows_in, *grads_in, both)
     return out[0:4], out[4:8], out[8], out[9]
 
 
@@ -1130,9 +1117,12 @@
         scores = narrow(scores)
         dq_out[:, lanes] = narrow(dot_nn(scores, keys) * SCALE)
         dk = dot_tn(scores, query)
-        dkv_out[:, lanes] = narrow(jnp.where(dims_low, dk[:slots], dk[slots:]))
+        strips = width // (2 * HD)
+        low_lanes = lanes_of(at % strips, 2 * HD)
+        dkv_out[at // strips, :, low_lanes] = narrow(jnp.where(dims_low, dk[:slots], dk[slots:]))
         dv = dot_tn(narrow(weight), grad)
-        dkv_out[:, value_lanes] = narrow(jnp.where(dims_low, dv[:slots], dv[slots:]))
+        high_lanes = lanes_of(at % strips + strips, 2 * HD)
+        dkv_out[at // strips, :, high_lanes] = narrow(jnp.where(dims_low, dv[:slots], dv[slots:]))
         return carry
 
     lax.fori_loop(0, model // (2 * HD), one_pair, 0)
@@ -1158,7 +1148,7 @@
         like((rows, model)),
         like((rows, model)),
         like((rows, model)),
-        like((slots, 2 * model)),
+        like((pieces[0].shape[0], slots, 2 * model // pieces[0].shape[0])),
         like((4, model), jnp.float32),
     ]
     vmem = pl.BlockSpec(memory_space=pltpu.VMEM)
@@ -1293,12 +1283,17 @@
     tokens,
     split,
     norm,
+    cross,
     clip_out,
     rows_own,
     rows_c,
     rows_x,
     rows_xc,
     weights,
+    cross_near_out,
+    cross_x_out,
+    cross_near,
+    cross_x,
     held,
     clip,
     normed,
@@ -1314,6 +1309,8 @@
     c_local,
     row_sem,
     out_sem,
+    cross_ring_sem,
+    cross_x_sem,
 ):
     at_y, at_x, at_c, at_z = where_am_i()
     rows = split.shape[1]
@@ -1349,6 +1346,25 @@
             y_side,
         )
 
+    def cross_send(step):
+        source = cross_near.at[step]
+        copies = [
+            send_to(
+                source, cross_x.at[step], cross_x_sem.at[0, step], cross_x_sem.at[1, step], x_side
+            )
+        ]
+        if step < size - 1:
+            copies.append(
+                send_to(
+                    source,
+                    cross_near.at[step + 1],
+                    cross_ring_sem.at[0, step],
+                    cross_ring_sem.at[1, step],
+                    z_next,
+                )
+            )
+        return copies
+
     def settle(step, other_y, side):
         target = weights.at[
             step % half, block_rows((at_y + other_y) % 2, (at_x + side) % 2, at_c, rows)
@@ -1370,6 +1386,8 @@
         def _():
             remote.start()
 
+    cross_own = pltpu.make_async_copy(cross, cross_near.at[0], out_sem.at[3])
+    cross_own.start()
     for side in range(2):
         if side == 0:
             first.wait()
@@ -1378,42 +1396,69 @@
         ring(0, side).start()
         across(0, side).start()
         settle_start(0, 0, side)
-    for step in range(1, size):
-        if step == size - 1:
-            for copy in frames:
-                if copy is frames[0]:
-                    copy.wait()
-                else:
-                    copy.wait_recv()
-            keep = pltpu.make_async_copy(clip, clip_out, out_sem.at[1])
-            keep.start()
-            gain, bias = norm[0:1, :], norm[1:2, :]
-
-            def one_block(at, carry):
-                here = pl.ds(pl.multiple_of(at * clip.shape[1], clip.shape[1]), clip.shape[1])
-                normed[here, :] = narrow(layer_norm(wide(clip[at]), gain, bias)[0])
-                return carry
-
-            lax.fori_loop(0, clip.shape[0], one_block, 0)
-            own = pltpu.make_async_copy(normed, rows_own, out_sem.at[2])
-            to_x = send_to(normed, rows_x, row_sem.at[0], row_sem.at[1], x_side)
-            to_c = send_to(normed, rows_c, row_sem.at[2], row_sem.at[3], c_side)
-            to_x.start()
-            to_c.start()
-            own.start()
+    cross_own.wait()
+
+    def ring_step(step):
         for side in range(2):
             ring(step - 1, side).wait_recv()
             if step < size - 1:
                 ring(step, side).start()
             across(step, side).start()
             settle_start(step, 0, side)
+
+    def cross_step(step):
+        if step:
+            cross_send(step - 1)[1].wait_recv()
+        for copy in cross_send(step):
+            copy.start()
+
+    ring_step(1)
+    for copy in frames:
+        if copy is frames[0]:
+            copy.wait()
+        else:
+            copy.wait_recv()
+    keep = pltpu.make_async_copy(clip, clip_out, out_sem.at[1])
+    keep.start()
+    gain, bias = norm[0:1, :], norm[1:2, :]
+
+    def one_block(at, carry):
+        here = pl.ds(pl.multiple_of(at * clip.shape[1], clip.shape[1]), clip.shape[1])
+        normed[here, :] = narrow(layer_norm(wide(clip[at]), gain, bias)[0])
+        return carry
+
+    lax.fori_loop(0, clip.shape[0], one_block, 0)
+    own = pltpu.make_async_copy(normed, rows_own, out_sem.at[2])
+    to_x = send_to(normed, rows_x, row_sem.at[0], row_sem.at[1], x_side)
+    to_c = send_to(normed, rows_c, row_sem.at[2], row_sem.at[3], c_side)
+    to_x.start()
+    to_c.start()
+    own.start()
+    ring_step(2)
+    ring_step(3)
+    cross_step(0)
     for step in range(size):
         for side in range(2):
             across(step, side).wait_recv()
             settle_start(step, 1, side)
+        if step:
+            cross_step(step)
     to_x.wait_recv()
     relay = send_to(rows_x, rows_xc, row_sem.at[4], row_sem.at[5], c_side)
     relay.start()
+    for step in range(size):
+        copies = cross_send(step)
+        copies[0].wait()
+        if step < size - 1:
+            copies[1].wait_send()
+    cross_outs = [
+        pltpu.make_async_copy(cross_near, cross_near_out, out_sem.at[3]),
+        pltpu.make_async_copy(cross_x, cross_x_out, out_sem.at[4]),
+    ]
+    for copy in cross_outs:
+        copy.start()
+    for copy in cross_outs:
+        copy.wait()
     for step in range(half):
         for other_y in range(2):
             for side in range(2):
@@ -1435,7 +1480,7 @@
                 ring(step, side).wait_send()
 
 
-def start_up(tokens, split, norm):
+def start_up(tokens, split, norm, cross):
     size = lax.axis_size("z")
     groups, frames, model = tokens.shape
     rows, units = split.shape[1:]
@@ -1444,12 +1489,15 @@
     dma = pltpu.SemaphoreType.DMA
     out = pl.pallas_call(
         functools.partial(start_kernel, size),
-        in_specs=[vmem] * 3,
-        out_specs=[ANYWHERE] * 6,
+        in_specs=[vmem] * 4,
+        out_specs=[ANYWHERE] * 8,
         out_shape=[like(tokens.shape)]
         + [like((groups * frames, model))] * PIECES
-        + [like((half, 8 * rows, units))],
+        + [like((half, 8 * rows, units))]
+        + [like((size,) + cross.shape)] * 2,
         scratch_shapes=[
+            pltpu.VMEM((size,) + cross.shape, jnp.bfloat16),
+            pltpu.VMEM((size,) + cross.shape, jnp.bfloat16),
             pltpu.VMEM((size, 2, 2, rows, units), jnp.bfloat16),
             pltpu.VMEM(tokens.shape, jnp.bfloat16),
             pltpu.VMEM((groups * frames, model), jnp.bfloat16),
@@ -1464,7 +1512,9 @@
             dma((half, 2, 2)),
             dma((half, 2, 2)),
             dma((6,)),
-            dma((3,)),
+            dma((5,)),
+            dma((2, size - 1)),
+            dma((2, size)),
         ],
         compiler_params=pltpu.CompilerParams(
             collective_id=1, has_side_effects=True, vmem_limit_bytes=32 * 2**20
@@ -1473,8 +1523,165 @@
             flops=10**7, bytes_accessed=200 * 2**20, transcendentals=0
         ),
         name="start_up",
-    )(tokens, split, norm)
-    return out[0].reshape(-1, model), out[1:5], out[5]
+    )(tokens, split, norm, cross)
+    return out[0].reshape(-1, model), out[1:5], out[5], out[6:8]
+
+
+def middle_kernel(
+    size,
+    part_own,
+    part_c,
+    part_x,
+    part_xc,
+    near,
+    side,
+    text,
+    cot,
+    term_c,
+    term_x,
+    near_y,
+    side_y,
+    near_c,
+    side_c,
+    near_yc,
+    side_yc,
+    text_out,
+    cot_c,
+    cot_x,
+    cot_xc,
+    text_parts,
+    far_held,
+    far_sum,
+    text_held,
+    text_sum,
+    core_sem,
+    x_sem,
+    y_sem,
+    c_sem,
+    text_sem,
+    out_sem,
+    text_send,
+    text_recv,
+    cot_sem,
+):
+    at_y, at_x, at_c, at_z = where_am_i()
+    x_side = (at_y, 1 - at_x, at_c, at_z)
+    y_side = (1 - at_y, at_x, at_c, at_z)
+    c_side = (at_y, at_x, 1 - at_c, at_z)
+    meet(size)
+    exchange = exchange_copies(text, text_parts, size, text_send, text_recv)
+
+    def swap(source, target, sem, at, device):
+        return send_to(source, target, sem.at[0, at], sem.at[1, at], device)
+
+    core_far = swap(part_xc, far_held, core_sem, 0, c_side)
+    core_near = swap(part_c, term_c, core_sem, 1, c_side)
+    y_near = swap(near, near_y, y_sem, 0, y_side)
+    y_side_copy = swap(side, side_y, y_sem, 1, y_side)
+    text_c = swap(text_sum.at[0], text_held.at[0], text_sem, 0, c_side)
+    text_x = swap(text_sum.at[1], text_held.at[1], text_sem, 1, x_side)
+    cots = [
+        swap(cot, cot_c, cot_sem, 0, c_side),
+        swap(cot, cot_x, cot_sem, 1, x_side),
+        swap(cot_x, cot_xc, cot_sem, 2, c_side),
+    ]
+    core_far.start()
+    for copy in exchange:
+        copy.start()
+    y_near.start()
+    core_far.wait_recv()
+    rows = 48
+
+    def add_far(at, carry):
+        here = pl.ds(pl.multiple_of(at * rows, rows), rows)
+        far_sum[here, :] = narrow(wide(part_x[here, :]) + wide(far_held[here, :]))
+        return carry
+
+    lax.fori_loop(0, part_x.shape[0] // rows, add_far, 0)
+    over = swap(far_sum, term_x, x_sem, 0, x_side)
+    over.start()
+    core_near.start()
+    y_side_copy.start()
+    pieces_c = [swap(near, near_c, c_sem, 0, c_side), swap(side, side_c, c_sem, 1, c_side)]
+    for copy in pieces_c:
+        copy.start()
+    cots[0].start()
+    for copy in exchange:
+        if copy is exchange[0]:
+            copy.wait()
+        else:
+            copy.wait_recv()
+    text_sum[0] = narrow(wide(text_parts[:size]) + wide(text_parts[size:]))
+    text_c.start()
+    text_c.wait_recv()
+    text_sum[1] = narrow(wide(text_sum[0]) + wide(text_held[0]))
+    text_x.start()
+    over.wait_recv()
+    cots[1].start()
+    y_near.wait_recv()
+    more = [swap(near_y, near_yc, c_sem, 2, c_side)]
+    more[0].start()
+    text_x.wait_recv()
+    text_sum[2] = narrow(wide(text_sum[1]) + wide(text_held[1]))
+    last = pltpu.make_async_copy(text_sum.at[2], text_out, out_sem.at[0])
+    last.start()
+    y_side_copy.wait_recv()
+    more.append(swap(side_y, side_yc, c_sem, 3, c_side))
+    more[1].start()
+    cots[1].wait_recv()
+    cots[2].start()
+    last.wait()
+    for copy in pieces_c + more:
+        copy.wait()
+    core_near.wait()
+    over.wait_send()
+    cots[0].wait()
+    cots[1].wait_send()
+    cots[2].wait()
+    for copy in exchange[1:]:
+        copy.wait_send()
+    for copy in (core_far, y_near, y_side_copy, text_c, text_x):
+        copy.wait_send()
+
+
+def middle(parts, near, side, text, cot):
+    size = lax.axis_size("z")
+    vmem = pl.BlockSpec(memory_space=pltpu.VMEM)
+    dma = pltpu.SemaphoreType.DMA
+    rows = like(parts[0].shape)
+    piece = like(near.shape)
+    out = pl.pallas_call(
+        functools.partial(middle_kernel, size),
+        in_specs=[vmem] * 8,
+        out_specs=[ANYWHERE] * 12,
+        out_shape=[rows, rows] + [piece] * 6 + [like((size,) + text.shape[1:])] + [rows] * 3,
+        scratch_shapes=[
+            pltpu.VMEM(text.shape, jnp.bfloat16),
+            pltpu.VMEM(rows.shape, jnp.bfloat16),
+            pltpu.VMEM(rows.shape, jnp.bfloat16),
+            pltpu.VMEM((2, size) + text.shape[1:], jnp.bfloat16),
+            pltpu.VMEM((3, size) + text.shape[1:], jnp.bfloat16),
+            dma((2, 2)),
+            dma((2, 1)),
+            dma((2, 2)),
+            dma((2, 4)),
+            dma((2, 2)),
+            dma((1,)),
+            dma((2 * size,)),
+            dma((2 * size,)),
+            dma((2, 3)),
+        ],
+        compiler_params=pltpu.CompilerParams(
+            collective_id=3, has_side_effects=True, vmem_limit_bytes=40 * 2**20
+        ),
+        cost_estimate=pl.CostEstimate(
+            flops=10**7, bytes_accessed=100 * 2**20, transcendentals=0
+        ),
+        name="middle",
+    )(*parts, near, side, text, cot)
+    near_y, side_y, near_c, side_c, near_yc, side_yc = out[2:8]
+    pieces = [near, near_y, side, side_y, near_c, near_yc, side_c, side_yc]
+    return [parts[0], out[0], out[1]], pieces, out[8], [cot] + list(out[9:])
 
 
 def end_kernel(
@@ -1489,10 +1696,17 @@
     clip,
     norm,
     norm_in,
+    cross,
+    text,
+    text_rows,
+    text_weights,
     grad_out,
     norm_out,
     unit_own,
     unit_x,
+    cross_out,
+    text_out,
+    memory_out,
     y_held,
     folded,
     both,
@@ -1520,6 +1734,20 @@
     hop_recv,
     unit_sem,
     out_sem,
+    cross_held,
+    cross_moved,
+    cross_final,
+    cross_sem,
+    text_held,
+    text_sum,
+    text_sem,
+    text_final,
+    memory_part,
+    memory_held,
+    memory_all,
+    memory_sem,
+    all_send,
+    all_recv,
 ):
     at_y, at_x, at_c, at_z = where_am_i()
     x_side = (at_y, 1 - at_x, at_c, at_z)
@@ -1541,26 +1769,91 @@
     places = [(at, side) for at in range(half) for side in range(2)]
     core_far = send_to(part_xc, core_held.at[1], core_sem.at[0], core_sem.at[1], c_side)
     core_near = send_to(part_c, core_held.at[0], core_sem.at[2], core_sem.at[3], c_side)
-    core_far.start()
-    for core in (1, 0):
-        for at, side in places:
-            across(core, at, side).start()
-    core_near.start()
-    frames = clip.shape[1]
-
-    def rows_of(at):
-        return pl.ds(pl.multiple_of(at * frames, frames), frames)
-
-    core_far.wait_recv()
-
-    def add_far(at, carry):
-        here = rows_of(at)
-        x_moved[here, :] = narrow(wide(part_x[here, :]) + wide(core_held[1, here, :]))
-        return carry
-
-    lax.fori_loop(0, clip.shape[0], add_far, 0)
-    over = send_to(x_moved, x_held, x_sem.at[0], x_sem.at[1], x_side)
-    over.start()
+    z_sides = []
+    for bit in (1, 2):
+        low = at_z % 2
+        other = (at_z + 1 - 2 * low) if bit == 1 else (at_z + 2) % size
+        z_sides.append((at_y, at_x, at_c, other))
+
+    def cross_ring(step):
+        return send_to(
+            cross.at[1] if step == 0 else cross_moved.at[step - 1],
+            cross_held.at[step],
+            cross_sem.at[0, step],
+            cross_sem.at[1, step],
+            z_next,
+        )
+
+    def cross_next(step):
+        cross_ring(step - 1).wait_recv()
+        total = wide(cross_held[step - 1]) + wide(cross[(step + 1) % size])
+        if step < size - 1:
+            cross_moved[step - 1] = narrow(total)
+            cross_ring(step).start()
+        else:
+            cross_final[...] = total
+
+    text_c = send_to(text, text_held.at[0], text_sem.at[0], text_sem.at[1], c_side)
+    text_x = send_to(text_sum.at[0], text_held.at[1], text_sem.at[2], text_sem.at[3], x_side)
+
+    def memory_hop(number):
+        return send_to(
+            memory_part.at[number],
+            memory_held.at[number],
+            memory_sem.at[0, number],
+            memory_sem.at[1, number],
+            z_sides[number],
+        )
+
+    def block_at(near_y, near_x, near_c):
+        return (((at_y + near_y) % 2) * 2 + (at_x + near_x) % 2) * 2 + (at_c + near_c) % 2
+
+    def memory_copies(stage):
+        if stage == 0:
+            blocks, device = [block_at(0, 0, 0)], y_side
+        elif stage == 1:
+            blocks, device = [block_at(i, 0, 0) for i in range(2)], x_side
+        else:
+            blocks, device = [block_at(i // 2, i % 2, 0) for i in range(4)], c_side
+        return [
+            send_to(
+                memory_all.at[block],
+                memory_all.at[block],
+                all_send.at[stage, i],
+                all_recv.at[stage, i],
+                device,
+            )
+            for i, block in enumerate(blocks)
+        ]
+
+    def text_step(step):
+        if step == 0:
+            text_c.wait_recv()
+            text_sum[0] = narrow(wide(text[...]) + wide(text_held[0]))
+            text_x.start()
+        elif step == 2:
+            text_x.wait_recv()
+            text_sum[1] = narrow(wide(text_sum[0]) + wide(text_held[1]))
+            whole = text_sum[1].reshape(-1, text.shape[2])
+            text_final[...] = dot_tn(text_rows[...], whole)
+            memory_part[0] = narrow(dot_nt(text_weights[...], whole))
+            memory_hop(0).start()
+        elif step == 3:
+            memory_hop(0).wait_recv()
+            memory_part[1] = narrow(wide(memory_part[0]) + wide(memory_held[0]))
+            memory_hop(1).start()
+        elif step == 4:
+            memory_hop(1).wait_recv()
+            memory_all[block_at(0, 0, 0)] = narrow(wide(memory_part[1]) + wide(memory_held[1]))
+            memory_copies(0)[0].start()
+        elif step < 7:
+            for copy in memory_copies(step - 5):
+                copy.wait_recv()
+            for copy in memory_copies(step - 4):
+                copy.start()
+        else:
+            for copy in memory_copies(2):
+                copy.wait_recv()
 
     def to_core(at, side):
         return send_to(
@@ -1571,55 +1864,12 @@
             c_side,
         )
 
-    for at, side in places:
+    def fold(at, side):
         across(1, at, side).wait_recv()
         folded[at, side] = narrow(wide(near[1, at, side]) + wide(y_held[1, at, side]))
         to_core(at, side).start()
-    core_near.wait_recv()
-    over.wait_recv()
-    sums[...] = jnp.zeros_like(sums)
-    sums[2:6, :] = norm_in[...]
-    gain, bias = norm[0:1, :], norm[1:2, :]
-
-    def one_block(at, carry):
-        here = rows_of(at)
-        change = wide(part_own[here, :]) + wide(core_held[0, here, :]) + wide(x_held[here, :])
-        back, gain_g, bias_g = norm_gradient(change, wide(clip[at]), gain, bias)
-        grads[at] = narrow(upstream[here, :] + back)
-        sums[0:1, :] += gain_g
-        sums[1:2, :] += bias_g
-        return carry
-
-    lax.fori_loop(0, clip.shape[0], one_block, 0)
-    exchange = exchange_copies(grads, grads_held, size, clip_send, clip_recv)
-    for copy in exchange:
-        copy.start()
-    hops = [c_side, x_side, y_side]
-    for bit in (1, 2):
-        low = at_z % 2
-        other = (at_z + 1 - 2 * low) if bit == 1 else (at_z + 2) % size
-        hops.append((at_y, at_x, at_c, other))
-
-    def hop(number):
-        source = sums if number == 0 else sums_held.at[1, number - 1]
-        return send_to(
-            source, sums_held.at[0, number], hop_send.at[number], hop_recv.at[number], hops[number]
-        )
-
-    def hop_next(number):
-        hop(number).wait_recv()
-        source = sums[...] if number == 0 else sums_held[1, number - 1]
-        sums_held[1, number] = source + sums_held[0, number]
-        if number + 1 < len(hops):
-            hop(number + 1).start()
-
-    hop(0).start()
-    hop_next(0)
-    for at, side in places:
         across(0, at, side).wait_recv()
         both[0, at, side] = narrow(wide(near[0, at, side]) + wide(y_held[0, at, side]))
-    hop_next(1)
-    for at, side in places:
         to_core(at, side).wait_recv()
 
     def chunk(step):
@@ -1635,22 +1885,105 @@
             z_next,
         )
 
-    for side in range(2):
-        ring(0, side).start()
-    hop_next(2)
-    for step in range(1, size):
+    def ring_next(step, side):
         which, at = chunk((step + 1) % size)
-        for side in range(2):
-            ring(step - 1, side).wait_recv()
-            moved[step - 1, side] = narrow(
-                wide(ring_held[step - 1, side]) + wide(both[which, at, side])
-            )
-            if step < size - 1:
-                ring(step, side).start()
+        ring(step - 1, side).wait_recv()
+        moved[step - 1, side] = narrow(
+            wide(ring_held[step - 1, side]) + wide(both[which, at, side])
+        )
         if step < size - 1:
-            hop_next(2 + step)
+            ring(step, side).start()
+
+    core_far.start()
+    def across_start(side):
+        for at in range(half - 1, -1, -1):
+            for core in (1, 0):
+                across(core, at, side).start()
+
+    across_start(1)
+    across_start(0)
+    cross_ring(0).start()
+    core_near.start()
+    frames = clip.shape[1]
+
+    def rows_of(at):
+        return pl.ds(pl.multiple_of(at * frames, frames), frames)
+
+    core_far.wait_recv()
+
+    def add_far(at, carry):
+        here = rows_of(at)
+        x_moved[here, :] = narrow(wide(part_x[here, :]) + wide(core_held[1, here, :]))
+        return carry
+
+    lax.fori_loop(0, clip.shape[0], add_far, 0)
+    over = send_to(x_moved, x_held, x_sem.at[0], x_sem.at[1], x_side)
+    over.start()
+    text_c.start()
+    fold(1, 1)
+    ring(0, 1).start()
+    cross_next(1)
+    fold(0, 1)
+    ring_next(1, 1)
+    cross_next(2)
+    text_step(0)
+    fold(1, 0)
+    ring(0, 0).start()
+    ring_next(2, 1)
+    cross_next(3)
+    core_near.wait_recv()
+    over.wait_recv()
+    sums[...] = jnp.zeros_like(sums)
+    sums[2:6, :] = norm_in[...]
+    gain, bias = norm[0:1, :], norm[1:2, :]
+
+    def one_block(at, carry):
+        here = rows_of(at)
+        change = wide(part_own[here, :]) + wide(core_held[0, here, :]) + wide(x_held[here, :])
+        back, gain_g, bias_g = norm_gradient(change, wide(clip[at]), gain, bias)
+        grads[at] = narrow(upstream[here, :] + back)
+        sums[0:1, :] += gain_g
+        sums[1:2, :] += bias_g
+        return carry
+
+    lax.fori_loop(0, clip.shape[0], one_block, 0)
+    exchange = exchange_copies(grads, grads_held, size, clip_send, clip_recv)
+    for copy in exchange:
+        copy.start()
+    hops = [c_side, x_side, y_side] + z_sides
+
+    def hop(number):
+        source = sums if number == 0 else sums_held.at[1, number - 1]
+        return send_to(
+            source, sums_held.at[0, number], hop_send.at[number], hop_recv.at[number], hops[number]
+        )
+
+    def hop_next(number):
+        hop(number).wait_recv()
+        source = sums[...] if number == 0 else sums_held[1, number - 1]
+        sums_held[1, number] = source + sums_held[0, number]
+        if number + 1 < len(hops):
+            hop(number + 1).start()
+
+    hop(0).start()
+    ring_next(3, 1)
     last = send_to(moved.at[size - 2, 1], unit_held, unit_sem.at[0], unit_sem.at[1], x_side)
     last.start()
+    text_step(2)
+    fold(0, 0)
+    text_step(3)
+    ring_next(1, 0)
+    text_step(4)
+    hop_next(0)
+    hop_next(1)
+    text_step(5)
+    ring_next(2, 0)
+    hop_next(2)
+    text_step(6)
+    ring_next(3, 0)
+    hop_next(3)
+    text_step(7)
+    hop_next(4)
     for copy in exchange:
         if copy is exchange[0]:
             copy.wait()
@@ -1660,6 +1993,9 @@
         pltpu.make_async_copy(grads_held, grad_out, out_sem.at[0]),
         pltpu.make_async_copy(moved.at[size - 2, 0], unit_own, out_sem.at[1]),
         pltpu.make_async_copy(sums_held.at[1, len(hops) - 1], norm_out, out_sem.at[2]),
+        pltpu.make_async_copy(cross_final, cross_out, out_sem.at[4]),
+        pltpu.make_async_copy(text_final, text_out, out_sem.at[5]),
+        pltpu.make_async_copy(memory_all, memory_out, out_sem.at[6]),
     ]
     for copy in outs:
         copy.start()
@@ -1684,9 +2020,18 @@
         copy.wait_send()
     for number in range(len(hops)):
         hop(number).wait_send()
-
-
-def end(far, near, parts, upstream, clip, norm, norm_in):
+    for step in range(size - 1):
+        cross_ring(step).wait_send()
+    text_c.wait_send()
+    text_x.wait_send()
+    for number in range(2):
+        memory_hop(number).wait_send()
+    for stage in range(3):
+        for copy in memory_copies(stage):
+            copy.wait_send()
+
+
+def end(far, near, parts, upstream, clip, norm, norm_in, cross, text, text_rows, text_weights):
     size = lax.axis_size("z")
     half = size // 2
     groups, frames, model = clip.shape
@@ -1699,13 +2044,16 @@
 
     return pl.pallas_call(
         functools.partial(end_kernel, size),
-        in_specs=[vmem] * 10,
-        out_specs=[ANYWHERE] * 4,
+        in_specs=[vmem] * 14,
+        out_specs=[ANYWHERE] * 7,
         out_shape=[
             like(clip.shape),
             like((8, model), jnp.float32),
             like((rows, units)),
             like((rows, units)),
+            like(cross.shape[1:], jnp.float32),
+            like((text_rows.shape[1], text.shape[2]), jnp.float32),
+            like((8, text_weights.shape[0], text_rows.shape[0])),
         ],
         scratch_shapes=[
             buffer(2, half, 2, rows, units),
@@ -1734,7 +2082,21 @@
             dma((5,)),
             dma((5,)),
             dma((2,)),
+            dma((7,)),
+            buffer(size - 1, *cross.shape[1:]),
+            buffer(size - 2, *cross.shape[1:]),
+            buffer(*cross.shape[1:], dtype=jnp.float32),
+            dma((2, size - 1)),
+            buffer(2, *text.shape),
+            buffer(2, *text.shape),
             dma((4,)),
+            buffer(text_rows.shape[1], text.shape[2], dtype=jnp.float32),
+            buffer(2, text_weights.shape[0], text_rows.shape[0]),
+            buffer(2, text_weights.shape[0], text_rows.shape[0]),
+            buffer(8, text_weights.shape[0], text_rows.shape[0]),
+            dma((2, 2)),
+            dma((3, 4)),
+            dma((3, 4)),
         ],
         compiler_params=pltpu.CompilerParams(
             collective_id=2, has_side_effects=True, vmem_limit_bytes=56 * 2**20
@@ -1743,7 +2105,19 @@
             flops=10**7, bytes_accessed=300 * 2**20, transcendentals=0
         ),
         name="end",
-    )(far, near, *parts, upstream, clip, norm, norm_in)
+    )(
+        far,
+        near,
+        *parts,
+        upstream,
+        clip,
+        norm,
+        norm_in,
+        cross,
+        text,
+        text_rows,
+        text_weights,
+    )
 
 
 def clip_body(
@@ -1776,55 +2150,45 @@
     size = lax.axis_size("z")
     frame_block = tokens.shape[2]
 
+    both = gather_units([w_up, w_down.T])
     split = split_heads([w_query, w_key, w_value, w_out.T])
     norm_one = jnp.stack([gain_one, bias_one])
-    clip_tokens, rows_one, attend_weights = start_up(
-        tokens.reshape(-1, frame_block, model), split, norm_one
-    )
-    cross_pieces = gather_whole(jnp.concatenate([c_query, c_out.T], axis=1), clip_tokens)
+    at_f = block_of(at_y, at_x, at_c)
+    text_mine = lax.dynamic_slice_in_dim(
+        memory.reshape(-1, model), at_f * shard_rows, shard_rows, 1
+    )
+    text_shard = jnp.concatenate([c_key, c_value], axis=1)
+    text_part = narrow(dot_nn(text_mine, text_shard)).reshape(-1, slots, 2 * shard_width)
+    clip_tokens, rows_one, attend_weights, cross_pieces = start_up(
+        tokens.reshape(-1, frame_block, model),
+        split,
+        norm_one,
+        jnp.concatenate([c_query, c_out.T], axis=1),
+    )
+    near, side = cross_pieces
     upstream = after(cotangent.reshape(-1, frame_block, model), clip_tokens)
     upstream = exchange_clips(upstream).reshape(-1, model)
-    up_full = gather_units(w_up, clip_tokens)
-    down_full = gather_units(w_down.T, clip_tokens)
-    grad_rows3 = group_rows(upstream)
-
-    at_f = block_of(at_y, at_x, at_c)
-    text_flat = memory.reshape(-1, model)
-    text_mine = lax.dynamic_slice_in_dim(text_flat, at_f * shard_rows, shard_rows, 1)
-    text_shard = jnp.concatenate([c_key, c_value], axis=1)
-    text_part = narrow(dot_nn(text_mine, text_shard)).reshape(2, -1, slots, 2 * shard_width)
-    got = wide(pair_swap(take(text_part, 1 - at_y), "y"))
-    text_part = narrow(wide(take(text_part, at_y)) + got)
-    text_clip = text_part
-    for distance in range(1, size):
-        piece = ring_shift(take(text_part, lax.rem(at_z + distance, size)), distance)
-        text_clip = place(text_clip, piece, lax.rem(at_z + size - distance, size))
-    for name in ("x", "c"):
-        text_clip = narrow(wide(text_clip) + wide(pair_swap(text_clip, name)))
+    count = take(take(text_len, at_y), at_z).reshape(1)
+    norms = jnp.stack([gain_two, bias_two, gain_three, bias_three])
+
+    self_parts, qkv, mixed_one, log_total = attend_forward(ids, rows_one, attend_weights)
+    self_terms, cross_pieces, text_clip, grad_rows3 = middle(
+        self_parts, near, side, text_part, upstream
+    )
     text_clip = text_clip.reshape(size, slots, 2, shard_width)
     keys_values = jnp.transpose(text_clip, (1, 2, 0, 3)).reshape(slots, -1)
-    count = take(take(text_len, at_y), at_z).reshape(1)
-    norms = jnp.stack([gain_two, bias_two, gain_three, bias_three])
-
-    self_parts, qkv, mixed_one, log_total = attend_forward(ids, rows_one, attend_weights)
     after_self, rows_two, cross_q, mixed_two, after_cross, own_three = cross_forward(
-        ids, count, clip_tokens, group_terms(self_parts), norms, keys_values, cross_pieces
+        ids, count, clip_tokens, self_terms, norms, keys_values, cross_pieces
     )
     rows_three = group_rows(own_three)
 
     feed_parts, back_parts, active, grad_hidden = feed(
-        ids, rows_three, grad_rows3, up_full, down_full
+        ids, rows_three, grad_rows3, both
     )
     back_terms = group_terms(back_parts)
     part_down = feed_grads(ids, grad_rows3, active)
     part_up = feed_grads(ids, rows_three, grad_hidden)
-    fin_down, fin_up = sum_units(part_down), sum_units(part_up)
-    feed_terms = group_terms(feed_parts)
-    result = after_cross + wide(feed_terms[0]) + wide(feed_terms[1]) + wide(feed_terms[2])
-    result = narrow(result)
-    own_result = result
-    result = exchange_clips(result.reshape(-1, frame_block, model)).reshape(tokens.shape)
-
+    sum_down, sum_up = scatter_units(part_down), scatter_units(part_up)
     grad_one_rows, own_one, own_two, grad_cq, grad_text, norm_grads = cross_backward(
         ids,
         count,
@@ -1839,49 +2203,45 @@
     )
     grad_rows1 = group_rows(own_one)
     cross_keep, cross_send = cross_grads(ids, rows_two, grad_cq, own_two, mixed_two)
-    fin_cross = sum_whole(cross_keep, cross_send)
-    fin_cquery, fin_cout = fin_cross[:, :shard_width], fin_cross[:, shard_width:].T
-
-    grad_text = grad_text.reshape(slots, 2, size, shard_width)
-    grad_text = jnp.transpose(grad_text, (2, 0, 1, 3)).reshape(size, slots, 2 * shard_width)
-    for name in ("x", "c"):
-        grad_text = narrow(wide(grad_text) + wide(pair_swap(grad_text, name)))
-    spread = grad_text
-    for distance in range(1, size):
-        piece = ring_shift(take(grad_text, lax.rem(at_z + distance, size)), distance)
-        spread = place(spread, piece, lax.rem(at_z + size - distance, size))
-    spread = ordered(at_y, spread, pair_swap(spread, "y")).reshape(-1, 2 * shard_width)
-    fin_text = dot_tn(text_mine, spread)
-    fin_ckey, fin_cvalue = fin_text[:, :shard_width], fin_text[:, shard_width:]
-    grad_memory = narrow(dot_nt(spread, text_shard))
-    bit = 1
-    while bit < size:
-        grad_memory = narrow(wide(grad_memory) + wide(ring_flip(grad_memory, bit)))
-        bit *= 2
-    for at, name in ((at_c, "c"), (at_x, "x"), (at_y, "y")):
-        grad_memory = ordered(at, grad_memory, pair_swap(grad_memory, name))
-    grad_memory = jnp.transpose(grad_memory.reshape(8, -1, shard_rows), (1, 0, 2))
-    grad_memory = wide(grad_memory.reshape(memory.shape))
-
+    cross_sum = sum_plane(cross_keep, cross_send, grad_rows1)
+    grad_text = exchange_clips(jnp.concatenate([grad_text, grad_text]))
+
+    feed_terms = group_terms(after(feed_parts, grad_rows1))
     self_back, grad_qkv = attend_backward(
-        after(ids, cross_keep, part_up, part_down, own_result),
+        after(ids, cross_keep, part_up, part_down),
         grad_rows1,
         attend_weights,
         qkv,
         mixed_one,
         log_total,
     )
+    feed_terms = after(feed_terms, self_back)
+    result = after_cross + wide(feed_terms[0]) + wide(feed_terms[1]) + wide(feed_terms[2])
+    result = narrow(result)
+    result = after(result.reshape(-1, frame_block, model), grad_text)
+    result = exchange_clips(result).reshape(tokens.shape)
+
+    cross_part = sum_plane_rest(*after(cross_sum, self_back))
     far = attend_grads(ids, rows_one, grad_rows1, grad_qkv, mixed_one, 1)
     near = attend_grads(ids, rows_one, grad_rows1, grad_qkv, mixed_one, 0)
-    input_grad, norm_grads, unit_own, unit_away = end(
-        far,
+    input_grad, norm_grads, unit_own, unit_away, fin_cross, fin_text, grad_memory = end(
+        after(far, result),
         near,
         self_back,
         grad_one_rows,
         clip_tokens.reshape(-1, frame_block, model),
         norm_one,
         norm_grads,
-    )
+        cross_part,
+        grad_text,
+        text_mine,
+        text_shard,
+    )
+    fin_down = join_units(after(sum_down, input_grad)).T
+    fin_up = join_units(after(sum_up, input_grad))
+    fin_cquery, fin_cout = fin_cross[:, :shard_width], fin_cross[:, shard_width:].T
+    fin_ckey, fin_cvalue = fin_text[:, :shard_width], fin_text[:, shard_width:]
+    grad_memory = wide(grad_memory.reshape(model, -1).T).reshape(memory.shape)
     input_grad = wide(input_grad).reshape(tokens.shape)
     fin_query, fin_key, fin_value, fin_out = join_heads(unit_own, unit_away)
 
@@ -1904,7 +2264,7 @@
         fin_cvalue,
         fin_cout,
         fin_up,
-        fin_down.T,
+        fin_down,
     )
 
 

time: 918 us -> 907 us (0.988)
  Pallas kernels: 452 us -> 573 us
  waiting for transfers between devices: 231 us -> 144 us
  starting transfers between devices: 64.2 us -> 39 us
  other arithmetic: 55.5 us -> 37.5 us
    pallas_call x3 -> x4, Pallas kernels: 259 us -> 381 us  [the longest x1 145 us: start_up(): pl.pallas_call(functools.partial(start_kernel, size), in_specs=[vmem] * 4...]
    ppermute x14 -> x0, waiting for transfers between devices: 64.4 us -> none  [the longest x12 53.7 us: ring_shift(): lax.ppermute(values, 'z', [(i, (i + distance) % size) for i in range(size)])]
    ppermute x45 -> x21, waiting for transfers between devices: 166 us -> 123 us  [pair_swap(): return lax.ppermute(values, axis_name, [(0, 1), (1, 0)])]
    ppermute x14 -> x0, starting transfers between devices: 32.2 us -> none  [the longest x12 25.6 us: ring_shift(): lax.ppermute(values, 'z', [(i, (i + distance) % size) for i in range(size)])]
    all_to_all x2 -> x3, waiting for transfers between devices: 0.01 us -> 20.7 us  [exchange_clips(): return lax.all_to_all(values, ('y', 'z'), 0, 0, tiled=True)]
    unnamed x170 -> x209, local copies, waits for them, and re-layouts: 42.5 us -> 60.5 us
    all_to_all x2 -> x3, starting transfers between devices: 7.95 us -> 18.5 us  [exchange_clips(): return lax.all_to_all(values, ('y', 'z'), 0, 0, tiled=True)]
    convert_element_type x2 -> x0, local copies, waits for them, and re-layouts: 10.5 us -> none  [wide(): return values.astype(jnp.float32)]
  transfers between devices with their start and end apart: 65 -> 27, of which waited for: 25 -> 13; matrix products, arithmetic and copies ran while one was open for 10% -> 5% of each run, Pallas kernels for 45% -> 57%
where the time goes in v4:
time: 907 us; the launch traced here: 898 us
  Pallas kernels  573 us (63%)
  waiting for transfers between devices  144 us (16%)
  local copies, waits for them, and re-layouts  89.5 us (10%)
  starting transfers between devices  39 us (4%)
  other arithmetic  37.5 us (4%)
  between operations  15.2 us (2%)
    pallas_call x1, Pallas kernels, start_up(): pl.pallas_call(functools.partial(start_kernel, size), in_specs=[vmem] * 4...  145 us
    ppermute x21, waiting for transfers between devices, pair_swap(): return lax.ppermute(values, axis_name, [(0, 1), (1, 0)])  123 us
    pallas_call x1, Pallas kernels, end(): pl.pallas_call(functools.partial(end_kernel, size), in_specs=[vmem] * 14,...  122 us
    pallas_call x1, Pallas kernels, middle(): pl.pallas_call(functools.partial(middle_kernel, size), in_specs=[vmem] *...  70.5 us
    unnamed x209, local copies, waits for them, and re-layouts  60.5 us
    pallas_call x1, Pallas kernels, attend_backward(): pl.pallas_call(attend_backward_kernel, in_specs=[SCALARS] + [vmem] * (PIE...  49.2 us
    pallas_call x1, Pallas kernels, feed(): pl.pallas_call(feed_kernel, in_specs=[SCALARS] + [ANYWHERE] * 9, out_spec...  44.6 us
    pallas_call x1, Pallas kernels, attend_forward(): pl.pallas_call(attend_forward_kernel, in_specs=[SCALARS] + [pl.BlockSpec(...  37.8 us
  transfers between devices with their start and end apart: 27, of which 13 were waited for; matrix products, arithmetic and copies ran while one was open for 5% of the time, Pallas kernels for 57%

profile of v4, /device:TPU:0, one launch (start us, length us, event | category | flops | bytes accessed | tf_op | source)
XLA Modules:
  0.0 897.8 jit_solution(10173219123657288424)
XLA Ops:
  16.8 13.5 %collective-permute-done.3 = bf16[2,2,192,384]{3,0,2,1:T(2,128)(2,1)S(1)} collective-permute-done((bf16[2,2,192,384]{3,0,2,1:T(2,128)(2,1)}, bf16[2,2,192,384]{3,0,2,1:T(2,128)(2,1)S(1)}, u32[]{:S(2)}, u32[]{:S(2)}) %collective-permute-start.3) | collective-permute-done | bytes 589856 | tf_op jit(solution)/shard_map/ppermute | solution.py:401
  46.1 144.6 %start_up.1 = (bf16[8,48,1536]{2,1,0:T(8,128)(2,1)S(1)}, bf16[384,1536]{1,0:T(8,128)(2,1)S(1)}, bf16[384,1536]{1,0:T(8,128)(2,1)S(1)}, bf16[384,1536]{1,0:T(8,12...) custom-call(bf16[8,48,1536]{2,1,0:T(8,128)(2,1)S(1)} %bitcast.117, ...), custom_call_target="tpu_custom_call" | custom-call | flops 10000000 | bytes 209715200 | tf_op jit(solution)/shard_map/start_up/pallas_call | solution.py:1490
  200.1 9.2 %all-to-all-start = ((bf16[8,48,1536]{2,1,0:T(8,128)(2,1)}), bf16[8,48,1536]{2,1,0:T(8,128)(2,1)S(1)}, u32[]{:S(2)}, u32[]{:S(2)}) async-start(bf16[8,48,1536]{2,1,0:T(8,128)(2,1)} %bitcast.123), calls=%async_computation | async-start | bytes 2359296 | tf_op jit(solution)/shard_map/all_to_all | solution.py:435
  212.0 37.8 %attend_forward.1 = (bf16[384,1536]{1,0:T(8,128)(2,1)}, bf16[384,1536]{1,0:T(8,128)(2,1)}, bf16[384,1536]{1,0:T(8,128)(2,1)}, bf16[384,1536]{1,0:T(8,128)(2,1)},...) custom-call(s32[4]{0:T(128)} %pad_add_fusion.ids, ...), custom_call_target="tpu_custom_call" | custom-call | flops 30000001024 | bytes 25165824 | tf_op jit(solution)/shard_map/attend_forward/pallas_call | solution.py:701
  249.8 20.7 %all-to-all-done = bf16[8,48,1536]{2,1,0:T(8,128)(2,1)S(1)} async-done(((bf16[8,48,1536]{2,1,0:T(8,128)(2,1)}), bf16[8,48,1536]{2,1,0:T(8,128)(2,1)S(1)}, u32[]{:S(2)}, u32[]{:S(2)}) %all-to-all-start) | async-done | bytes 1179680 | tf_op jit(solution)/shard_map/all_to_all | solution.py:435
  271.5 70.5 %middle.1 = (bf16[384,1536]{1,0:T(8,128)(2,1)S(1)}, bf16[384,1536]{1,0:T(8,128)(2,1)S(1)}, bf16[4,192,768]{2,1,0:T(8,128)(2,1)S(1)}, bf16[4,192,768]{2,1,0:T(8,1...) custom-call(bf16[384,1536]{1,0:T(8,128)(2,1)} %get-tuple-element.104, ...), custom_call_target="tpu_custom_call" | custom-call | flops 10000000 | bytes 104857600 | tf_op jit(solution)/shard_map/middle/pallas_call | solution.py:1653
  353.3 20.3 %cross_forward.1 = (f32[384,1536]{1,0:T(8,128)}, bf16[384,1536]{1,0:T(8,128)(2,1)S(1)}, bf16[384,1536]{1,0:T(8,128)(2,1)S(1)}, bf16[384,1536]{1,0:T(8,128)(2,1)S...) custom-call(s32[4]{0:T(128)S(1)} %copy-done.16, s32[1]{0:T(128)} %bitcast.4.count, bf16[384,1536]{1,0:T(8,128)(2,1)} %bitcast.116, ...), custom_call_target="tpu_custom_call" | custom-call | flops 12000000000 | bytes 25165824 | tf_op jit(solution)/shard_map/cross_forward/pallas_call | solution.py:1049
  378.3 26.6 %collective-permute-done.1.refs_2_ = bf16[384,1536]{1,0:T(8,128)(2,1)S(1)} collective-permute-done((bf16[384,1536]{1,0:T(8,128)(2,1)S(1)}, bf16[384,1536]{1,0:T(8,128)(2,1)S(1)}, u32[]{:S(2)}, u32[]{:S(2)}) %collective-permute-start.1) | collective-permute-done | bytes 1179680 | tf_op jit(solution)/shard_map/ppermute | solution.py:401
  407.9 44.6 %feed_forward.1 = (bf16[384,1536]{1,0:T(8,128)(2,1)}, bf16[384,1536]{1,0:T(8,128)(2,1)}, bf16[384,1536]{1,0:T(8,128)(2,1)}, bf16[384,1536]{1,0:T(8,128)(2,1)}, b...) custom-call(s32[4]{0:T(128)} %pad_add_fusion.ids, ...), custom_call_target="tpu_custom_call" | custom-call | flops 28991029248 | bytes 37748736 | tf_op jit(solution)/shard_map/feed_forward/pallas_call | solution.py:892
  454.9 14.0 %feed_grads.3 = bf16[2,4,2,2,192,384]{5,4,3,2,1,0:T(8,128)(2,1)S(1)} custom-call(s32[4]{0:T(128)S(1)} %copy-done.17, bf16[384,1536]{1,0:T(8,128)(2,1)S(1)} %bitcast.112, bf16[384,1536]{1,0:T(8,128)(2,1)S(1)} %copy-done.50, bf16[384,1536]{1,0:T(8,128)(2,1)S(1)} %copy-done.52, bf16[384,1536]{1,0:T(8,128)(2,1)S(1)} %copy-done.54, ...), custom_call_target="tpu_custom_call" | custom-call | flops 7247757312 | bytes 16777216 | tf_op jit(solution)/shard_map/feed_grads/pallas_call | solution.py:938
  476.2 26.5 %collective-permute-done.7.refs_3_ = bf16[384,1536]{1,0:T(8,128)(2,1)S(1)} collective-permute-done((bf16[384,1536]{1,0:T(8,128)(2,1)S(1)}, bf16[384,1536]{1,0:T(8,128)(2,1)S(1)}, u32[]{:S(2)}, u32[]{:S(2)}) %collective-permute-start.7) | collective-permute-done | bytes 1179680 | tf_op jit(solution)/shard_map/ppermute | solution.py:401
  503.7 26.6 %cross_backward.1 = (f32[384,1536]{1,0:T(8,128)}, bf16[384,1536]{1,0:T(8,128)(2,1)}, bf16[384,1536]{1,0:T(8,128)(2,1)}, bf16[384,1536]{1,0:T(8,128)(2,1)}, bf16[...) custom-call(s32[4]{0:T(128)} %pad_add_fusion.ids, s32[1]{0:T(128)} %bitcast.4.count, bf16[384,1536]{1,0:T(8,128)(2,1)} %bitcast.111, ...), custom_call_target="tpu_custom_call" | custom-call | flops 16000000000 | bytes 29360128 | tf_op jit(solution)/shard_map/cross_backward/pallas_call | solution.py:1156
  532.9 8.5 cross_grads.1
  545.5 26.6 %collective-permute-done.9.refs_2_.refs_6_ = bf16[384,1536]{1,0:T(8,128)(2,1)S(1)} collective-permute-done((bf16[384,1536]{1,0:T(8,128)(2,1)S(1)}, bf16[384,1536]{1,0:T(8,128)(2,1)S(1)}, u32[]{:S(2)}, u32[]{:S(2)}) %collective-permute-start.9) | collective-permute-done | bytes 1179680 | tf_op jit(solution)/shard_map/ppermute | solution.py:401
  577.7 14.8 %feed_grads.2 = bf16[2,4,2,2,192,384]{5,4,3,2,1,0:T(8,128)(2,1)S(1)} custom-call(s32[4]{0:T(128)S(1)} %copy-done.18, bf16[384,1536]{1,0:T(8,128)(2,1)S(1)} %copy-done.32, bf16[384,1536]{1,0:T(8,128)(2,1)S(1)} %copy-done.36, bf16[384,1536]{1,0:T(8,128)(2,1)S(1)} %copy-done.34, bf16[384,1536]{1,0:T(8,128)(2,1)} %collective-permute-done.2.refs_3_, ...), custom_call_target="tpu_custom_call" | custom-call | flops 7247757312 | bytes 16777216 | tf_op jit(solution)/shard_map/feed_grads/pallas_call | solution.py:938
  604.6 5.7 fusion.1
  610.7 49.2 %attend_backward.1 = (bf16[384,1536]{1,0:T(8,128)(2,1)}, bf16[384,1536]{1,0:T(8,128)(2,1)}, bf16[384,1536]{1,0:T(8,128)(2,1)}, bf16[384,1536]{1,0:T(8,128)(2,1)}, bf16[2,4,384,576]{3,2,1,0:T(8,128)(2,1)}) custom-call(s32[4]{0:T(128)} %pad_add_fusion.ids, bf16[384,1536]{1,0:T(8,128)(2,1)} %get-tuple-element.135.refs_0_.refs_4_, bf16[384,1536]{1,0:T(8,128)(2,1)} %copy-done.39, ...), custom_call_target="tpu_custom_call" | custom-call | flops 49999998976 | bytes 25165824 | tf_op jit(solution)/shard_map/attend_backward/pallas_call | solution.py:724
  663.8 5.8 all-to-all-start.2
  669.6 12.6 %collective-permute-done.15 = bf16[2,4,192,768]{3,2,1,0:T(8,128)(2,1)} collective-permute-done((bf16[2,4,192,768]{3,2,1,0:T(8,128)(2,1)}, bf16[2,4,192,768]{3,2,1,0:T(8,128)(2,1)}, u32[]{:S(2)}, u32[]{:S(2)}) %collective-permute-start.15) | collective-permute-done | bytes 2359328 | tf_op jit(solution)/shard_map/ppermute | solution.py:401
  696.2 10.0 %attend_grads.3.near = bf16[2,2,2,192,768]{4,3,2,1,0:T(8,128)(2,1)S(1)} custom-call(s32[4]{0:T(128)S(1)} %copy-done.19, bf16[384,1536]{1,0:T(8,128)(2,1)S(1)} %copy-done.22, bf16[384,1536]{1,0:T(8,128)(2,1)S(1)} %copy-done.24, bf16[384,1536]{1,0:T(8,128)(2,1)S(1)} %copy-done.26, bf16[384,1536]{1,0:T(8,128)(2,1)S(1)} %copy-done.28, ...), custom_call_target="tpu_custom_call" | custom-call | flops 6000000000 | bytes 12582912 | tf_op jit(solution)/shard_map/attend_grads/pallas_call | solution.py:769
  707.5 10.0 %attend_grads.2.far = bf16[2,2,2,192,768]{4,3,2,1,0:T(8,128)(2,1)S(1)} custom-call(s32[4]{0:T(128)S(1)} %copy-done.19, bf16[384,1536]{1,0:T(8,128)(2,1)S(1)} %copy-done.22, bf16[384,1536]{1,0:T(8,128)(2,1)S(1)} %copy-done.24, bf16[384,1536]{1,0:T(8,128)(2,1)S(1)} %copy-done.26, bf16[384,1536]{1,0:T(8,128)(2,1)S(1)} %copy-done.28, ...), custom_call_target="tpu_custom_call" | custom-call | flops 6000000000 | bytes 12582912 | tf_op jit(solution)/shard_map/attend_grads/pallas_call | solution.py:769
  719.0 6.8 collective-permute-done.16
  729.3 121.6 %end.1 = (bf16[8,48,1536]{2,1,0:T(8,128)(2,1)}, f32[8,1536]{1,0:T(8,128)}, bf16[192,768]{1,0:T(8,128)(2,1)}, bf16[192,768]{1,0:T(8,128)(2,1)}, f32[192,768]{1,0:...) custom-call(bf16[2,2,2,192,768]{4,3,2,1,0:T(8,128)(2,1)} %copy-done.8, ...), custom_call_target="tpu_custom_call" | custom-call | flops 10000000 | bytes 314572800 | tf_op jit(solution)/shard_map/end/pallas_call | solution.py:2045
  874.3 3.6 copy.108
  (320 shorter events, 152.5 us)
Async XLA Ops:
  7.2 400.7 %all-gather.2.cloned.1.call-start = ((), (), s32[]{:S(2)}) async-start(), calls=%async_computation.5 | async-start | bytes 10616832 | tf_op jit(solution)/shard_map/all_gather | solution.py:485
  13.9 16.5 %collective-permute-start.3 = (bf16[2,2,192,384]{3,0,2,1:T(2,128)(2,1)}, bf16[2,2,192,384]{3,0,2,1:T(2,128)(2,1)S(1)}, u32[]{:S(2)}, u32[]{:S(2)}) collective-permute-start(bf16[2,2,192,384]{3,0,2,1:T(2,128)(2,1)} %get-tuple-element.196), channel_id=1, source_target_pairs={{0,8},{8,0},{1,9},{9,1},{2,10},{10,2},{3,11},{11,3},{4,12},{12,4},... | collective-permute-start | bytes 1769480 | tf_op jit(solution)/shard_map/ppermute | solution.py:401
  200.1 70.4 %all-to-all-start = ((bf16[8,48,1536]{2,1,0:T(8,128)(2,1)}), bf16[8,48,1536]{2,1,0:T(8,128)(2,1)S(1)}, u32[]{:S(2)}, u32[]{:S(2)}) async-start(bf16[8,48,1536]{2,1,0:T(8,128)(2,1)} %bitcast.123), calls=%async_computation | async-start | bytes 2359296 | tf_op jit(solution)/shard_map/all_to_all | solution.py:435
  209.3 641.6 %reduce-scatter.5.cloned.1.call-start = ((), (), s32[]{:S(2)}) async-start(), calls=%async_computation.7 | async-start | bytes 5308416 | tf_op jit(solution)/shard_map/reduce_scatter | solution.py:490
  376.8 28.1 %collective-permute-start.1 = (bf16[384,1536]{1,0:T(8,128)(2,1)S(1)}, bf16[384,1536]{1,0:T(8,128)(2,1)S(1)}, u32[]{:S(2)}, u32[]{:S(2)}) collective-permute-start(bf16[384,1536]{1,0:T(8,128)(2,1)S(1)} %get-tuple-element.121.refs_0_), channel_id=1, source_target_pairs={{0,8},{8,0},{1,9},{9,1},{2,10},{10,2},{3,11},{11,3},{4,12},{12,4},... | collective-permute-start | bytes 3538952 | tf_op jit(solution)/shard_map/ppermute | solution.py:401
  378.2 26.7 %collective-permute-start = (bf16[384,1536]{1,0:T(8,128)(2,1)S(1)}, bf16[384,1536]{1,0:T(8,128)(2,1)S(1)}, u32[]{:S(2)}, u32[]{:S(2)}) collective-permute-start(bf16[384,1536]{1,0:T(8,128)(2,1)S(1)} %get-tuple-element.121.refs_0_), channel_id=1, source_target_pairs={{0,4},{4,0},{1,5},{5,1},{2,6},{6,2},{3,7},{7,3},{8,12},{12,8},{9,1... | collective-permute-start | bytes 3538952 | tf_op jit(solution)/shard_map/ppermute | solution.py:401
  471.2 381.7 %reduce-scatter.3.cloned.1.call-start = ((), (), s32[]{:S(2)}) async-start(), calls=%async_computation.6 | async-start | bytes 5308416 | tf_op jit(solution)/shard_map/reduce_scatter | solution.py:490
  471.2 3.1 collective-permute-start.6
  472.4 3.8 collective-permute-start.5
  474.6 28.1 %collective-permute-start.7 = (bf16[384,1536]{1,0:T(8,128)(2,1)S(1)}, bf16[384,1536]{1,0:T(8,128)(2,1)S(1)}, u32[]{:S(2)}, u32[]{:S(2)}) collective-permute-start(bf16[384,1536]{1,0:T(8,128)(2,1)S(1)} %add_convert_fusion.6), channel_id=1, source_target_pairs={{0,8},{8,0},{1,9},{9,1},{2,10},{10,2},{3,11},{11,3},{4,12},{12,4},... | collective-permute-start | bytes 3538952 | tf_op jit(solution)/shard_map/ppermute | solution.py:401
  543.7 60.9 %collective-permute-start.14 = (bf16[2,2,4,192,768]{4,3,2,1,0:T(8,128)(2,1)}, bf16[2,2,4,192,768]{4,3,2,1,0:T(8,128)(2,1)}, u32[]{:S(2)}, u32[]{:S(2)}) collective-permute-start(bf16[2,2,4,192,768]{4,3,2,1,0:T(8,128)(2,1)} %get-tuple-element.162), channel_id=1, source_target_pairs={{0,4},{4,0},{1,5},{5,1},{2,6},{6,2},{3,7},{7,3},{8,12},{12,8},{9,1... | collective-permute-start | bytes 14155784 | tf_op jit(solution)/shard_map/ppermute | solution.py:401
  543.7 28.4 %collective-permute-start.9 = (bf16[384,1536]{1,0:T(8,128)(2,1)S(1)}, bf16[384,1536]{1,0:T(8,128)(2,1)S(1)}, u32[]{:S(2)}, u32[]{:S(2)}) collective-permute-start(bf16[384,1536]{1,0:T(8,128)(2,1)S(1)} %copy-done.29), channel_id=1, source_target_pairs={{0,8},{8,0},{1,9},{9,1},{2,10},{10,2},{3,11},{11,3},{4,12},{12,4},... | collective-permute-start | bytes 3538952 | tf_op jit(solution)/shard_map/ppermute | solution.py:401
  545.2 26.8 %collective-permute-start.8 = (bf16[384,1536]{1,0:T(8,128)(2,1)S(1)}, bf16[384,1536]{1,0:T(8,128)(2,1)S(1)}, u32[]{:S(2)}, u32[]{:S(2)}) collective-permute-start(bf16[384,1536]{1,0:T(8,128)(2,1)S(1)} %copy-done.29), channel_id=1, source_target_pairs={{0,4},{4,0},{1,5},{5,1},{2,6},{6,2},{3,7},{7,3},{8,12},{12,8},{9,1... | collective-permute-start | bytes 3538952 | tf_op jit(solution)/shard_map/ppermute | solution.py:401
  574.9 25.5 %collective-permute-start.12 = (bf16[384,1536]{1,0:T(8,128)(2,1)}, bf16[384,1536]{1,0:T(8,128)(2,1)}, u32[]{:S(2)}, u32[]{:S(2)}) collective-permute-start(bf16[384,1536]{1,0:T(8,128)(2,1)} %get-tuple-element.139), channel_id=1, source_target_pairs={{0,4},{4,0},{1,5},{5,1},{2,6},{6,2},{3,7},{7,3},{8,12},{12,8},{9,1... | collective-permute-start | bytes 3538952 | tf_op jit(solution)/shard_map/ppermute | solution.py:401
  596.7 66.2 %all-to-all-start.1 = ((bf16[8,64,768]{2,1,0:T(8,128)(2,1)}), bf16[8,64,768]{2,1,0:T(8,128)(2,1)S(1)}, u32[]{:S(2)}, u32[]{:S(2)}) async-start(bf16[8,64,768]{2,1,0:T(8,128)(2,1)} %pad_maximum_fusion.1), calls=%async_computation.1 | async-start | bytes 1572864 | tf_op jit(solution)/shard_map/all_to_all | solution.py:435
  600.2 59.7 %collective-permute-start.11 = (bf16[384,1536]{1,0:T(8,128)(2,1)}, bf16[384,1536]{1,0:T(8,128)(2,1)S(1)}, u32[]{:S(2)}, u32[]{:S(2)}) collective-permute-start(bf16[384,1536]{1,0:T(8,128)(2,1)} %get-tuple-element.137), channel_id=1, source_target_pairs={{0,4},{4,0},{1,5},{5,1},{2,6},{6,2},{3,7},{7,3},{8,12},{12,8},{9,1... | collective-permute-start | bytes 3538952 | tf_op jit(solution)/shard_map/ppermute | solution.py:401
  603.0 57.0 %collective-permute-start.13 = (bf16[384,1536]{1,0:T(8,128)(2,1)}, bf16[384,1536]{1,0:T(8,128)(2,1)}, u32[]{:S(2)}, u32[]{:S(2)}) collective-permute-start(bf16[384,1536]{1,0:T(8,128)(2,1)} %add_convert_fusion.5), channel_id=1, source_target_pairs={{0,8},{8,0},{1,9},{9,1},{2,10},{10,2},{3,11},{11,3},{4,12},{12,4},... | collective-permute-start | bytes 3538952 | tf_op jit(solution)/shard_map/ppermute | solution.py:401
  610.3 71.8 %collective-permute-start.15 = (bf16[2,4,192,768]{3,2,1,0:T(8,128)(2,1)}, bf16[2,4,192,768]{3,2,1,0:T(8,128)(2,1)}, u32[]{:S(2)}, u32[]{:S(2)}) collective-permute-start(bf16[2,4,192,768]{3,2,1,0:T(8,128)(2,1)} %get-tuple-element.163), channel_id=1, source_target_pairs={{0,8},{8,0},{1,9},{9,1},{2,10},{10,2},{3,11},{11,3},{4,12},{12,4},... | collective-permute-start | bytes 7077896 | tf_op jit(solution)/shard_map/ppermute | solution.py:401
  663.8 55.2 %all-to-all-start.2 = ((bf16[8,48,1536]{2,1,0:T(8,128)(2,1)}), bf16[8,48,1536]{2,1,0:T(8,128)(2,1)}, u32[]{:S(2)}, u32[]{:S(2)}) async-start(bf16[8,48,1536]{2,1,0:T(8,128)(2,1)} %bitcast.23), calls=%async_computation.2 | async-start | bytes 2359296 | tf_op jit(solution)/shard_map/all_to_all | solution.py:435
  685.3 40.6 %collective-permute-start.16 = (bf16[4,192,768]{2,1,0:T(8,128)(2,1)}, bf16[4,192,768]{2,1,0:T(8,128)(2,1)}, u32[]{:S(2)}, u32[]{:S(2)}) collective-permute-start(bf16[4,192,768]{2,1,0:T(8,128)(2,1)} %fusion.4), channel_id=1, source_target_pairs={{0,16},{16,0},{1,17},{17,1},{2,18},{18,2},{3,19},{19,3},{4,20},{20... | collective-permute-start | bytes 3538952 | tf_op jit(solution)/shard_map/ppermute | solution.py:401
  854.9 9.8 %collective-permute-start.17 = (bf16[2,192,384]{2,1,0:T(8,128)(2,1)}, bf16[2,192,384]{2,1,0:T(8,128)(2,1)}, u32[]{:S(2)}, u32[]{:S(2)}) collective-permute-start(bf16[2,192,384]{2,1,0:T(8,128)(2,1)} %get-tuple-element.204), channel_id=1, source_target_pairs={{0,8},{8,0},{1,9},{9,1},{2,10},{10,2},{3,11},{11,3},{4,12},{12,4},... | collective-permute-start | bytes 884744 | tf_op jit(solution)/shard_map/ppermute | solution.py:401
  858.0 12.9 %collective-permute-start.19 = (bf16[2,192,384]{2,1,0:T(8,128)(2,1)}, bf16[2,192,384]{2,1,0:T(8,128)(2,1)}, u32[]{:S(2)}, u32[]{:S(2)}) collective-permute-start(bf16[2,192,384]{2,1,0:T(8,128)(2,1)} %get-tuple-element.200), channel_id=1, source_target_pairs={{0,8},{8,0},{1,9},{9,1},{2,10},{10,2},{3,11},{11,3},{4,12},{12,4},... | collective-permute-start | bytes 884744 | tf_op jit(solution)/shard_map/ppermute | solution.py:401
  865.9 14.8 %collective-permute-start.18 = (bf16[2,192,384]{2,1,0:T(8,128)(2,1)S(1)}, bf16[2,192,384]{2,1,0:T(8,128)(2,1)S(1)}, u32[]{:S(2)}, u32[]{:S(2)}) collective-permute-start(bf16[2,192,384]{2,1,0:T(8,128)(2,1)S(1)} %get-tuple-element.202), channel_id=1, source_target_pairs={{0,4},{4,0},{1,5},{5,1},{2,6},{6,2},{3,7},{7,3},{8,12},{12,8},{9,1... | collective-permute-start | bytes 884744 | tf_op jit(solution)/shard_map/ppermute | solution.py:401
  872.2 8.5 collective-permute-start.20
  (105 other events, 1231.9 us)
Sparse Core Ops, SparseCore 0:
  37.3 238.4 all-gather.1
  471.3 93.5 reduce-scatter.4
  594.9 123.4 reduce-scatter.2

commit v5 on v4

--- a/solution.py
+++ b/solution.py
@@ -440,9 +440,12 @@
     return [own, pair_swap(own, "c"), across, pair_swap(across, "c")]
 
 
-def group_terms(parts):
-    far = wide(parts[2]) + wide(pair_swap(parts[3], "c"))
-    return [parts[0], pair_swap(parts[1], "c"), pair_swap(narrow(far), "x")]
+def far_sum(parts):
+    return narrow(wide(parts[2]) + wide(pair_swap(parts[3], "c")))
+
+
+def group_terms(parts, far):
+    return [parts[0], pair_swap(parts[1], "c"), pair_swap(far, "x")]
 
 
 def everywhere(values):
@@ -499,11 +502,11 @@
     return whole.reshape(whole.shape[0], -1)
 
 
-def sum_plane(keep, send, gate):
+def sum_plane(keep, send):
     got = pair_swap(send, "c")
     away = narrow(wide(keep[1]) + wide(got[1]))
     near = narrow(wide(keep[0]) + wide(got[0]))
-    return near, pair_swap(after(away, gate), "x")
+    return near, away
 
 
 def sum_plane_rest(near, got):
@@ -2185,8 +2188,9 @@
     feed_parts, back_parts, active, grad_hidden = feed(
         ids, rows_three, grad_rows3, both
     )
-    back_terms = group_terms(back_parts)
-    part_down = feed_grads(ids, grad_rows3, active)
+    back_far = far_sum(back_parts)
+    back_terms = group_terms(back_parts, back_far)
+    part_down = feed_grads(after(ids, back_far), grad_rows3, active)
     part_up = feed_grads(ids, rows_three, grad_hidden)
     sum_down, sum_up = scatter_units(part_down), scatter_units(part_up)
     grad_one_rows, own_one, own_two, grad_cq, grad_text, norm_grads = cross_backward(
@@ -2201,12 +2205,17 @@
         cross_q,
         cross_pieces,
     )
-    grad_rows1 = group_rows(own_one)
+    across = pair_swap(own_one, "x")
+    grad_rows1 = [own_one, pair_swap(own_one, "c"), across]
     cross_keep, cross_send = cross_grads(ids, rows_two, grad_cq, own_two, mixed_two)
-    cross_sum = sum_plane(cross_keep, cross_send, grad_rows1)
+    cross_near, cross_away = sum_plane(cross_keep, cross_send)
+    relay = pair_swap(after(across, part_up, part_down, cross_near, cross_away), "c")
+    grad_rows1 = grad_rows1 + [relay]
+    cross_sum = (cross_near, pair_swap(after(cross_away, grad_rows1), "x"))
     grad_text = exchange_clips(jnp.concatenate([grad_text, grad_text]))
 
-    feed_terms = group_terms(after(feed_parts, grad_rows1))
+    feed_parts = after(feed_parts, grad_rows1)
+    feed_terms = group_terms(feed_parts, far_sum(feed_parts))
     self_back, grad_qkv = attend_backward(
         after(ids, cross_keep, part_up, part_down),
         grad_rows1,
@@ -2237,7 +2246,7 @@
         text_mine,
         text_shard,
     )
-    fin_down = join_units(after(sum_down, input_grad)).T
+    fin_down = join_units(sum_down).T
     fin_up = join_units(after(sum_up, input_grad))
     fin_cquery, fin_cout = fin_cross[:, :shard_width], fin_cross[:, shard_width:].T
     fin_ckey, fin_cvalue = fin_text[:, :shard_width], fin_text[:, shard_width:]

time: 907 us -> 871 us (0.960)
  waiting for transfers between devices: 144 us -> 109 us
    ppermute x21, waiting for transfers between devices: 123 us -> 88 us  [pair_swap(): return lax.ppermute(values, axis_name, [(0, 1), (1, 0)])]
    unnamed x209 -> x213, local copies, waits for them, and re-layouts: 60.5 us -> 59.7 us
  transfers between devices with their start and end apart: 27 -> 27, of which waited for: 13 -> 12; matrix products, arithmetic and copies ran while one was open for 5% -> 6% of each run, Pallas kernels for 57% -> 62%
where the time goes in v5:
time: 871 us; the launch traced here: 862 us
  Pallas kernels  575 us (66%)
  waiting for transfers between devices  109 us (13%)
  local copies, waits for them, and re-layouts  88.8 us (10%)
  other arithmetic  37.6 us (4%)
  starting transfers between devices  35.5 us (4%)
  between operations  15.1 us (2%)
    pallas_call x1, Pallas kernels, start_up(): pl.pallas_call(functools.partial(start_kernel, size), in_specs=[vmem] * 4...  145 us
    pallas_call x1, Pallas kernels, end(): pl.pallas_call(functools.partial(end_kernel, size), in_specs=[vmem] * 14,...  125 us
    ppermute x21, waiting for transfers between devices, pair_swap(): return lax.ppermute(values, axis_name, [(0, 1), (1, 0)])  88 us
    pallas_call x1, Pallas kernels, middle(): pl.pallas_call(functools.partial(middle_kernel, size), in_specs=[vmem] *...  70.5 us
    unnamed x213, local copies, waits for them, and re-layouts  59.7 us
    pallas_call x1, Pallas kernels, attend_backward(): pl.pallas_call(attend_backward_kernel, in_specs=[SCALARS] + [vmem] * (PIE...  49.3 us
    pallas_call x1, Pallas kernels, feed(): pl.pallas_call(feed_kernel, in_specs=[SCALARS] + [ANYWHERE] * 9, out_spec...  44.2 us
    pallas_call x1, Pallas kernels, attend_forward(): pl.pallas_call(attend_forward_kernel, in_specs=[SCALARS] + [pl.BlockSpec(...  37.8 us
  transfers between devices with their start and end apart: 27, of which 12 were waited for; matrix products, arithmetic and copies ran while one was open for 6% of the time, Pallas kernels for 62%

profile of v5, /device:TPU:0, one launch (start us, length us, event | category | flops | bytes accessed | tf_op | source)
XLA Modules:
  0.0 861.6 jit_solution(12161313167549924729)
XLA Ops:
  16.8 13.5 %collective-permute-done.3 = bf16[2,2,192,384]{3,0,2,1:T(2,128)(2,1)S(1)} collective-permute-done((bf16[2,2,192,384]{3,0,2,1:T(2,128)(2,1)}, bf16[2,2,192,384]{3,0,2,1:T(2,128)(2,1)S(1)}, u32[]{:S(2)}, u32[]{:S(2)}) %collective-permute-start.3) | collective-permute-done | bytes 589856 | tf_op jit(solution)/shard_map/ppermute | solution.py:401
  46.1 144.6 %start_up.1 = (bf16[8,48,1536]{2,1,0:T(8,128)(2,1)S(1)}, bf16[384,1536]{1,0:T(8,128)(2,1)S(1)}, bf16[384,1536]{1,0:T(8,128)(2,1)S(1)}, bf16[384,1536]{1,0:T(8,12...) custom-call(bf16[8,48,1536]{2,1,0:T(8,128)(2,1)S(1)} %bitcast.118, ...), custom_call_target="tpu_custom_call" | custom-call | flops 10000000 | bytes 209715200 | tf_op jit(solution)/shard_map/start_up/pallas_call | solution.py:1493
  200.1 9.2 %all-to-all-start = ((bf16[8,48,1536]{2,1,0:T(8,128)(2,1)}), bf16[8,48,1536]{2,1,0:T(8,128)(2,1)S(1)}, u32[]{:S(2)}, u32[]{:S(2)}) async-start(bf16[8,48,1536]{2,1,0:T(8,128)(2,1)} %bitcast.124), calls=%async_computation | async-start | bytes 2359296 | tf_op jit(solution)/shard_map/all_to_all | solution.py:435
  211.9 37.8 %attend_forward.1 = (bf16[384,1536]{1,0:T(8,128)(2,1)}, bf16[384,1536]{1,0:T(8,128)(2,1)}, bf16[384,1536]{1,0:T(8,128)(2,1)}, bf16[384,1536]{1,0:T(8,128)(2,1)},...) custom-call(s32[4]{0:T(128)} %pad_add_fusion.ids, ...), custom_call_target="tpu_custom_call" | custom-call | flops 30000001024 | bytes 25165824 | tf_op jit(solution)/shard_map/attend_forward/pallas_call | solution.py:704
  249.7 20.8 %all-to-all-done = bf16[8,48,1536]{2,1,0:T(8,128)(2,1)S(1)} async-done(((bf16[8,48,1536]{2,1,0:T(8,128)(2,1)}), bf16[8,48,1536]{2,1,0:T(8,128)(2,1)S(1)}, u32[]{:S(2)}, u32[]{:S(2)}) %all-to-all-start) | async-done | bytes 1179680 | tf_op jit(solution)/shard_map/all_to_all | solution.py:435
  271.5 70.5 %middle.1 = (bf16[384,1536]{1,0:T(8,128)(2,1)S(1)}, bf16[384,1536]{1,0:T(8,128)(2,1)S(1)}, bf16[4,192,768]{2,1,0:T(8,128)(2,1)S(1)}, bf16[4,192,768]{2,1,0:T(8,1...) custom-call(bf16[384,1536]{1,0:T(8,128)(2,1)} %get-tuple-element.105, ...), custom_call_target="tpu_custom_call" | custom-call | flops 10000000 | bytes 104857600 | tf_op jit(solution)/shard_map/middle/pallas_call | solution.py:1656
  353.4 20.3 %cross_forward.1 = (f32[384,1536]{1,0:T(8,128)}, bf16[384,1536]{1,0:T(8,128)(2,1)S(1)}, bf16[384,1536]{1,0:T(8,128)(2,1)S(1)}, bf16[384,1536]{1,0:T(8,128)(2,1)S...) custom-call(s32[4]{0:T(128)S(1)} %copy-done.15, s32[1]{0:T(128)} %bitcast.4.count, bf16[384,1536]{1,0:T(8,128)(2,1)} %bitcast.117, ...), custom_call_target="tpu_custom_call" | custom-call | flops 12000000000 | bytes 25165824 | tf_op jit(solution)/shard_map/cross_forward/pallas_call | solution.py:1052
  378.3 26.6 %collective-permute-done.1.refs_2_ = bf16[384,1536]{1,0:T(8,128)(2,1)S(1)} collective-permute-done((bf16[384,1536]{1,0:T(8,128)(2,1)S(1)}, bf16[384,1536]{1,0:T(8,128)(2,1)S(1)}, u32[]{:S(2)}, u32[]{:S(2)}) %collective-permute-start.1) | collective-permute-done | bytes 1179680 | tf_op jit(solution)/shard_map/ppermute | solution.py:401
  407.9 44.2 %feed_forward.1 = (bf16[384,1536]{1,0:T(8,128)(2,1)}, bf16[384,1536]{1,0:T(8,128)(2,1)}, bf16[384,1536]{1,0:T(8,128)(2,1)}, bf16[384,1536]{1,0:T(8,128)(2,1)}, b...) custom-call(s32[4]{0:T(128)} %pad_add_fusion.ids, ...), custom_call_target="tpu_custom_call" | custom-call | flops 28991029248 | bytes 37748736 | tf_op jit(solution)/shard_map/feed_forward/pallas_call | solution.py:895
  461.2 14.0 %feed_grads.3 = bf16[2,4,2,2,192,384]{5,4,3,2,1,0:T(8,128)(2,1)S(1)} custom-call(s32[4]{0:T(128)S(1)} %copy-done.16, bf16[384,1536]{1,0:T(8,128)(2,1)S(1)} %bitcast.113, bf16[384,1536]{1,0:T(8,128)(2,1)S(1)} %copy-done.56, bf16[384,1536]{1,0:T(8,128)(2,1)S(1)} %copy-done.58, bf16[384,1536]{1,0:T(8,128)(2,1)S(1)} %copy-done.60, ...), custom_call_target="tpu_custom_call" | custom-call | flops 7247757312 | bytes 16777216 | tf_op jit(solution)/shard_map/feed_grads/pallas_call | solution.py:941
  477.5 7.9 collective-permute-done.7.refs_3_
  485.4 26.5 %cross_backward.1 = (f32[384,1536]{1,0:T(8,128)}, bf16[384,1536]{1,0:T(8,128)(2,1)}, bf16[384,1536]{1,0:T(8,128)(2,1)}, bf16[384,1536]{1,0:T(8,128)(2,1)}, bf16[...) custom-call(s32[4]{0:T(128)} %pad_add_fusion.ids, s32[1]{0:T(128)} %bitcast.4.count, bf16[384,1536]{1,0:T(8,128)(2,1)} %bitcast.112, ...), custom_call_target="tpu_custom_call" | custom-call | flops 16000000000 | bytes 29360128 | tf_op jit(solution)/shard_map/cross_backward/pallas_call | solution.py:1159
  514.5 8.6 %cross_grads.1 = (bf16[2,2,4,192,768]{4,3,2,1,0:T(8,128)(2,1)S(1)}, bf16[2,2,4,192,768]{4,3,2,1,0:T(8,128)(2,1)}) custom-call(s32[4]{0:T(128)S(1)} %copy-done.17, bf16[384,1536]{1,0:T(8,128)(2,1)S(1)} %copy-done.67, bf16[384,1536]{1,0:T(8,128)(2,1)S(1)} %copy-done.71, bf16[384,1536]{1,0:T(8,128)(2,1)S(1)} %copy-done.70, bf16[384,1536]{1,0:T(8,128)(2,1)S(1)} %copy-done.69), custom_call_target="tpu_custom_call" | custom-call | flops 3623878656 | bytes 14680064 | tf_op jit(solution)/shard_map/cross_grads/pallas_call | solution.py:1210
  527.0 14.8 %feed_grads.2 = bf16[2,4,2,2,192,384]{5,4,3,2,1,0:T(8,128)(2,1)S(1)} custom-call(s32[4]{0:T(128)S(1)} %copy-done.17, bf16[384,1536]{1,0:T(8,128)(2,1)S(1)} %copy-done.41, bf16[384,1536]{1,0:T(8,128)(2,1)S(1)} %copy-done.54, bf16[384,1536]{1,0:T(8,128)(2,1)S(1)} %copy-done.43, bf16[384,1536]{1,0:T(8,128)(2,1)} %collective-permute-done.2.refs_3_, ...), custom_call_target="tpu_custom_call" | custom-call | flops 7247757312 | bytes 16777216 | tf_op jit(solution)/shard_map/feed_grads/pallas_call | solution.py:941
  542.0 5.8 fusion.1
  547.8 3.7 collective-permute-done.9.refs_2_.refs_6_
  557.6 3.5 all-to-all-start.1
  566.2 49.3 %attend_backward.1 = (bf16[384,1536]{1,0:T(8,128)(2,1)}, bf16[384,1536]{1,0:T(8,128)(2,1)}, bf16[384,1536]{1,0:T(8,128)(2,1)}, bf16[384,1536]{1,0:T(8,128)(2,1)}, bf16[2,4,384,576]{3,2,1,0:T(8,128)(2,1)}) custom-call(s32[4]{0:T(128)} %pad_add_fusion.ids, bf16[384,1536]{1,0:T(8,128)(2,1)} %get-tuple-element.136.refs_0_.refs_4_, bf16[384,1536]{1,0:T(8,128)(2,1)} %copy-done.37, ...), custom_call_target="tpu_custom_call" | custom-call | flops 49999998976 | bytes 25165824 | tf_op jit(solution)/shard_map/attend_backward/pallas_call | solution.py:727
  615.5 25.0 %collective-permute-done.14 = bf16[384,1536]{1,0:T(8,128)(2,1)} collective-permute-done((bf16[384,1536]{1,0:T(8,128)(2,1)}, bf16[384,1536]{1,0:T(8,128)(2,1)}, u32[]{:S(2)}, u32[]{:S(2)}) %collective-permute-start.14) | collective-permute-done | bytes 1179680 | tf_op jit(solution)/shard_map/ppermute | solution.py:401
  644.4 5.9 all-to-all-start.2
  662.0 10.0 %attend_grads.3.near = bf16[2,2,2,192,768]{4,3,2,1,0:T(8,128)(2,1)S(1)} custom-call(s32[4]{0:T(128)S(1)} %copy-done.18, bf16[384,1536]{1,0:T(8,128)(2,1)S(1)} %copy-done.21, bf16[384,1536]{1,0:T(8,128)(2,1)S(1)} %copy-done.23, bf16[384,1536]{1,0:T(8,128)(2,1)S(1)} %copy-done.26, bf16[384,1536]{1,0:T(8,128)(2,1)S(1)} %copy-done.29, ...), custom_call_target="tpu_custom_call" | custom-call | flops 6000000000 | bytes 12582912 | tf_op jit(solution)/shard_map/attend_grads/pallas_call | solution.py:772
  683.5 10.0 %attend_grads.2.far = bf16[2,2,2,192,768]{4,3,2,1,0:T(8,128)(2,1)S(1)} custom-call(s32[4]{0:T(128)S(1)} %copy-done.18, bf16[384,1536]{1,0:T(8,128)(2,1)S(1)} %copy-done.21, bf16[384,1536]{1,0:T(8,128)(2,1)S(1)} %copy-done.24, bf16[384,1536]{1,0:T(8,128)(2,1)S(1)} %copy-done.27, bf16[384,1536]{1,0:T(8,128)(2,1)S(1)} %copy-done.30, ...), custom_call_target="tpu_custom_call" | custom-call | flops 6000000000 | bytes 12582912 | tf_op jit(solution)/shard_map/attend_grads/pallas_call | solution.py:772
  699.8 124.9 %end.1 = (bf16[8,48,1536]{2,1,0:T(8,128)(2,1)}, f32[8,1536]{1,0:T(8,128)}, bf16[192,768]{1,0:T(8,128)(2,1)}, bf16[192,768]{1,0:T(8,128)(2,1)}, f32[192,768]{1,0:...) custom-call(bf16[2,2,2,192,768]{4,3,2,1,0:T(8,128)(2,1)} %copy-done.7, ...), custom_call_target="tpu_custom_call" | custom-call | flops 10000000 | bytes 314572800 | tf_op jit(solution)/shard_map/end/pallas_call | solution.py:2048
  838.8 3.6 copy.108
  (324 shorter events, 145.6 us)
Async XLA Ops:
  7.2 400.6 %all-gather.2.cloned.1.call-start = ((), (), s32[]{:S(2)}) async-start(), calls=%async_computation.5 | async-start | bytes 10616832 | tf_op jit(solution)/shard_map/all_gather | solution.py:488
  13.9 16.5 %collective-permute-start.3 = (bf16[2,2,192,384]{3,0,2,1:T(2,128)(2,1)}, bf16[2,2,192,384]{3,0,2,1:T(2,128)(2,1)S(1)}, u32[]{:S(2)}, u32[]{:S(2)}) collective-permute-start(bf16[2,2,192,384]{3,0,2,1:T(2,128)(2,1)} %get-tuple-element.198), channel_id=1, source_target_pairs={{0,8},{8,0},{1,9},{9,1},{2,10},{10,2},{3,11},{11,3},{4,12},{12,4},... | collective-permute-start | bytes 1769480 | tf_op jit(solution)/shard_map/ppermute | solution.py:401
  200.1 70.4 %all-to-all-start = ((bf16[8,48,1536]{2,1,0:T(8,128)(2,1)}), bf16[8,48,1536]{2,1,0:T(8,128)(2,1)S(1)}, u32[]{:S(2)}, u32[]{:S(2)}) async-start(bf16[8,48,1536]{2,1,0:T(8,128)(2,1)} %bitcast.124), calls=%async_computation | async-start | bytes 2359296 | tf_op jit(solution)/shard_map/all_to_all | solution.py:435
  209.3 464.1 %reduce-scatter.5.cloned.1.call-start = ((), (), s32[]{:S(2)}) async-start(), calls=%async_computation.7 | async-start | bytes 5308416 | tf_op jit(solution)/shard_map/reduce_scatter | solution.py:493
  376.8 28.1 %collective-permute-start.1 = (bf16[384,1536]{1,0:T(8,128)(2,1)S(1)}, bf16[384,1536]{1,0:T(8,128)(2,1)S(1)}, u32[]{:S(2)}, u32[]{:S(2)}) collective-permute-start(bf16[384,1536]{1,0:T(8,128)(2,1)S(1)} %get-tuple-element.122.refs_0_), channel_id=1, source_target_pairs={{0,8},{8,0},{1,9},{9,1},{2,10},{10,2},{3,11},{11,3},{4,12},{12,4},... | collective-permute-start | bytes 3538952 | tf_op jit(solution)/shard_map/ppermute | solution.py:401
  378.2 26.7 %collective-permute-start = (bf16[384,1536]{1,0:T(8,128)(2,1)S(1)}, bf16[384,1536]{1,0:T(8,128)(2,1)S(1)}, u32[]{:S(2)}, u32[]{:S(2)}) collective-permute-start(bf16[384,1536]{1,0:T(8,128)(2,1)S(1)} %get-tuple-element.122.refs_0_), channel_id=1, source_target_pairs={{0,4},{4,0},{1,5},{5,1},{2,6},{6,2},{3,7},{7,3},{8,12},{12,8},{9,1... | collective-permute-start | bytes 3538952 | tf_op jit(solution)/shard_map/ppermute | solution.py:401
  452.1 3.4 collective-permute-start.6
  452.3 25.2 %collective-permute-start.5 = (bf16[384,1536]{1,0:T(8,128)(2,1)}, bf16[384,1536]{1,0:T(8,128)(2,1)}, u32[]{:S(2)}, u32[]{:S(2)}) collective-permute-start(bf16[384,1536]{1,0:T(8,128)(2,1)} %get-tuple-element.131), channel_id=1, source_target_pairs={{0,4},{4,0},{1,5},{5,1},{2,6},{6,2},{3,7},{7,3},{8,12},{12,8},{9,1... | collective-permute-start | bytes 3538952 | tf_op jit(solution)/shard_map/ppermute | solution.py:401
  457.2 28.2 %collective-permute-start.7 = (bf16[384,1536]{1,0:T(8,128)(2,1)S(1)}, bf16[384,1536]{1,0:T(8,128)(2,1)}, u32[]{:S(2)}, u32[]{:S(2)}) collective-permute-start(bf16[384,1536]{1,0:T(8,128)(2,1)S(1)} %add_convert_fusion.6), channel_id=1, source_target_pairs={{0,8},{8,0},{1,9},{9,1},{2,10},{10,2},{3,11},{11,3},{4,12},{12,4},... | collective-permute-start | bytes 3538952 | tf_op jit(solution)/shard_map/ppermute | solution.py:401
  477.5 347.3 %reduce-scatter.3.cloned.1.call-start = ((), (), s32[]{:S(2)}) async-start(), calls=%async_computation.6 | async-start | bytes 5308416 | tf_op jit(solution)/shard_map/reduce_scatter | solution.py:493
  523.1 18.9 %collective-permute-start.10 = (bf16[2,2,4,192,768]{4,3,2,1,0:T(8,128)(2,1)}, bf16[2,2,4,192,768]{4,3,2,1,0:T(8,128)(2,1)}, u32[]{:S(2)}, u32[]{:S(2)}) collective-permute-start(bf16[2,2,4,192,768]{4,3,2,1,0:T(8,128)(2,1)} %get-tuple-element.145), channel_id=1, source_target_pairs={{0,4},{4,0},{1,5},{5,1},{2,6},{6,2},{3,7},{7,3},{8,12},{12,8},{9,1... | collective-permute-start | bytes 14155784 | tf_op jit(solution)/shard_map/ppermute | solution.py:401
  523.1 28.4 %collective-permute-start.9 = (bf16[384,1536]{1,0:T(8,128)(2,1)S(1)}, bf16[384,1536]{1,0:T(8,128)(2,1)S(1)}, u32[]{:S(2)}, u32[]{:S(2)}) collective-permute-start(bf16[384,1536]{1,0:T(8,128)(2,1)S(1)} %copy-done.31), channel_id=1, source_target_pairs={{0,8},{8,0},{1,9},{9,1},{2,10},{10,2},{3,11},{11,3},{4,12},{12,4},... | collective-permute-start | bytes 3538952 | tf_op jit(solution)/shard_map/ppermute | solution.py:401
  541.7 9.8 %collective-permute-start.8 = (bf16[384,1536]{1,0:T(8,128)(2,1)S(1)}, bf16[384,1536]{1,0:T(8,128)(2,1)S(1)}, u32[]{:S(2)}, u32[]{:S(2)}) collective-permute-start(bf16[384,1536]{1,0:T(8,128)(2,1)S(1)} %copy-done.31), channel_id=1, source_target_pairs={{0,4},{4,0},{1,5},{5,1},{2,6},{6,2},{3,7},{7,3},{8,12},{12,8},{9,1... | collective-permute-start | bytes 3538952 | tf_op jit(solution)/shard_map/ppermute | solution.py:401
  555.4 7.6 collective-permute-start.13
  557.6 85.8 %all-to-all-start.1 = ((bf16[8,64,768]{2,1,0:T(8,128)(2,1)}), bf16[8,64,768]{2,1,0:T(8,128)(2,1)S(1)}, u32[]{:S(2)}, u32[]{:S(2)}) async-start(bf16[8,64,768]{2,1,0:T(8,128)(2,1)} %pad_maximum_fusion.1), calls=%async_computation.1 | async-start | bytes 1572864 | tf_op jit(solution)/shard_map/all_to_all | solution.py:435
  561.1 54.3 %collective-permute-start.12 = (bf16[384,1536]{1,0:T(8,128)(2,1)}, bf16[384,1536]{1,0:T(8,128)(2,1)S(1)}, u32[]{:S(2)}, u32[]{:S(2)}) collective-permute-start(bf16[384,1536]{1,0:T(8,128)(2,1)} %get-tuple-element.148), channel_id=1, source_target_pairs={{0,4},{4,0},{1,5},{5,1},{2,6},{6,2},{3,7},{7,3},{8,12},{12,8},{9,1... | collective-permute-start | bytes 3538952 | tf_op jit(solution)/shard_map/ppermute | solution.py:401
  561.6 88.7 %collective-permute-start.15 = (bf16[2,4,192,768]{3,2,1,0:T(8,128)(2,1)}, bf16[2,4,192,768]{3,2,1,0:T(8,128)(2,1)}, u32[]{:S(2)}, u32[]{:S(2)}) collective-permute-start(bf16[2,4,192,768]{3,2,1,0:T(8,128)(2,1)} %get-tuple-element.168), channel_id=1, source_target_pairs={{0,8},{8,0},{1,9},{9,1},{2,10},{10,2},{3,11},{11,3},{4,12},{12,4},... | collective-permute-start | bytes 7077896 | tf_op jit(solution)/shard_map/ppermute | solution.py:401
  565.6 74.8 %collective-permute-start.14 = (bf16[384,1536]{1,0:T(8,128)(2,1)}, bf16[384,1536]{1,0:T(8,128)(2,1)}, u32[]{:S(2)}, u32[]{:S(2)}) collective-permute-start(bf16[384,1536]{1,0:T(8,128)(2,1)} %add_convert_fusion.5), channel_id=1, source_target_pairs={{0,8},{8,0},{1,9},{9,1},{2,10},{10,2},{3,11},{11,3},{4,12},{12,4},... | collective-permute-start | bytes 3538952 | tf_op jit(solution)/shard_map/ppermute | solution.py:401
  644.4 55.5 %all-to-all-start.2 = ((bf16[8,48,1536]{2,1,0:T(8,128)(2,1)}), bf16[8,48,1536]{2,1,0:T(8,128)(2,1)}, u32[]{:S(2)}, u32[]{:S(2)}) async-start(bf16[8,48,1536]{2,1,0:T(8,128)(2,1)} %bitcast.27), calls=%async_computation.2 | async-start | bytes 2359296 | tf_op jit(solution)/shard_map/all_to_all | solution.py:435
  653.4 43.3 %collective-permute-start.16 = (bf16[4,192,768]{2,1,0:T(8,128)(2,1)}, bf16[4,192,768]{2,1,0:T(8,128)(2,1)}, u32[]{:S(2)}, u32[]{:S(2)}) collective-permute-start(bf16[4,192,768]{2,1,0:T(8,128)(2,1)} %fusion.4), channel_id=1, source_target_pairs={{0,16},{16,0},{1,17},{17,1},{2,18},{18,2},{3,19},{19,3},{4,20},{20... | collective-permute-start | bytes 3538952 | tf_op jit(solution)/shard_map/ppermute | solution.py:401
  674.6 18.9 %collective-permute-start.19 = (bf16[2,192,384]{2,1,0:T(8,128)(2,1)S(1)}, bf16[2,192,384]{2,1,0:T(8,128)(2,1)S(1)}, u32[]{:S(2)}, u32[]{:S(2)}) collective-permute-start(bf16[2,192,384]{2,1,0:T(8,128)(2,1)S(1)} %get-tuple-element.202), channel_id=1, source_target_pairs={{0,8},{8,0},{1,9},{9,1},{2,10},{10,2},{3,11},{11,3},{4,12},{12,4},... | collective-permute-start | bytes 884744 | tf_op jit(solution)/shard_map/ppermute | solution.py:401
  695.1 150.1 %collective-permute-start.20 = (bf16[2,192,384]{2,1,0:T(8,128)(2,1)}, bf16[2,192,384]{2,1,0:T(8,128)(2,1)}, u32[]{:S(2)}, u32[]{:S(2)}) collective-permute-start(bf16[2,192,384]{2,1,0:T(8,128)(2,1)} %get-tuple-element.200), channel_id=1, source_target_pairs={{0,4},{4,0},{1,5},{5,1},{2,6},{6,2},{3,7},{7,3},{8,12},{12,8},{9,1... | collective-permute-start | bytes 884744 | tf_op jit(solution)/shard_map/ppermute | solution.py:401
  826.7 8.9 %collective-permute-start.17 = (bf16[2,192,384]{2,1,0:T(8,128)(2,1)}, bf16[2,192,384]{2,1,0:T(8,128)(2,1)}, u32[]{:S(2)}, u32[]{:S(2)}) collective-permute-start(bf16[2,192,384]{2,1,0:T(8,128)(2,1)} %get-tuple-element.206), channel_id=1, source_target_pairs={{0,8},{8,0},{1,9},{9,1},{2,10},{10,2},{3,11},{11,3},{4,12},{12,4},... | collective-permute-start | bytes 884744 | tf_op jit(solution)/shard_map/ppermute | solution.py:401
  837.0 8.2 collective-permute-start.18
  (107 other events, 960.1 us)
Sparse Core Ops, SparseCore 0:
  37.4 238.4 all-gather.1
  477.6 95.3 reduce-scatter.4
  576.6 122.1 reduce-scatter.2
